TPU v7x, 32 devices: a whole 2x2x4 slice. The times are simulated.
32 devices in a mesh: groups: 2 (over y), xz: 4 (over z), gy: 4 (over x, core).
Axes of the slice: x: 2, y: 2, z: 4, core: 2. Of those that a mesh axis runs over, the one named last changes fastest.
Arguments:
- vorticity: float32 [3, 64, 256, 256], P(None, ('groups', 'xz'), 'gy'), parts along dimension 1, may hold values from -6 to 6
- velocity: float32 [3, 64, 256, 256], P(None, ('groups', 'xz'), 'gy'), parts along dimension 1, may hold values from -4 to 4
- sources: bfloat16 [8, 3, 256, 256], P(('groups', 'xz'), None, 'gy'), parts along dimension 0, may hold values from -6 to 6
- incidence: int32 [8, 32, 2], P('groups'), parts along dimension 0, may hold values from 0 to 4
- azimuth: int32 [6], P('groups'), parts along dimension 0, may hold values from 0 to 3
Outputs:
- vorticity_out: float32 [3, 64, 256, 256], P(None, ('groups', 'xz'), 'gy'), parts along dimension 1
There are 2 independent parts, one for each index of `groups`. A program takes and returns all parts, laid end to end along the dimension named above; each array names one. Nothing has to cross between parts.
Inputs may be any that keep to these rules, and one draw needn't show every extreme that they name: `incidence`: an entry below 4 names a source block; 4 marks an empty slot. `azimuth`: which row of incidence each step uses.
All inputs are finite; a program needn't handle non-finite values.
Results may differ from a plain program's by a relative error of at most 0.0003.
Values may be sent and summed in bfloat16 or wider, within the bound.
No kernel may reach another device: no remote copies, remote signals or barrier semaphores. Data moves between devices by JAX's collectives and lax.ppermute only.
A program may use at most 128 MiB of HBM per device.

v0:
```python
import jax
import jax.numpy as jnp
from jax import lax
from jax.sharding import PartitionSpec as P

time_step = 0.2
viscous = 0.1


def with_halo(cells, sides, width):
    for axis, dim in sides:
        count = lax.axis_size(axis)
        ends = count - 1
        head = lax.slice_in_dim(cells, 0, width, axis=dim)
        tail = lax.slice_in_dim(cells, cells.shape[dim] - width, cells.shape[dim], axis=dim)
        cells = jnp.concatenate(
            [
                lax.ppermute(tail, axis, [(i, (i + 1) % count) for i in range(ends)]),
                cells,
                lax.ppermute(head, axis, [((i + 1) % count, i) for i in range(ends)]),
            ],
            axis=dim,
        )
    return cells


def derivatives(padded):
    zpadded = jnp.pad(padded, ((0, 0), (0, 0), (0, 0), (1, 1)))
    center = zpadded[:, 1:-1, 1:-1, 1:-1]
    plus_x = zpadded[:, 2:, 1:-1, 1:-1]
    minus_x = zpadded[:, :-2, 1:-1, 1:-1]
    plus_y = zpadded[:, 1:-1, 2:, 1:-1]
    minus_y = zpadded[:, 1:-1, :-2, 1:-1]
    plus_z = zpadded[:, 1:-1, 1:-1, 2:]
    minus_z = zpadded[:, 1:-1, 1:-1, :-2]
    slopes = ((plus_x - minus_x) * 0.5, (plus_y - minus_y) * 0.5, (plus_z - minus_z) * 0.5)
    laplace = plus_x + minus_x + plus_y + minus_y + plus_z + minus_z - 6.0 * center
    return (center, slopes, laplace)


def advance(padded, velocity, vel_slopes, source):
    center, slopes, laplace = derivatives(padded)
    carried = velocity[0] * slopes[0] + velocity[1] * slopes[1] + velocity[2] * slopes[2]
    stretched = center[0] * vel_slopes[0] + center[1] * vel_slopes[1] + center[2] * vel_slopes[2]
    return center + time_step * (stretched - carried + source) + viscous * laplace


def per_device(vorticity, velocity, sources, incidence, azimuth):
    planes = vorticity.shape[1]
    rows_y = vorticity.shape[2]
    depth = vorticity.shape[3]
    steps = azimuth.shape[0]
    blocks = lax.axis_size("xz") * sources.shape[0]
    start_x = lax.axis_index("xz") * planes
    margin = 0
    extent = planes + 2 * margin
    vel_pad = with_halo(velocity, (("xz", 1), ("gy", 2)), max(margin, 1))
    unused, vel_slopes, unused_lap = derivatives(vel_pad)
    vel_inner = vel_pad[:, 1:-1, 1:-1]
    selector = (
        azimuth[:, None] == jnp.arange(incidence.shape[0], dtype=jnp.int32)[None, :]
    ).astype(jnp.int32)
    chosen = jnp.sum(selector[:, :, None, None] * incidence[None], axis=1)
    local_ids = lax.dynamic_slice_in_dim(chosen, start_x, extent, 1)
    counts = jnp.sum(
        local_ids[:, :, :, None] == jnp.arange(blocks, dtype=jnp.int32)[None, None, None, :], axis=2
    )
    counts = counts.astype(jnp.bfloat16).reshape(steps * extent, blocks)
    gathered = lax.all_gather(sources, "xz", axis=0, tiled=True)
    deposit = jnp.dot(counts, gathered.reshape(blocks, -1), preferred_element_type=jnp.float32)
    deposit = deposit.reshape(steps, extent, 3, rows_y, depth).transpose(0, 2, 1, 3, 4)
    field = vorticity
    for step in range(steps):
        padded = with_halo(field, (("xz", 1), ("gy", 2)), 1)
        field = advance(padded, vel_inner, vel_slopes, deposit[step])
    return field


def solution(mesh):
    in_specs = (
        P(None, ("groups", "xz"), "gy", None),
        P(None, ("groups", "xz"), "gy", None),
        P(("groups", "xz"), None, "gy", None),
        P("groups", None, None),
        P("groups"),
    )
    out_specs = P(None, ("groups", "xz"), "gy", None)
    return jax.shard_map(
        per_device, mesh=mesh, in_specs=in_specs, out_specs=out_specs, check_vma=False
    )
```

profile of v0, /device:TPU:1, one launch (start us, length us, event | category | flops | bytes accessed | tf_op | source)
XLA Modules:
  0.0 132.8 jit_solution(13536344690931140637)
XLA Ops:
  0.0 1.2 fusion.33
  1.2 0.9 copy.54
  2.1 1.3 collective-permute-start.4
  3.3 0.9 copy.56
  4.2 5.3 %collective-permute-start.5 = (f32[3,1,64,256]{3,1,2,0:T(1,128)}, f32[3,1,64,256]{3,1,2,0:T(1,128)}, u32[]{:S(2)}, u32[]{:S(2)}) collective-permute-start(f32[3,1,64,256]{3,1,2,0:T(1,128)} %copy.56), channel_id=1, source_target_pairs={{0,4},{4,8},{8,12},{1,5},{5,9},{9,13},{2,6},{6,10},{10,14},{3,7},{... | collective-permute-start | bytes 589832 | tf_op jit(solution)/shard_map/ppermute | solution.py:18
  9.6 0.9 copy.48
  10.5 2.7 %collective-permute-start.1 = (f32[3,1,64,256]{3,1,2,0:T(1,128)}, f32[3,1,64,256]{3,1,2,0:T(1,128)S(1)}, u32[]{:S(2)}, u32[]{:S(2)}) collective-permute-start(f32[3,1,64,256]{3,1,2,0:T(1,128)} %copy.48), channel_id=1, source_target_pairs={{0,4},{4,8},{8,12},{1,5},{5,9},{9,13},{2,6},{6,10},{10,14},{3,7},{... | collective-permute-start | bytes 589832 | tf_op jit(solution)/shard_map/ppermute | solution.py:18
  13.2 0.9 copy.46
  14.1 1.3 collective-permute-start
  15.4 0.9 copy.47
  16.3 0.5 copy-done.7
  16.8 0.9 copy.63
  18.0 14.4 %all_gather.3 = bf16[4,3,64,256]{3,2,1,0:T(8,128)(2,1)S(1)} all-gather(bf16[1,3,64,256]{3,2,1,0:T(8,128)(2,1)} %param.7), channel_id=1, replica_groups=mesh['groups'=2,'xz'=4,'gy'=4] {'xz'}, dimensions={0}, use_global_device_ids=true | all-gather | bytes 491520 | tf_op jit(solution)/shard_map/all_gather | solution.py:69
  32.3 0.3 copy.67
  32.6 2.8 %convolution_bitcast_fusion = f32[3,3,8,64,256]{4,2,3,1,0:T(8,128)} fusion(bf16[3,64,256,4,1]{2,3,1,0,4:T(4,128)(2,1)S(1)} %bitcast.71, s32[3,8,4]{1,2,0:T(4,128)S(1)} %convert_reduce_fusion), kind=kOutput, calls=%fused_computation.19 | convolution fusion | flops 9437280 | bytes 5112192 | tf_op jit(solution)/shard_map/dot_general | solution.py:70
  35.4 0.2 fusion.23
  35.7 0.7 pad_maximum_fusion.41
  36.4 6.8 %collective-permute-start.3 = (f32[3,10,1,256]{3,1,2,0:T(8,128)S(1)}, f32[3,10,1,256]{3,1,2,0:T(8,128)S(1)}, u32[]{:S(2)}, u32[]{:S(2)}) collective-permute-start(f32[3,10,1,256]{3,1,2,0:T(8,128)S(1)} %get-tuple-element.9), channel_id=1, source_target_pairs={{0,1},{1,2},{2,3},{4,5},{5,6},{6,7},{8,9},{9,10},{10,11},{12,13},{... | collective-permute-start | bytes 92168 | tf_op jit(solution)/shard_map/ppermute | solution.py:18
  43.2 1.9 %collective-permute-start.2 = (f32[3,10,1,256]{3,1,2,0:T(8,128)S(1)}, f32[3,10,1,256]{3,1,2,0:T(8,128)S(1)}, u32[]{:S(2)}, u32[]{:S(2)}) collective-permute-start(f32[3,10,1,256]{3,1,2,0:T(8,128)S(1)} %get-tuple-element.10), channel_id=1, source_target_pairs={{1,0},{2,1},{3,2},{5,4},{6,5},{7,6},{9,8},{10,9},{11,10},{13,12},{... | collective-permute-start | bytes 92168 | tf_op jit(solution)/shard_map/ppermute | solution.py:20
  45.1 0.7 pad_maximum_fusion.38
  45.8 3.6 %collective-permute-start.7 = (f32[3,10,1,256]{3,1,2,0:T(8,128)S(1)}, f32[3,10,1,256]{3,1,2,0:T(8,128)S(1)}, u32[]{:S(2)}, u32[]{:S(2)}) collective-permute-start(f32[3,10,1,256]{3,1,2,0:T(8,128)S(1)} %get-tuple-element.11), channel_id=1, source_target_pairs={{0,1},{1,2},{2,3},{4,5},{5,6},{6,7},{8,9},{9,10},{10,11},{12,13},{... | collective-permute-start | bytes 92168 | tf_op jit(solution)/shard_map/ppermute | solution.py:18
  49.5 1.9 %collective-permute-start.6 = (f32[3,10,1,256]{3,1,2,0:T(8,128)S(1)}, f32[3,10,1,256]{3,1,2,0:T(8,128)S(1)}, u32[]{:S(2)}, u32[]{:S(2)}) collective-permute-start(f32[3,10,1,256]{3,1,2,0:T(8,128)S(1)} %get-tuple-element.12), channel_id=1, source_target_pairs={{1,0},{2,1},{3,2},{5,4},{6,5},{7,6},{9,8},{10,9},{11,10},{13,12},{... | collective-permute-start | bytes 92168 | tf_op jit(solution)/shard_map/ppermute | solution.py:20
  51.4 4.7 %select_maximum_fusion.12 = f32[3,10,66,258]{3,1,2,0:T(8,128)S(1)} fusion(f32[3,10,1,256]{3,1,2,0:T(8,128)S(1)} %collective-permute-done.2, f32[3,10,1,256]{3,1,2,0:T(8,128)S(1)} %collective-permute-done.3, f32[3,1,64,256]{3,1,2,0:T(1,128)} %collective-permute-done, f32[3,8,64,256]{3,1,2,0:T(8,128)S(1)} %copy.47, f32[3,1,64,256]{3,1,2,0:T(1,128)S(1)} %collective-permute-done.1), kind=kLoop, calls=%fused_computation.14 | loop fusion | flops 6130080 | bytes 4070880 | tf_op jit(solution)/shard_map/concatenate | solution.py:16
  56.2 7.0 %select_maximum_fusion.8 = f32[3,10,66,258]{3,1,2,0:T(8,128)} fusion(f32[3,10,1,256]{3,1,2,0:T(8,128)S(1)} %collective-permute-done.6, f32[3,10,1,256]{3,1,2,0:T(8,128)S(1)} %collective-permute-done.7, f32[3,1,64,256]{3,1,2,0:T(1,128)S(1)} %collective-permute-done.4, f32[3,8,64,256]{3,1,2,0:T(8,128)S(1)} %copy.63, f32[3,1,64,256]{3,1,2,0:T(1,128)} %collective-permute-done.5), kind=kLoop, calls=%fused_computation.10 | loop fusion | flops 6130080 | bytes 4070880 | tf_op jit(solution)/shard_map/concatenate | solution.py:16
  63.2 8.0 %fusion.12 = f32[3,8,64,256]{3,1,2,0:T(8,128)S(1)} fusion(f32[3,8,64,256]{3,1,2,0:T(8,128)S(1)} %copy.63, f32[3,3,8,64,256]{4,2,3,1,0:T(8,128)} %convolution_bitcast_fusion, f32[3,10,66,258]{3,1,2,0:T(8,128)} %select_maximum_fusion.8, f32[3,10,1,256]{3,1,2,0:T(8,128)S(1)} %collective-permute-done.6, f32[3,1,64,256]{3,1,2,0:T(1,128)S(1)} %collective-permute-done.4, ...), kind=kLoop, calls=%fused_computation.50 | loop fusion | flops 17694720 | bytes 16637952 | tf_op jit(solution)/shard_map/add | solution.py:45
  71.2 0.2 fusion.31
  71.5 2.5 %collective-permute-start.9 = (f32[3,1,64,256]{3,1,2,0:T(1,128)S(1)}, f32[3,1,64,256]{3,1,2,0:T(1,128)S(1)}, u32[]{:S(2)}, u32[]{:S(2)}) collective-permute-start(f32[3,1,64,256]{3,1,2,0:T(1,128)S(1)} %get-tuple-element.21), channel_id=1, source_target_pairs={{0,4},{4,8},{8,12},{1,5},{5,9},{9,13},{2,6},{6,10},{10,14},{3,7},{... | collective-permute-start | bytes 589832 | tf_op jit(solution)/shard_map/ppermute | solution.py:18
  74.0 1.3 collective-permute-start.8
  75.3 2.0 %collective-permute-done.9 = f32[3,1,64,256]{3,1,2,0:T(1,128)S(1)} collective-permute-done((f32[3,1,64,256]{3,1,2,0:T(1,128)S(1)}, f32[3,1,64,256]{3,1,2,0:T(1,128)S(1)}, u32[]{:S(2)}, u32[]{:S(2)}) %collective-permute-start.9) | collective-permute-done | bytes 196640 | tf_op jit(solution)/shard_map/ppermute | solution.py:18
  77.3 4.1 %collective-permute-done.8 = f32[3,1,64,256]{3,1,2,0:T(1,128)S(1)} collective-permute-done((f32[3,1,64,256]{3,1,2,0:T(1,128)S(1)}, f32[3,1,64,256]{3,1,2,0:T(1,128)S(1)}, u32[]{:S(2)}, u32[]{:S(2)}) %collective-permute-start.8) | collective-permute-done | bytes 196640 | tf_op jit(solution)/shard_map/ppermute | solution.py:20
  81.4 4.1 %collective-permute-start.11 = (f32[3,10,1,256]{3,1,2,0:T(8,128)S(1)}, f32[3,10,1,256]{3,1,2,0:T(8,128)S(1)}, u32[]{:S(2)}, u32[]{:S(2)}) collective-permute-start(f32[3,10,1,256]{3,1,2,0:T(8,128)S(1)} %get-tuple-element.7), channel_id=1, source_target_pairs={{0,1},{1,2},{2,3},{4,5},{5,6},{6,7},{8,9},{9,10},{10,11},{12,13},{... | collective-permute-start | bytes 92168 | tf_op jit(solution)/shard_map/ppermute | solution.py:18
  85.5 2.1 %collective-permute-start.10 = (f32[3,10,1,256]{3,1,2,0:T(8,128)S(1)}, f32[3,10,1,256]{3,1,2,0:T(8,128)S(1)}, u32[]{:S(2)}, u32[]{:S(2)}) collective-permute-start(f32[3,10,1,256]{3,1,2,0:T(8,128)S(1)} %get-tuple-element.8), channel_id=1, source_target_pairs={{1,0},{2,1},{3,2},{5,4},{6,5},{7,6},{9,8},{10,9},{11,10},{13,12},{... | collective-permute-start | bytes 92168 | tf_op jit(solution)/shard_map/ppermute | solution.py:20
  87.6 1.2 fusion.20
  88.9 2.1 %collective-permute-done.10 = f32[3,10,1,256]{3,1,2,0:T(8,128)S(1)} collective-permute-done((f32[3,10,1,256]{3,1,2,0:T(8,128)S(1)}, f32[3,10,1,256]{3,1,2,0:T(8,128)S(1)}, u32[]{:S(2)}, u32[]{:S(2)}) %collective-permute-start.10) | collective-permute-done | bytes 30752 | tf_op jit(solution)/shard_map/ppermute | solution.py:20
  90.9 3.8 %select_maximum_fusion.4 = f32[3,10,66,258]{3,1,2,0:T(8,128)S(1)} fusion(f32[3,10,1,256]{3,1,2,0:T(8,128)S(1)} %collective-permute-done.10, f32[3,10,1,256]{3,1,2,0:T(8,128)S(1)} %collective-permute-done.11, f32[3,1,64,256]{3,1,2,0:T(1,128)S(1)} %collective-permute-done.8, f32[3,8,64,256]{3,1,2,0:T(8,128)S(1)} %fusion.12, ...), kind=kLoop, calls=%fused_computation.6 | loop fusion | flops 6130080 | bytes 4070880 | tf_op jit(solution)/shard_map/concatenate | solution.py:16
  94.8 7.2 %fusion.8 = f32[3,8,64,256]{3,1,2,0:T(8,128)S(1)} fusion(f32[3,8,64,256]{3,1,2,0:T(8,128)S(1)} %fusion.12, f32[3,3,8,64,256]{4,2,3,1,0:T(8,128)} %convolution_bitcast_fusion, f32[3,10,66,258]{3,1,2,0:T(8,128)S(1)} %select_maximum_fusion.4, f32[3,10,1,256]{3,1,2,0:T(8,128)} %copy-done.17, f32[3,1,64,256]{3,1,2,0:T(1,128)} %copy-done.11, ...), kind=kLoop, calls=%fused_computation.37 | loop fusion | flops 17694720 | bytes 16637952 | tf_op jit(solution)/shard_map/add | solution.py:45
  102.0 0.2 fusion.30
  102.3 2.7 %collective-permute-start.13 = (f32[3,1,64,256]{3,1,2,0:T(1,128)S(1)}, f32[3,1,64,256]{3,1,2,0:T(1,128)S(1)}, u32[]{:S(2)}, u32[]{:S(2)}) collective-permute-start(f32[3,1,64,256]{3,1,2,0:T(1,128)S(1)} %get-tuple-element.16), channel_id=1, source_target_pairs={{0,4},{4,8},{8,12},{1,5},{5,9},{9,13},{2,6},{6,10},{10,14},{3,7},{... | collective-permute-start | bytes 589832 | tf_op jit(solution)/shard_map/ppermute | solution.py:18
  105.0 1.3 collective-permute-start.12
  106.3 1.6 %collective-permute-done.13 = f32[3,1,64,256]{3,1,2,0:T(1,128)S(1)} collective-permute-done((f32[3,1,64,256]{3,1,2,0:T(1,128)S(1)}, f32[3,1,64,256]{3,1,2,0:T(1,128)S(1)}, u32[]{:S(2)}, u32[]{:S(2)}) %collective-permute-start.13) | collective-permute-done | bytes 196640 | tf_op jit(solution)/shard_map/ppermute | solution.py:18
  107.9 4.1 %collective-permute-done.12 = f32[3,1,64,256]{3,1,2,0:T(1,128)S(1)} collective-permute-done((f32[3,1,64,256]{3,1,2,0:T(1,128)S(1)}, f32[3,1,64,256]{3,1,2,0:T(1,128)S(1)}, u32[]{:S(2)}, u32[]{:S(2)}) %collective-permute-start.12) | collective-permute-done | bytes 196640 | tf_op jit(solution)/shard_map/ppermute | solution.py:20
  112.0 2.7 %collective-permute-start.15 = (f32[3,10,1,256]{3,1,2,0:T(8,128)S(1)}, f32[3,10,1,256]{3,1,2,0:T(8,128)S(1)}, u32[]{:S(2)}, u32[]{:S(2)}) collective-permute-start(f32[3,10,1,256]{3,1,2,0:T(8,128)S(1)} %get-tuple-element.5), channel_id=1, source_target_pairs={{0,1},{1,2},{2,3},{4,5},{5,6},{6,7},{8,9},{9,10},{10,11},{12,13},{... | collective-permute-start | bytes 92168 | tf_op jit(solution)/shard_map/ppermute | solution.py:18
  114.7 1.9 %collective-permute-start.14 = (f32[3,10,1,256]{3,1,2,0:T(8,128)S(1)}, f32[3,10,1,256]{3,1,2,0:T(8,128)S(1)}, u32[]{:S(2)}, u32[]{:S(2)}) collective-permute-start(f32[3,10,1,256]{3,1,2,0:T(8,128)S(1)} %get-tuple-element.6), channel_id=1, source_target_pairs={{1,0},{2,1},{3,2},{5,4},{6,5},{7,6},{9,8},{10,9},{11,10},{13,12},{... | collective-permute-start | bytes 92168 | tf_op jit(solution)/shard_map/ppermute | solution.py:20
  116.7 1.2 fusion.17
  117.9 2.3 %collective-permute-done.14 = f32[3,10,1,256]{3,1,2,0:T(8,128)S(1)} collective-permute-done((f32[3,10,1,256]{3,1,2,0:T(8,128)S(1)}, f32[3,10,1,256]{3,1,2,0:T(8,128)S(1)}, u32[]{:S(2)}, u32[]{:S(2)}) %collective-permute-start.14) | collective-permute-done | bytes 30752 | tf_op jit(solution)/shard_map/ppermute | solution.py:20
  120.1 3.8 %select_maximum_fusion = f32[3,10,66,258]{3,1,2,0:T(8,128)S(1)} fusion(f32[3,10,1,256]{3,1,2,0:T(8,128)S(1)} %collective-permute-done.14, f32[3,10,1,256]{3,1,2,0:T(8,128)S(1)} %collective-permute-done.15, f32[3,1,64,256]{3,1,2,0:T(1,128)S(1)} %collective-permute-done.12, f32[3,8,64,256]{3,1,2,0:T(8,128)S(1)} %fusion.8, ...), kind=kLoop, calls=%fused_computation.2 | loop fusion | flops 6130080 | bytes 4070880 | tf_op jit(solution)/shard_map/concatenate | solution.py:16
  124.0 7.2 %fusion.4 = f32[3,8,64,256]{3,1,2,0:T(8,128)S(1)} fusion(f32[3,8,64,256]{3,1,2,0:T(8,128)S(1)} %fusion.8, f32[3,3,8,64,256]{4,2,3,1,0:T(8,128)} %convolution_bitcast_fusion, f32[3,10,66,258]{3,1,2,0:T(8,128)S(1)} %select_maximum_fusion, f32[3,10,1,256]{3,1,2,0:T(8,128)} %copy-done.15, f32[3,1,64,256]{3,1,2,0:T(1,128)} %copy-done.9, ...), kind=kLoop, calls=%fused_computation.24 | loop fusion | flops 17694720 | bytes 16637952 | tf_op jit(solution)/shard_map/add | solution.py:45
  131.2 1.6 %copy.65 = f32[3,8,64,256]{3,2,1,0:T(8,128)} copy(f32[3,8,64,256]{3,1,2,0:T(8,128)S(1)} %fusion.4) | data formatting | bytes 3145728 | tf_op jit(solution)/shard_map/add | solution.py:45
  (57 shorter events, 0.4 us)
Async XLA Ops:
  0.0 9.5 %copy-start.6 = (f32[3,8,64,256]{3,2,1,0:T(8,128)S(1)}, f32[3,8,64,256]{3,2,1,0:T(8,128)}, u32[]{:S(2)}) copy-start(f32[3,8,64,256]{3,2,1,0:T(8,128)} %param.6) | copy-start | bytes 4718596
  2.1 43.0 %collective-permute-start.4 = (f32[3,1,64,256]{3,1,2,0:T(1,128)}, f32[3,1,64,256]{3,1,2,0:T(1,128)S(1)}, u32[]{:S(2)}, u32[]{:S(2)}) collective-permute-start(f32[3,1,64,256]{3,1,2,0:T(1,128)} %copy.54), channel_id=1, source_target_pairs={{4,0},{8,4},{12,8},{5,1},{9,5},{13,9},{6,2},{10,6},{14,10},{7,3},{... | collective-permute-start | bytes 589832 | tf_op jit(solution)/shard_map/ppermute | solution.py:20
  4.2 40.9 %collective-permute-start.5 = (f32[3,1,64,256]{3,1,2,0:T(1,128)}, f32[3,1,64,256]{3,1,2,0:T(1,128)}, u32[]{:S(2)}, u32[]{:S(2)}) collective-permute-start(f32[3,1,64,256]{3,1,2,0:T(1,128)} %copy.56), channel_id=1, source_target_pairs={{0,4},{4,8},{8,12},{1,5},{5,9},{9,13},{2,6},{6,10},{10,14},{3,7},{... | collective-permute-start | bytes 589832 | tf_op jit(solution)/shard_map/ppermute | solution.py:18
  10.5 25.2 %collective-permute-start.1 = (f32[3,1,64,256]{3,1,2,0:T(1,128)}, f32[3,1,64,256]{3,1,2,0:T(1,128)S(1)}, u32[]{:S(2)}, u32[]{:S(2)}) collective-permute-start(f32[3,1,64,256]{3,1,2,0:T(1,128)} %copy.48), channel_id=1, source_target_pairs={{0,4},{4,8},{8,12},{1,5},{5,9},{9,13},{2,6},{6,10},{10,14},{3,7},{... | collective-permute-start | bytes 589832 | tf_op jit(solution)/shard_map/ppermute | solution.py:18
  14.1 21.6 %collective-permute-start = (f32[3,1,64,256]{3,1,2,0:T(1,128)}, f32[3,1,64,256]{3,1,2,0:T(1,128)}, u32[]{:S(2)}, u32[]{:S(2)}) collective-permute-start(f32[3,1,64,256]{3,1,2,0:T(1,128)} %copy.46), channel_id=1, source_target_pairs={{4,0},{8,4},{12,8},{5,1},{9,5},{13,9},{6,2},{10,6},{14,10},{7,3},{... | collective-permute-start | bytes 589832 | tf_op jit(solution)/shard_map/ppermute | solution.py:20
  15.3 1.4 %copy-start.7 = (f32[3,8,64,256]{3,2,1,0:T(8,128)S(1)}, f32[3,8,64,256]{3,2,1,0:T(8,128)}, u32[]{:S(2)}) copy-start(f32[3,8,64,256]{3,2,1,0:T(8,128)} %param.5) | copy-start | bytes 4718596
  16.8 0.9 copy-start.19
  16.8 1.0 copy-start.18
  35.6 27.6 %copy-start = (f32[8,64,256]{2,0,1:T(8,128)}, f32[8,64,256]{2,0,1:T(8,128)S(1)}, u32[]{:S(2)}) copy-start(f32[8,64,256]{2,0,1:T(8,128)S(1)} %get-tuple-element.28) | copy-start | bytes 1572868
  35.6 27.6 %copy-start.2 = (f32[8,64,256]{2,0,1:T(8,128)}, f32[8,64,256]{2,0,1:T(8,128)S(1)}, u32[]{:S(2)}) copy-start(f32[8,64,256]{2,0,1:T(8,128)S(1)} %get-tuple-element.29) | copy-start | bytes 1572868
  35.6 27.6 %copy-start.4 = (f32[8,64,256]{2,0,1:T(8,128)}, f32[8,64,256]{2,0,1:T(8,128)S(1)}, u32[]{:S(2)}) copy-start(f32[8,64,256]{2,0,1:T(8,128)S(1)} %get-tuple-element.30) | copy-start | bytes 1572868
  36.4 15.0 %collective-permute-start.3 = (f32[3,10,1,256]{3,1,2,0:T(8,128)S(1)}, f32[3,10,1,256]{3,1,2,0:T(8,128)S(1)}, u32[]{:S(2)}, u32[]{:S(2)}) collective-permute-start(f32[3,10,1,256]{3,1,2,0:T(8,128)S(1)} %get-tuple-element.9), channel_id=1, source_target_pairs={{0,1},{1,2},{2,3},{4,5},{5,6},{6,7},{8,9},{9,10},{10,11},{12,13},{... | collective-permute-start | bytes 92168 | tf_op jit(solution)/shard_map/ppermute | solution.py:18
  43.2 8.3 %collective-permute-start.2 = (f32[3,10,1,256]{3,1,2,0:T(8,128)S(1)}, f32[3,10,1,256]{3,1,2,0:T(8,128)S(1)}, u32[]{:S(2)}, u32[]{:S(2)}) collective-permute-start(f32[3,10,1,256]{3,1,2,0:T(8,128)S(1)} %get-tuple-element.10), channel_id=1, source_target_pairs={{1,0},{2,1},{3,2},{5,4},{6,5},{7,6},{9,8},{10,9},{11,10},{13,12},{... | collective-permute-start | bytes 92168 | tf_op jit(solution)/shard_map/ppermute | solution.py:20
  45.8 10.4 %collective-permute-start.7 = (f32[3,10,1,256]{3,1,2,0:T(8,128)S(1)}, f32[3,10,1,256]{3,1,2,0:T(8,128)S(1)}, u32[]{:S(2)}, u32[]{:S(2)}) collective-permute-start(f32[3,10,1,256]{3,1,2,0:T(8,128)S(1)} %get-tuple-element.11), channel_id=1, source_target_pairs={{0,1},{1,2},{2,3},{4,5},{5,6},{6,7},{8,9},{9,10},{10,11},{12,13},{... | collective-permute-start | bytes 92168 | tf_op jit(solution)/shard_map/ppermute | solution.py:18
  49.5 6.7 %collective-permute-start.6 = (f32[3,10,1,256]{3,1,2,0:T(8,128)S(1)}, f32[3,10,1,256]{3,1,2,0:T(8,128)S(1)}, u32[]{:S(2)}, u32[]{:S(2)}) collective-permute-start(f32[3,10,1,256]{3,1,2,0:T(8,128)S(1)} %get-tuple-element.12), channel_id=1, source_target_pairs={{1,0},{2,1},{3,2},{5,4},{6,5},{7,6},{9,8},{10,9},{11,10},{13,12},{... | collective-permute-start | bytes 92168 | tf_op jit(solution)/shard_map/ppermute | solution.py:20
  51.4 11.8 %copy-start.12 = (f32[3,10,1,256]{3,1,2,0:T(8,128)}, f32[3,10,1,256]{3,1,2,0:T(8,128)S(1)}, u32[]{:S(2)}) copy-start(f32[3,10,1,256]{3,1,2,0:T(8,128)S(1)} %collective-permute-done.3) | copy-start | bytes 92164
  51.4 11.8 %copy-start.13 = (f32[3,10,1,256]{3,1,2,0:T(8,128)}, f32[3,10,1,256]{3,1,2,0:T(8,128)S(1)}, u32[]{:S(2)}) copy-start(f32[3,10,1,256]{3,1,2,0:T(8,128)S(1)} %collective-permute-done.2) | copy-start | bytes 92164
  71.5 5.8 %collective-permute-start.9 = (f32[3,1,64,256]{3,1,2,0:T(1,128)S(1)}, f32[3,1,64,256]{3,1,2,0:T(1,128)S(1)}, u32[]{:S(2)}, u32[]{:S(2)}) collective-permute-start(f32[3,1,64,256]{3,1,2,0:T(1,128)S(1)} %get-tuple-element.21), channel_id=1, source_target_pairs={{0,4},{4,8},{8,12},{1,5},{5,9},{9,13},{2,6},{6,10},{10,14},{3,7},{... | collective-permute-start | bytes 589832 | tf_op jit(solution)/shard_map/ppermute | solution.py:18
  74.0 7.4 %collective-permute-start.8 = (f32[3,1,64,256]{3,1,2,0:T(1,128)S(1)}, f32[3,1,64,256]{3,1,2,0:T(1,128)S(1)}, u32[]{:S(2)}, u32[]{:S(2)}) collective-permute-start(f32[3,1,64,256]{3,1,2,0:T(1,128)S(1)} %get-tuple-element.22), channel_id=1, source_target_pairs={{4,0},{8,4},{12,8},{5,1},{9,5},{13,9},{6,2},{10,6},{14,10},{7,3},{... | collective-permute-start | bytes 589832 | tf_op jit(solution)/shard_map/ppermute | solution.py:20
  77.3 13.6 %copy-start.10 = (f32[3,1,64,256]{3,1,2,0:T(1,128)}, f32[3,1,64,256]{3,1,2,0:T(1,128)S(1)}, u32[]{:S(2)}) copy-start(f32[3,1,64,256]{3,1,2,0:T(1,128)S(1)} %collective-permute-done.9) | copy-start | bytes 589828
  81.4 9.5 %copy-start.11 = (f32[3,1,64,256]{3,1,2,0:T(1,128)}, f32[3,1,64,256]{3,1,2,0:T(1,128)S(1)}, u32[]{:S(2)}) copy-start(f32[3,1,64,256]{3,1,2,0:T(1,128)S(1)} %collective-permute-done.8) | copy-start | bytes 589828
  81.4 7.4 %collective-permute-start.11 = (f32[3,10,1,256]{3,1,2,0:T(8,128)S(1)}, f32[3,10,1,256]{3,1,2,0:T(8,128)S(1)}, u32[]{:S(2)}, u32[]{:S(2)}) collective-permute-start(f32[3,10,1,256]{3,1,2,0:T(8,128)S(1)} %get-tuple-element.7), channel_id=1, source_target_pairs={{0,1},{1,2},{2,3},{4,5},{5,6},{6,7},{8,9},{9,10},{10,11},{12,13},{... | collective-permute-start | bytes 92168 | tf_op jit(solution)/shard_map/ppermute | solution.py:18
  85.5 5.4 %collective-permute-start.10 = (f32[3,10,1,256]{3,1,2,0:T(8,128)S(1)}, f32[3,10,1,256]{3,1,2,0:T(8,128)S(1)}, u32[]{:S(2)}, u32[]{:S(2)}) collective-permute-start(f32[3,10,1,256]{3,1,2,0:T(8,128)S(1)} %get-tuple-element.8), channel_id=1, source_target_pairs={{1,0},{2,1},{3,2},{5,4},{6,5},{7,6},{9,8},{10,9},{11,10},{13,12},{... | collective-permute-start | bytes 92168 | tf_op jit(solution)/shard_map/ppermute | solution.py:20
  88.8 5.9 %copy-start.1 = (f32[8,64,256]{2,0,1:T(8,128)S(1)}, f32[8,64,256]{2,0,1:T(8,128)}, u32[]{:S(2)}) copy-start(f32[8,64,256]{2,0,1:T(8,128)} %copy-done) | copy-start | bytes 1572868
  88.8 5.9 %copy-start.3 = (f32[8,64,256]{2,0,1:T(8,128)S(1)}, f32[8,64,256]{2,0,1:T(8,128)}, u32[]{:S(2)}) copy-start(f32[8,64,256]{2,0,1:T(8,128)} %copy-done.2) | copy-start | bytes 1572868
  88.8 5.9 %copy-start.5 = (f32[8,64,256]{2,0,1:T(8,128)S(1)}, f32[8,64,256]{2,0,1:T(8,128)}, u32[]{:S(2)}) copy-start(f32[8,64,256]{2,0,1:T(8,128)} %copy-done.4) | copy-start | bytes 1572868
  88.9 5.9 %copy-start.16 = (f32[3,10,1,256]{3,1,2,0:T(8,128)}, f32[3,10,1,256]{3,1,2,0:T(8,128)S(1)}, u32[]{:S(2)}) copy-start(f32[3,10,1,256]{3,1,2,0:T(8,128)S(1)} %collective-permute-done.11) | copy-start | bytes 92164
  90.9 3.8 %copy-start.17 = (f32[3,10,1,256]{3,1,2,0:T(8,128)}, f32[3,10,1,256]{3,1,2,0:T(8,128)S(1)}, u32[]{:S(2)}) copy-start(f32[3,10,1,256]{3,1,2,0:T(8,128)S(1)} %collective-permute-done.10) | copy-start | bytes 92164
  102.3 5.6 %collective-permute-start.13 = (f32[3,1,64,256]{3,1,2,0:T(1,128)S(1)}, f32[3,1,64,256]{3,1,2,0:T(1,128)S(1)}, u32[]{:S(2)}, u32[]{:S(2)}) collective-permute-start(f32[3,1,64,256]{3,1,2,0:T(1,128)S(1)} %get-tuple-element.16), channel_id=1, source_target_pairs={{0,4},{4,8},{8,12},{1,5},{5,9},{9,13},{2,6},{6,10},{10,14},{3,7},{... | collective-permute-start | bytes 589832 | tf_op jit(solution)/shard_map/ppermute | solution.py:18
  105.0 7.0 %collective-permute-start.12 = (f32[3,1,64,256]{3,1,2,0:T(1,128)S(1)}, f32[3,1,64,256]{3,1,2,0:T(1,128)S(1)}, u32[]{:S(2)}, u32[]{:S(2)}) collective-permute-start(f32[3,1,64,256]{3,1,2,0:T(1,128)S(1)} %get-tuple-element.17), channel_id=1, source_target_pairs={{4,0},{8,4},{12,8},{5,1},{9,5},{13,9},{6,2},{10,6},{14,10},{7,3},{... | collective-permute-start | bytes 589832 | tf_op jit(solution)/shard_map/ppermute | solution.py:20
  107.8 12.3 %copy-start.8 = (f32[3,1,64,256]{3,1,2,0:T(1,128)}, f32[3,1,64,256]{3,1,2,0:T(1,128)S(1)}, u32[]{:S(2)}) copy-start(f32[3,1,64,256]{3,1,2,0:T(1,128)S(1)} %collective-permute-done.13) | copy-start | bytes 589828
  112.0 8.2 %copy-start.9 = (f32[3,1,64,256]{3,1,2,0:T(1,128)}, f32[3,1,64,256]{3,1,2,0:T(1,128)S(1)}, u32[]{:S(2)}) copy-start(f32[3,1,64,256]{3,1,2,0:T(1,128)S(1)} %collective-permute-done.12) | copy-start | bytes 589828
  112.0 5.9 %collective-permute-start.15 = (f32[3,10,1,256]{3,1,2,0:T(8,128)S(1)}, f32[3,10,1,256]{3,1,2,0:T(8,128)S(1)}, u32[]{:S(2)}, u32[]{:S(2)}) collective-permute-start(f32[3,10,1,256]{3,1,2,0:T(8,128)S(1)} %get-tuple-element.5), channel_id=1, source_target_pairs={{0,1},{1,2},{2,3},{4,5},{5,6},{6,7},{8,9},{9,10},{10,11},{12,13},{... | collective-permute-start | bytes 92168 | tf_op jit(solution)/shard_map/ppermute | solution.py:18
  114.7 5.4 %collective-permute-start.14 = (f32[3,10,1,256]{3,1,2,0:T(8,128)S(1)}, f32[3,10,1,256]{3,1,2,0:T(8,128)S(1)}, u32[]{:S(2)}, u32[]{:S(2)}) collective-permute-start(f32[3,10,1,256]{3,1,2,0:T(8,128)S(1)} %get-tuple-element.6), channel_id=1, source_target_pairs={{1,0},{2,1},{3,2},{5,4},{6,5},{7,6},{9,8},{10,9},{11,10},{13,12},{... | collective-permute-start | bytes 92168 | tf_op jit(solution)/shard_map/ppermute | solution.py:20
  117.9 6.1 %copy-start.14 = (f32[3,10,1,256]{3,1,2,0:T(8,128)}, f32[3,10,1,256]{3,1,2,0:T(8,128)S(1)}, u32[]{:S(2)}) copy-start(f32[3,10,1,256]{3,1,2,0:T(8,128)S(1)} %collective-permute-done.15) | copy-start | bytes 92164
  120.1 3.8 %copy-start.15 = (f32[3,10,1,256]{3,1,2,0:T(8,128)}, f32[3,10,1,256]{3,1,2,0:T(8,128)S(1)}, u32[]{:S(2)}) copy-start(f32[3,10,1,256]{3,1,2,0:T(8,128)S(1)} %collective-permute-done.14) | copy-start | bytes 92164
where the time goes:
time: 134 us; the launch traced here: 133 us
  other arithmetic  46.1 us (34%)
  starting transfers between devices  43.4 us (32%)
  waiting for transfers between devices  16.2 us (12%)
  blocking collectives  14.4 us (11%)
  local copies, waits for them, and re-layouts  9.57 us (7%)
  matrix products  2.76 us (2%)
    ppermute x8, starting transfers between devices, with_halo(): lax.ppermute(tail, axis, [(i, (i + 1) % count) for i in range(ends)])  30.4 us
    add x3, other arithmetic, advance(): center + time_step * (stretched - carried + source) + viscous * laplace  22.5 us
    concatenate x8, other arithmetic, with_halo(): jnp.concatenate([lax.ppermute(tail, axis, [(i, (i + 1) % count) for i in...  20.8 us
    all_gather x1, blocking collectives, per_device(): gathered = lax.all_gather(sources, 'xz', axis=0, tiled=True)  14.4 us
    ppermute x8, starting transfers between devices, with_halo(): lax.ppermute(head, axis, [((i + 1) % count, i) for i in range(ends)])  13 us
    ppermute x8, waiting for transfers between devices, with_halo(): lax.ppermute(head, axis, [((i + 1) % count, i) for i in range(ends)])  12.6 us
    ppermute x8, waiting for transfers between devices, with_halo(): lax.ppermute(tail, axis, [(i, (i + 1) % count) for i in range(ends)])  3.59 us
    slice x5, local copies, waits for them, and re-layouts, with_halo(): lax.slice_in_dim(cells, cells.shape[dim] - width, cells.shape[dim], axis=...  3.39 us
  transfers between devices with their start and end apart: 16, of which 6 were waited for; matrix products, arithmetic and copies ran while one was open for 13% of the time, Pallas kernels for 0%

commit v1 on v0

v1 whole, which is shorter than its diff:
```python
import functools

import jax
import jax.numpy as jnp
from jax import lax
from jax.experimental import pallas as pl
from jax.experimental.pallas import tpu as pltpu
from jax.sharding import PartitionSpec as P

time_step = 0.2
viscous = 0.1
slope = 0.5 * time_step

LANES = 128
ROWS = 8
VMEM = pl.BlockSpec(memory_space=pltpu.VMEM)
SMEM = pl.BlockSpec(memory_space=pltpu.SMEM)
f32 = jnp.float32
f16 = jnp.float16

velocity_scale = 2.0**13
field_scales = (2.0**13, 2.0**10, 2.0**8)


def in_vmem(x):
    return pltpu.with_memory_space_constraint(x, pltpu.VMEM)


def call(kernel, outs, *args, smem=1, aliases=None, cost=None):
    args = args[:smem] + tuple(in_vmem(a) for a in args[smem:])
    multiple = isinstance(outs, list)
    return pl.pallas_call(
        kernel,
        out_shape=[pltpu.VMEM(o.shape, o.dtype) for o in outs] if multiple else pltpu.VMEM(outs.shape, outs.dtype),
        in_specs=[SMEM] * smem + [VMEM] * (len(args) - smem),
        out_specs=[VMEM] * len(outs) if multiple else VMEM,
        input_output_aliases=aliases or {},
        compiler_params=pltpu.CompilerParams(vmem_limit_bytes=16 * 1024 * 1024),
        cost_estimate=pl.CostEstimate(flops=cost, bytes_accessed=cost // 4, transcendentals=0) if cost else None,
    )(*args)


def pack_planes(pos, field, scale, out_refs, first):
    even = pos[0] == 0
    last = field.shape[1] - 1
    toward_first = jnp.where(even, last, 0)
    for out, plane in ((out_refs[0], toward_first), (out_refs[1], last - toward_first)):
        for c in range(3):
            out[first + c] = field[c, plane] * scale


def pack_rows(pos, field, out_refs, first):
    even = pos[1] == 0
    for c in range(3):
        low = field[c, :, 0, :]
        high = field[c, :, field.shape[2] - 1, :]
        out_refs[0][first + c] = jnp.where(even, high, low)
        out_refs[1][first + c] = jnp.where(even, low, high)


def pack_kernel(pos, w, v, x1, x2, y1, y2):
    pack_planes(pos, w, field_scales[0], (x1, x2), 0)
    pack_planes(pos, v, velocity_scale, (x1, x2), 3)
    pack_rows(pos, w, (y1, y2), 0)
    pack_rows(pos, v, (y1, y2), 3)


def gather_kernel(blocks, stages, pos, *refs):
    *parts, table = refs
    z = pos[2]
    toward = 1 - 2 * pos[0]
    per = parts[0].shape[0]

    def put(part, owner):
        for b in range(per):
            table[owner * per + b] = part[b].astype(f32) * time_step

    put(parts[0], z)
    for stage in range(1, stages):
        for part, way in ((parts[2 * stage - 1], toward), (parts[2 * stage], -toward)):
            owner = z + way * stage
            pl.when((owner >= 0) & (owner < stages))(functools.partial(put, part, owner))
    table[blocks] = jnp.zeros(table.shape[1:], f32)


def shifted(parts, lane, up):
    out = []
    for i, part in enumerate(parts):
        other = i + 1 if up else i - 1
        edge = pltpu.roll(parts[other], LANES - 1 if up else 1, 1) if 0 <= other < len(parts) else 0.0
        own = pltpu.roll(part, LANES - 1 if up else 1, 1)
        out.append(jnp.where(lane == (LANES - 1 if up else 0), edge, own))
    return out


def local_kernel(step, slots, ids, w, v, *refs):
    if step:
        table, out = refs
    else:
        (out,) = refs
    planes, rows, depth = w.shape[1:]
    slabs = depth // LANES
    lane = lax.broadcasted_iota(jnp.int32, (ROWS, LANES), 1)
    sub = lax.broadcasted_iota(jnp.int32, (ROWS, LANES), 0)

    def plane_body(x, _):
        before = jnp.maximum(x - 1, 0)
        after = jnp.minimum(x + 1, planes - 1)
        low = jnp.where(x > 0, slope, 0.0)
        high = jnp.where(x < planes - 1, slope, 0.0)

        def piece(ref, first, second, j, s):
            return ref[first, second, j * ROWS : (j + 1) * ROWS, s * LANES : (s + 1) * LANES]

        def around(ref, c, j):
            centre = [piece(ref, c, x, j, s) for s in range(slabs)]
            up_z = shifted(centre, lane, True)
            down_z = shifted(centre, lane, False)
            up_y, down_y = [], []
            for s in range(slabs):
                nxt = piece(ref, c, x, j + 1, s) if (j + 1) * ROWS < rows else 0.0
                prv = piece(ref, c, x, j - 1, s) if j else 0.0
                up_y.append(pltpu.roll(jnp.where(sub == 0, nxt, centre[s]), ROWS - 1, 0))
                down_y.append(pltpu.roll(jnp.where(sub == ROWS - 1, prv, centre[s]), 1, 0))
            up_x = [piece(ref, c, after, j, s) for s in range(slabs)]
            down_x = [piece(ref, c, before, j, s) for s in range(slabs)]
            return centre, up_x, down_x, up_y, down_y, up_z, down_z

        for j in range(rows // ROWS):
            vel = [around(v, c, j) for c in range(3)]
            fld = [around(w, c, j) for c in range(3)]
            for s in range(slabs):
                v0, v1, v2 = (vel[c][0][s] for c in range(3))
                up_x = high - high * v0
                down_x = low + low * v0
                p1, p2 = slope * v1, slope * v2
                up_y, down_y = slope - p1, slope + p1
                up_z, down_z = slope - p2, slope + p2
                w0 = fld[0][0][s]
                w0_up, w0_down = high * w0, low * w0
                w1, w2 = slope * fld[1][0][s], slope * fld[2][0][s]
                for c in range(3):
                    centre, ux, dx, uy, dy, uz, dz = (a[s] for a in fld[c])
                    vc, vux, vdx, vuy, vdy, vuz, vdz = (a[s] for a in vel[c])
                    total = (1.0 - 6.0 * viscous) * centre
                    total += up_x * ux + down_x * dx
                    total += up_y * uy + down_y * dy
                    total += up_z * uz + down_z * dz
                    total += w0_up * vux - w0_down * vdx
                    total += w1 * (vuy - vdy) + w2 * (vuz - vdz)
                    if step:
                        for k in range(slots):
                            block = ids[(step * planes + x) * slots + k]
                            total += piece(table, block, c, j, s)
                    out[c, x, j * ROWS : (j + 1) * ROWS, s * LANES : (s + 1) * LANES] = total
        return 0

    lax.fori_loop(0, planes, plane_body, 0)


def fix_kernel(step, slots, final, *refs):
    if step:
        pos, new, w, v, x1, x2, vx1, vx2, y1, y2, vy1, vy2, out, *sends = refs
        off = 0
    else:
        pos, ids, new, w, v, x1, x2, y1, y2, table, out, *sends = refs
        vx1, vx2, vy1, vy2 = x1, x2, y1, y2
    planes, rows = new.shape[1:3]
    last = planes - 1
    even_x, even_y = pos[0] == 0, pos[1] == 0

    if not step:

        def deposit(x, _):
            for k in range(slots):
                block = ids[x * slots + k]
                for c in range(3):
                    out[c, x] = new[c, x] + table[block, c] if k == 0 else out[c, x] + table[block, c]
            return 0

        lax.fori_loop(0, planes, deposit, 0)
        base = out
    else:
        base = new

    toward_first = jnp.where(even_x, last, 0)
    sign_first = jnp.where(even_x, -slope, slope)
    unscale = 1.0 / field_scales[step]
    v_unscale = 1.0 / velocity_scale
    for halo, v_halo, plane, sign in (
        (x1, vx1, toward_first, sign_first),
        (x2, vx2, last - toward_first, -sign_first),
    ):
        coef = slope + sign * v[0, plane]
        stretch = (-sign * v_unscale) * w[0, plane]
        coef = coef * unscale
        for c in range(3):
            out[c, plane] = base[c, plane] + coef * halo[c] + stretch * v_halo[3 + c]

    for low in (True, False):
        row = 0 if low else rows - 1
        sign = slope if low else -slope
        first = even_y if not low else jnp.logical_not(even_y)
        coef = slope + sign * v[1, :, row, :]
        stretch = -sign * w[1, :, row, :]
        for c in range(3):
            halo = jnp.where(first, y1[c], y2[c])
            v_halo = jnp.where(first, vy1[3 + c], vy2[3 + c])
            out[c, :, row, :] = out[c, :, row, :] + coef * halo + stretch * v_halo

    if not final:
        px1, px2, py1, py2 = sends
        pack_planes(pos, out, field_scales[step + 1], (px1, px2), 0)
        pack_rows(pos, out, (py1, py2), 0)


def swaps(axis):
    count = lax.axis_size(axis)
    pairs = []
    for start in (0, 1):
        both = []
        for i in range(start, count - 1, 2):
            both += [(i, i + 1), (i + 1, i)]
        pairs.append(both)
    return pairs


def per_device(vorticity, velocity, sources, incidence, azimuth):
    planes, rows, depth = vorticity.shape[1:]
    steps = azimuth.shape[0]
    slots = incidence.shape[2]
    count = lax.axis_size("xz")
    blocks = count * sources.shape[0]
    z = lax.axis_index("xz")
    y = lax.axis_index("gy")
    pos = jnp.stack([z % 2, y % 2, z]).astype(jnp.int32)
    chosen = incidence[azimuth]
    ids = lax.dynamic_slice_in_dim(chosen, z * planes, planes, 1).reshape(-1)
    ids = jnp.clip(ids, 0, blocks)
    x_pairs, y_pairs = swaps("xz"), swaps("gy")

    def shape(*dims, dtype=f32):
        return jax.ShapeDtypeStruct(dims, dtype)

    def swap_x(a, which):
        return lax.ppermute(a, "xz", x_pairs[which])

    def swap_planes(pair):
        return [swap_x(a.astype(f16), i).astype(f32) for i, a in enumerate(pair)]

    def swap_rows(pair):
        return [lax.ppermute(a, "gy", y_pairs[i]) for i, a in enumerate(pair)]

    work = 3 * planes * rows * depth * 40
    whole = shape(3, planes, rows, depth)
    sends = call(
        pack_kernel, [shape(6, rows, depth)] * 2 + [shape(6, planes, depth)] * 2, pos, vorticity, velocity
    )
    parts = [sources]
    came = [sources, sources]
    halo = swap_planes(sends[:2])
    side = swap_rows(sends[2:])
    for stage in range(1, count):
        came = [swap_x(came[1], 0), swap_x(came[0], 1)]
        parts += came
    table = call(
        functools.partial(gather_kernel, blocks, count), shape(blocks + 1, 3, rows, depth), pos, *parts
    )
    v_halo, v_side = halo, side
    field = vorticity
    for step in range(steps):
        final = step == steps - 1
        extra = [table] if step else []
        new = call(
            functools.partial(local_kernel, step, slots), whole, ids, field, velocity, *extra, cost=work
        )
        outs = [whole] + ([] if final else [shape(3, rows, depth)] * 2 + [shape(3, planes, depth)] * 2)
        fix = functools.partial(fix_kernel, step, slots, final)
        if step:
            result = call(
                fix, outs, pos, new, field, velocity, *halo, *v_halo, *side, *v_side, aliases={1: 0}, cost=work // 10
            )
        else:
            result = call(
                fix, outs, pos, ids, new, field, velocity, *halo, *side, table, smem=2, aliases={2: 0}, cost=work // 10
            )
        field = result[0]
        if not final:
            halo = swap_planes(result[1:3])
            side = swap_rows(result[3:5])
    return field


def solution(mesh):
    in_specs = (
        P(None, ("groups", "xz"), "gy", None),
        P(None, ("groups", "xz"), "gy", None),
        P(("groups", "xz"), None, "gy", None),
        P("groups", None, None),
        P("groups"),
    )
    out_specs = P(None, ("groups", "xz"), "gy", None)
    return jax.shard_map(
        per_device, mesh=mesh, in_specs=in_specs, out_specs=out_specs, check_vma=False
    )
```

time: 134 us -> 59.6 us (0.44)
  other arithmetic: 46.1 us -> 3.59 us
  waiting for transfers between devices: 16.2 us -> 0.05 us
  Pallas kernels: 0 us -> 14.4 us
  blocking collectives: 14.4 us -> 0 us
  starting transfers between devices: 43.4 us -> 34.7 us
  local copies, waits for them, and re-layouts: 9.57 us -> 6.05 us
  matrix products: 2.76 us -> 0 us
    add x3 -> x0, other arithmetic: 22.5 us -> none  [advance(): center + time_step * (stretched - carried + source) + viscous * laplace]
    concatenate x8 -> x0, other arithmetic: 20.8 us -> none  [with_halo(): jnp.concatenate([lax.ppermute(tail, axis, [(i, (i + 1) % count) for i in...]
    ppermute x16 -> x18, waiting for transfers between devices: 16.2 us -> 0.05 us  [the longest x12 0.03 us: swap_x(): return lax.ppermute(a, 'xz', x_pairs[which])]
    pallas_call x0 -> x8, Pallas kernels: none -> 14.4 us  [call(): pl.pallas_call(kernel, out_shape=[pltpu.VMEM(o.shape, o.dtype) for o in o...]
    all_gather x1 -> x0, blocking collectives: 14.4 us -> none  [per_device(): gathered = lax.all_gather(sources, 'xz', axis=0, tiled=True)]
    ppermute x16 -> x18, starting transfers between devices: 43.4 us -> 34.7 us  [the longest x12 24 us: swap_x(): return lax.ppermute(a, 'xz', x_pairs[which])]
    slice x8 -> x0, local copies, waits for them, and re-layouts: 5.18 us -> none  [the longest x5 3.39 us: with_halo(): lax.slice_in_dim(cells, cells.shape[dim] - width, cells.shape[dim], axis=...]
    convert_element_type x1 -> x12, other arithmetic: 0.07 us -> 3.43 us  [swap_planes(): return [swap_x(a.astype(f16), i).astype(f32) for i, a in enumerate(pair)]]
  transfers between devices with their start and end apart: 16 -> 18, of which waited for: 6 -> 0; matrix products, arithmetic and copies ran while one was open for 13% -> 10% of each run, Pallas kernels for 0% -> 20%
where the time goes in v1:
time: 59.6 us; the launch traced here: 59.1 us
  starting transfers between devices  34.7 us (58%)
  Pallas kernels  14.4 us (24%)
  local copies, waits for them, and re-layouts  6.05 us (10%)
  other arithmetic  3.59 us (6%)
    ppermute x12, starting transfers between devices, swap_x(): return lax.ppermute(a, 'xz', x_pairs[which])  24 us
    pallas_call x8, Pallas kernels, call(): pl.pallas_call(kernel, out_shape=[pltpu.VMEM(o.shape, o.dtype) for o in o...  14.4 us
    ppermute x6, starting transfers between devices, swap_rows(): return [lax.ppermute(a, 'gy', y_pairs[i]) for i, a in enumerate(pair)]  10.6 us
    unnamed x17, local copies, waits for them, and re-layouts  3.99 us
    convert_element_type x12, other arithmetic, swap_planes(): return [swap_x(a.astype(f16), i).astype(f32) for i, a in enumerate(pair)]  3.43 us
    min x2, local copies, waits for them, and re-layouts, per_device(): ids = jnp.clip(ids, 0, blocks)  1.49 us
  transfers between devices with their start and end apart: 18, of which 0 were waited for; matrix products, arithmetic and copies ran while one was open for 10% of the time, Pallas kernels for 20%

profile of v1, /device:TPU:1, one launch (start us, length us, event | category | flops | bytes accessed | tf_op | source)
XLA Modules:
  0.0 59.1 jit_solution(4874667404203843186)
XLA Ops:
  0.0 2.1 %collective-permute-start.4 = (bf16[1,3,64,256]{3,2,1,0:T(8,128)(2,1)}, bf16[1,3,64,256]{3,2,1,0:T(8,128)(2,1)S(1)}, u32[]{:S(2)}, u32[]{:S(2)}) collective-permute-start(bf16[1,3,64,256]{3,2,1,0:T(8,128)(2,1)} %refs_0_.1), channel_id=1, source_target_pairs={{0,4},{4,0},{8,12},{12,8},{1,5},{5,1},{9,13},{13,9},{2,6},{6,2},{1... | collective-permute-start | bytes 294920 | tf_op jit(solution)/shard_map/ppermute | solution.py:246
  2.1 0.7 %collective-permute-start.5 = (bf16[1,3,64,256]{3,2,1,0:T(8,128)(2,1)}, bf16[1,3,64,256]{3,2,1,0:T(8,128)(2,1)S(1)}, u32[]{:S(2)}, u32[]{:S(2)}) collective-permute-start(bf16[1,3,64,256]{3,2,1,0:T(8,128)(2,1)} %refs_0_.1), channel_id=1, source_target_pairs={{4,8},{8,4},{5,9},{9,5},{6,10},{10,6},{7,11},{11,7},{20,24},{24,20... | collective-permute-start | bytes 294920 | tf_op jit(solution)/shard_map/ppermute | solution.py:246
  2.8 0.1 pad_add_fusion.pos.refs_0_
  2.9 1.4 %copy-done.1 = f32[3,8,64,256]{3,2,1,0:T(8,128)S(1)} copy-done((f32[3,8,64,256]{3,2,1,0:T(8,128)S(1)}, f32[3,8,64,256]{3,2,1,0:T(8,128)}, u32[]{:S(2)}) %copy-start.1) | copy-done | bytes 1572888
  4.3 1.4 %copy-done.3 = f32[3,8,64,256]{3,2,1,0:T(8,128)S(1)} copy-done((f32[3,8,64,256]{3,2,1,0:T(8,128)S(1)}, f32[3,8,64,256]{3,2,1,0:T(8,128)}, u32[]{:S(2)}) %copy-start.3) | copy-done | bytes 1572888
  5.7 1.2 %shard_map.56 = (f32[6,64,256]{2,1,0:T(8,128)S(1)}, f32[6,64,256]{2,1,0:T(8,128)S(1)}, f32[6,8,256]{2,1,0:T(8,128)}, f32[6,8,256]{2,1,0:T(8,128)S(1)}) custom-call(s32[3]{0:T(128)S(1)} %pad_add_fusion.pos.refs_0_, f32[3,8,64,256]{3,2,1,0:T(8,128)S(1)} %copy-done.3, f32[3,8,64,256]{3,2,1,0:T(8,128)S(1)} %copy-done.1), custom_call_target="tpu_custom_call" | custom-call | tf_op jit(solution)/shard_map/pallas_call | solution.py:32
  7.0 1.0 %collective-permute-start.2 = (f32[6,8,256]{2,1,0:T(8,128)}, f32[6,8,256]{2,1,0:T(8,128)S(1)}, u32[]{:S(2)}, u32[]{:S(2)}) collective-permute-start(f32[6,8,256]{2,1,0:T(8,128)} %get-tuple-element.21), channel_id=1, source_target_pairs={{0,1},{1,0},{2,3},{3,2},{4,5},{5,4},{6,7},{7,6},{8,9},{9,8},{10,11... | collective-permute-start | bytes 147464 | tf_op jit(solution)/shard_map/ppermute | solution.py:252
  7.9 0.7 %convert_element_type.38 = f16[6,64,256]{2,1,0:T(8,128)(2,1)} convert(f32[6,64,256]{2,1,0:T(8,128)S(1)} %get-tuple-element.20) | non-fusion elementwise | flops 98304 | bytes 589824 | tf_op jit(solution)/shard_map/convert_element_type | solution.py:249
  8.6 1.3 %collective-permute-start.1 = (f16[6,64,256]{2,1,0:T(8,128)(2,1)}, f16[6,64,256]{2,1,0:T(8,128)(2,1)}, u32[]{:S(2)}, u32[]{:S(2)}) collective-permute-start(f16[6,64,256]{2,1,0:T(8,128)(2,1)} %convert_element_type.38), channel_id=1, source_target_pairs={{4,8},{8,4},{5,9},{9,5},{6,10},{10,6},{7,11},{11,7},{20,24},{24,20... | collective-permute-start | bytes 589832 | tf_op jit(solution)/shard_map/ppermute | solution.py:246
  9.9 0.7 %convert_element_type.36 = f16[6,64,256]{2,1,0:T(8,128)(2,1)} convert(f32[6,64,256]{2,1,0:T(8,128)S(1)} %get-tuple-element.19) | non-fusion elementwise | flops 98304 | bytes 589824 | tf_op jit(solution)/shard_map/convert_element_type | solution.py:249
  10.6 4.7 %collective-permute-start = (f16[6,64,256]{2,1,0:T(8,128)(2,1)}, f16[6,64,256]{2,1,0:T(8,128)(2,1)}, u32[]{:S(2)}, u32[]{:S(2)}) collective-permute-start(f16[6,64,256]{2,1,0:T(8,128)(2,1)} %convert_element_type.36), channel_id=1, source_target_pairs={{0,4},{4,0},{8,12},{12,8},{1,5},{5,1},{9,13},{13,9},{2,6},{6,2},{1... | collective-permute-start | bytes 589832 | tf_op jit(solution)/shard_map/ppermute | solution.py:246
  15.4 0.0 collective-permute-done.4.refs_1_
  15.4 0.7 %collective-permute-start.7 = (bf16[1,3,64,256]{3,2,1,0:T(8,128)(2,1)S(1)}, bf16[1,3,64,256]{3,2,1,0:T(8,128)(2,1)S(1)}, u32[]{:S(2)}, u32[]{:S(2)}) collective-permute-start(bf16[1,3,64,256]{3,2,1,0:T(8,128)(2,1)S(1)} %collective-permute-done.4.refs_1_), channel_id=1, source_target_pairs={{4,8},{8,4},{5,9},{9,5},{6,10},{10,6},{7,11},{11,7},{20,24},{24,20... | collective-permute-start | bytes 294920 | tf_op jit(solution)/shard_map/ppermute | solution.py:246
  16.0 0.0 collective-permute-done.5.refs_2_
  16.0 2.8 %collective-permute-start.6 = (bf16[1,3,64,256]{3,2,1,0:T(8,128)(2,1)S(1)}, bf16[1,3,64,256]{3,2,1,0:T(8,128)(2,1)}, u32[]{:S(2)}, u32[]{:S(2)}) collective-permute-start(bf16[1,3,64,256]{3,2,1,0:T(8,128)(2,1)S(1)} %collective-permute-done.5.refs_2_), channel_id=1, source_target_pairs={{0,4},{4,0},{8,12},{12,8},{1,5},{5,1},{9,13},{13,9},{2,6},{6,2},{1... | collective-permute-start | bytes 294920 | tf_op jit(solution)/shard_map/ppermute | solution.py:246
  18.8 0.6 gather_fusion
  19.4 0.0 collective-permute-done.7.refs_4_
  19.4 3.8 %collective-permute-start.3 = (f32[6,8,256]{2,1,0:T(8,128)}, f32[6,8,256]{2,1,0:T(8,128)S(1)}, u32[]{:S(2)}, u32[]{:S(2)}) collective-permute-start(f32[6,8,256]{2,1,0:T(8,128)} %copy-done.6), channel_id=1, source_target_pairs={{1,2},{2,1},{5,6},{6,5},{9,10},{10,9},{13,14},{14,13},{17,18},{18,... | collective-permute-start | bytes 147464 | tf_op jit(solution)/shard_map/ppermute | solution.py:252
  23.3 0.0 collective-permute-done.6.refs_3_
  23.3 4.0 %collective-permute-start.8 = (bf16[1,3,64,256]{3,2,1,0:T(8,128)(2,1)S(1)}, bf16[1,3,64,256]{3,2,1,0:T(8,128)(2,1)}, u32[]{:S(2)}, u32[]{:S(2)}) collective-permute-start(bf16[1,3,64,256]{3,2,1,0:T(8,128)(2,1)S(1)} %collective-permute-done.7.refs_4_), channel_id=1, source_target_pairs={{0,4},{4,0},{8,12},{12,8},{1,5},{5,1},{9,13},{13,9},{2,6},{6,2},{1... | collective-permute-start | bytes 294920 | tf_op jit(solution)/shard_map/ppermute | solution.py:246
  27.3 1.3 %collective-permute-start.9 = (bf16[1,3,64,256]{3,2,1,0:T(8,128)(2,1)}, bf16[1,3,64,256]{3,2,1,0:T(8,128)(2,1)}, u32[]{:S(2)}, u32[]{:S(2)}) collective-permute-start(bf16[1,3,64,256]{3,2,1,0:T(8,128)(2,1)} %collective-permute-done.6.refs_3_), channel_id=1, source_target_pairs={{4,8},{8,4},{5,9},{9,5},{6,10},{10,6},{7,11},{11,7},{20,24},{24,20... | collective-permute-start | bytes 294920 | tf_op jit(solution)/shard_map/ppermute | solution.py:246
  28.6 0.1 dynamic-slice_clamp_fusion
  28.7 0.7 %copy.10 = s32[3,8,2]{2,1,0:T(8,128)} copy(s32[3,8,2]{1,2,0:T(2,128)S(1)} %dynamic-slice_clamp_fusion) | data formatting | bytes 384 | tf_op jit(solution)/shard_map/jit(clip)/min | solution.py:239
  29.4 0.8 %min.12.ids.refs_1_ = s32[48]{0:T(128)S(1)} reshape(s32[3,8,2]{2,1,0:T(8,128)} %copy.10) | data formatting | bytes 384 | tf_op jit(solution)/shard_map/jit(clip)/min | solution.py:239
  30.2 0.0 copy-start.5
  30.2 3.1 %shard_map.55.refs_2_ = f32[3,8,64,256]{3,2,1,0:T(8,128)S(1)} custom-call(s32[48]{0:T(128)S(1)} %min.12.ids.refs_1_, f32[3,8,64,256]{3,2,1,0:T(8,128)S(1)} %copy-done.4, f32[3,8,64,256]{3,2,1,0:T(8,128)S(1)} %copy-done.2), custom_call_target="tpu_custom_call" | custom-call | flops 15728640 | bytes 3932160 | tf_op jit(solution)/shard_map/pallas_call | solution.py:32
  33.3 1.0 %convert_element_type.39.refs_6_.refs_7_ = f32[6,64,256]{2,1,0:T(8,128)S(1)} convert(f16[6,64,256]{2,1,0:T(8,128)(2,1)} %collective-permute-done.1) | non-fusion elementwise | flops 98304 | bytes 589824 | tf_op jit(solution)/shard_map/convert_element_type | solution.py:249
  34.3 1.0 %convert_element_type.37.refs_5_.refs_6_ = f32[6,64,256]{2,1,0:T(8,128)S(1)} convert(f16[6,64,256]{2,1,0:T(8,128)(2,1)} %collective-permute-done) | non-fusion elementwise | flops 98304 | bytes 589824 | tf_op jit(solution)/shard_map/convert_element_type | solution.py:249
  35.2 0.0 collective-permute-done.8.refs_5_
  35.3 1.1 %shard_map.57.refs_9_.refs_0_ = f32[5,3,64,256]{3,2,1,0:T(8,128)S(1)} custom-call(s32[3]{0:T(128)S(1)} %pad_add_fusion.pos.refs_0_, bf16[1,3,64,256]{3,2,1,0:T(8,128)(2,1)S(1)} %copy-done.5, bf16[1,3,64,256]{3,2,1,0:T(8,128)(2,1)S(1)} %collective-permute-done.4.refs_1_, bf16[1,3,64,256]{3,2,1,0:T(8,128)(2,1)S(1)} %collective-permute-done.5.refs_2_, ...), custom_call_target="tpu_custom_call" | custom-call | tf_op jit(solution)/shard_map/pallas_call | solution.py:32
  36.4 0.0 collective-permute-done.3.refs_8_.refs_11_
  36.4 1.1 %shard_map.58 = (f32[3,8,64,256]{3,2,1,0:T(8,128)S(1)}, f32[3,64,256]{2,1,0:T(8,128)S(1)}, f32[3,64,256]{2,1,0:T(8,128)S(1)}, f32[3,8,256]{2,1,0:T(8,128)S(1)}, f32[3,8,256]{2,1,0:T(8,128)S(1)}) custom-call(s32[3]{0:T(128)S(1)} %pad_add_fusion.pos.refs_0_, s32[48]{0:T(128)S(1)} %min.12.ids.refs_1_, ...), custom_call_target="tpu_custom_call", output_to_operand_aliasing={{0}: (2, {})} | custom-call | flops 1572864 | bytes 393216 | tf_op jit(solution)/shard_map/pallas_call | solution.py:32
  37.5 0.7 %collective-permute-start.11 = (f16[3,64,256]{2,1,0:T(8,128)(2,1)S(1)}, f16[3,64,256]{2,1,0:T(8,128)(2,1)S(1)}, u32[]{:S(2)}, u32[]{:S(2)}) collective-permute-start(f16[3,64,256]{2,1,0:T(8,128)(2,1)S(1)} %convert_element_type.42), channel_id=1, source_target_pairs={{4,8},{8,4},{5,9},{9,5},{6,10},{10,6},{7,11},{11,7},{20,24},{24,20... | collective-permute-start | bytes 294920 | tf_op jit(solution)/shard_map/ppermute | solution.py:246
  38.2 3.4 %collective-permute-start.10 = (f16[3,64,256]{2,1,0:T(8,128)(2,1)S(1)}, f16[3,64,256]{2,1,0:T(8,128)(2,1)S(1)}, u32[]{:S(2)}, u32[]{:S(2)}) collective-permute-start(f16[3,64,256]{2,1,0:T(8,128)(2,1)S(1)} %convert_element_type.40), channel_id=1, source_target_pairs={{0,4},{4,0},{8,12},{12,8},{1,5},{5,1},{9,13},{13,9},{2,6},{6,2},{1... | collective-permute-start | bytes 294920 | tf_op jit(solution)/shard_map/ppermute | solution.py:246
  41.7 0.0 collective-permute-start.12
  41.7 2.7 %collective-permute-start.13 = (f32[3,8,256]{2,1,0:T(8,128)S(1)}, f32[3,8,256]{2,1,0:T(8,128)S(1)}, u32[]{:S(2)}, u32[]{:S(2)}) collective-permute-start(f32[3,8,256]{2,1,0:T(8,128)S(1)} %get-tuple-element.27), channel_id=1, source_target_pairs={{1,2},{2,1},{5,6},{6,5},{9,10},{10,9},{13,14},{14,13},{17,18},{18,... | collective-permute-start | bytes 73736 | tf_op jit(solution)/shard_map/ppermute | solution.py:252
  44.4 3.2 %shard_map.59.refs_1_ = f32[3,8,64,256]{3,2,1,0:T(8,128)S(1)} custom-call(s32[48]{0:T(128)S(1)} %min.12.ids.refs_1_, f32[3,8,64,256]{3,2,1,0:T(8,128)S(1)} %get-tuple-element.23.w.refs_2_, f32[3,8,64,256]{3,2,1,0:T(8,128)S(1)} %copy-done.2, f32[5,3,64,256]{3,2,1,0:T(8,128)S(1)} %shard_map.57.refs_9_.refs_0_), custom_call_target="tpu_custom_call" | custom-call | flops 15728640 | bytes 3932160 | tf_op jit(solution)/shard_map/pallas_call | solution.py:32
  47.6 0.0 collective-permute-done.10
  47.7 0.0 collective-permute-done.13.refs_9_
  47.7 0.8 %shard_map.60 = (f32[3,8,64,256]{3,2,1,0:T(8,128)S(1)}, f32[3,64,256]{2,1,0:T(8,128)S(1)}, f32[3,64,256]{2,1,0:T(8,128)S(1)}, f32[3,8,256]{2,1,0:T(8,128)S(1)}, f32[3,8,256]{2,1,0:T(8,128)S(1)}) custom-call(s32[3]{0:T(128)S(1)} %pad_add_fusion.pos.refs_0_, f32[3,8,64,256]{3,2,1,0:T(8,128)S(1)} %shard_map.59.refs_1_, ...), custom_call_target="tpu_custom_call", output_to_operand_aliasing={{0}: (1, {})} | custom-call | flops 1572864 | bytes 393216 | tf_op jit(solution)/shard_map/pallas_call | solution.py:32
  48.5 0.7 %collective-permute-start.15 = (f16[3,64,256]{2,1,0:T(8,128)(2,1)S(1)}, f16[3,64,256]{2,1,0:T(8,128)(2,1)S(1)}, u32[]{:S(2)}, u32[]{:S(2)}) collective-permute-start(f16[3,64,256]{2,1,0:T(8,128)(2,1)S(1)} %convert_element_type.46), channel_id=1, source_target_pairs={{4,8},{8,4},{5,9},{9,5},{6,10},{10,6},{7,11},{11,7},{20,24},{24,20... | collective-permute-start | bytes 294920 | tf_op jit(solution)/shard_map/ppermute | solution.py:246
  49.2 1.7 %collective-permute-start.14 = (f16[3,64,256]{2,1,0:T(8,128)(2,1)S(1)}, f16[3,64,256]{2,1,0:T(8,128)(2,1)S(1)}, u32[]{:S(2)}, u32[]{:S(2)}) collective-permute-start(f16[3,64,256]{2,1,0:T(8,128)(2,1)S(1)} %convert_element_type.44), channel_id=1, source_target_pairs={{0,4},{4,0},{8,12},{12,8},{1,5},{5,1},{9,13},{13,9},{2,6},{6,2},{1... | collective-permute-start | bytes 294920 | tf_op jit(solution)/shard_map/ppermute | solution.py:246
  50.9 3.1 %collective-permute-start.17 = (f32[3,8,256]{2,1,0:T(8,128)S(1)}, f32[3,8,256]{2,1,0:T(8,128)S(1)}, u32[]{:S(2)}, u32[]{:S(2)}) collective-permute-start(f32[3,8,256]{2,1,0:T(8,128)S(1)} %get-tuple-element.32), channel_id=1, source_target_pairs={{1,2},{2,1},{5,6},{6,5},{9,10},{10,9},{13,14},{14,13},{17,18},{18,... | collective-permute-start | bytes 73736 | tf_op jit(solution)/shard_map/ppermute | solution.py:252
  54.0 3.2 %shard_map.61.refs_1_ = f32[3,8,64,256]{3,2,1,0:T(8,128)S(1)} custom-call(s32[48]{0:T(128)S(1)} %min.12.ids.refs_1_, f32[3,8,64,256]{3,2,1,0:T(8,128)S(1)} %get-tuple-element.28.w.refs_2_, f32[3,8,64,256]{3,2,1,0:T(8,128)S(1)} %copy-done.2, f32[5,3,64,256]{3,2,1,0:T(8,128)S(1)} %shard_map.57.refs_9_.refs_0_), custom_call_target="tpu_custom_call" | custom-call | flops 15728640 | bytes 3932160 | tf_op jit(solution)/shard_map/pallas_call | solution.py:32
  57.2 0.0 collective-permute-done.14
  57.2 0.0 collective-permute-done.17.refs_9_
  57.3 0.7 %shard_map.62 = f32[3,8,64,256]{3,2,1,0:T(8,128)S(1)} custom-call(s32[3]{0:T(128)S(1)} %pad_add_fusion.pos.refs_0_, f32[3,8,64,256]{3,2,1,0:T(8,128)S(1)} %shard_map.61.refs_1_, f32[3,8,64,256]{3,2,1,0:T(8,128)S(1)} %get-tuple-element.28.w.refs_2_, f32[3,8,64,256]{3,2,1,0:T(8,128)S(1)} %copy-done.2, ...), custom_call_target="tpu_custom_call", output_to_operand_aliasing={{}: (1, {})} | custom-call | flops 1572864 | bytes 393216 | tf_op jit(solution)/shard_map/pallas_call | solution.py:32
  58.0 1.1 %copy.14 = f32[3,8,64,256]{3,2,1,0:T(8,128)} copy(f32[3,8,64,256]{3,2,1,0:T(8,128)S(1)} %shard_map.62) | data formatting | bytes 3145728
  (32 shorter events, 0.2 us)
Async XLA Ops:
  0.0 18.8 %copy-start = (s32[4,32,2]{1,2,0:T(2,128)S(1)}, s32[4,32,2]{1,2,0:T(2,128)}, u32[]{:S(2)}) copy-start(s32[4,32,2]{1,2,0:T(2,128)} %param.8) | copy-start | bytes 3076
  0.0 15.4 %collective-permute-start.4 = (bf16[1,3,64,256]{3,2,1,0:T(8,128)(2,1)}, bf16[1,3,64,256]{3,2,1,0:T(8,128)(2,1)S(1)}, u32[]{:S(2)}, u32[]{:S(2)}) collective-permute-start(bf16[1,3,64,256]{3,2,1,0:T(8,128)(2,1)} %refs_0_.1), channel_id=1, source_target_pairs={{0,4},{4,0},{8,12},{12,8},{1,5},{5,1},{9,13},{13,9},{2,6},{6,2},{1... | collective-permute-start | bytes 294920 | tf_op jit(solution)/shard_map/ppermute | solution.py:246
  2.1 13.9 %collective-permute-start.5 = (bf16[1,3,64,256]{3,2,1,0:T(8,128)(2,1)}, bf16[1,3,64,256]{3,2,1,0:T(8,128)(2,1)S(1)}, u32[]{:S(2)}, u32[]{:S(2)}) collective-permute-start(bf16[1,3,64,256]{3,2,1,0:T(8,128)(2,1)} %refs_0_.1), channel_id=1, source_target_pairs={{4,8},{8,4},{5,9},{9,5},{6,10},{10,6},{7,11},{11,7},{20,24},{24,20... | collective-permute-start | bytes 294920 | tf_op jit(solution)/shard_map/ppermute | solution.py:246
  2.9 1.4 %copy-start.1 = (f32[3,8,64,256]{3,2,1,0:T(8,128)S(1)}, f32[3,8,64,256]{3,2,1,0:T(8,128)}, u32[]{:S(2)}) copy-start(f32[3,8,64,256]{3,2,1,0:T(8,128)} %refs_3_.5) | copy-start | bytes 4718596
  4.3 1.4 %copy-start.3 = (f32[3,8,64,256]{3,2,1,0:T(8,128)S(1)}, f32[3,8,64,256]{3,2,1,0:T(8,128)}, u32[]{:S(2)}) copy-start(f32[3,8,64,256]{3,2,1,0:T(8,128)} %refs_3_.3) | copy-start | bytes 4718596
  5.7 9.6 %copy-start.7 = (s32[3]{0:T(128)S(1)}, s32[3]{0:T(128)}, u32[]{:S(2)}) copy-start(s32[3]{0:T(128)} %param.9) | copy-start | bytes 40
  5.7 24.5 %copy-start.2 = (f32[3,8,64,256]{3,2,1,0:T(8,128)S(1)}, f32[3,8,64,256]{3,2,1,0:T(8,128)}, u32[]{:S(2)}) copy-start(f32[3,8,64,256]{3,2,1,0:T(8,128)} %refs_3_.5) | copy-start | bytes 4718596
  5.7 24.5 %copy-start.4 = (f32[3,8,64,256]{3,2,1,0:T(8,128)S(1)}, f32[3,8,64,256]{3,2,1,0:T(8,128)}, u32[]{:S(2)}) copy-start(f32[3,8,64,256]{3,2,1,0:T(8,128)} %refs_3_.3) | copy-start | bytes 4718596
  7.0 3.7 %copy-start.6 = (f32[6,8,256]{2,1,0:T(8,128)}, f32[6,8,256]{2,1,0:T(8,128)S(1)}, u32[]{:S(2)}) copy-start(f32[6,8,256]{2,1,0:T(8,128)S(1)} %get-tuple-element.22) | copy-start | bytes 147460
  7.0 29.4 %collective-permute-start.2 = (f32[6,8,256]{2,1,0:T(8,128)}, f32[6,8,256]{2,1,0:T(8,128)S(1)}, u32[]{:S(2)}, u32[]{:S(2)}) collective-permute-start(f32[6,8,256]{2,1,0:T(8,128)} %get-tuple-element.21), channel_id=1, source_target_pairs={{0,1},{1,0},{2,3},{3,2},{4,5},{5,4},{6,7},{7,6},{8,9},{9,8},{10,11... | collective-permute-start | bytes 147464 | tf_op jit(solution)/shard_map/ppermute | solution.py:252
  8.6 18.7 %collective-permute-start.1 = (f16[6,64,256]{2,1,0:T(8,128)(2,1)}, f16[6,64,256]{2,1,0:T(8,128)(2,1)}, u32[]{:S(2)}, u32[]{:S(2)}) collective-permute-start(f16[6,64,256]{2,1,0:T(8,128)(2,1)} %convert_element_type.38), channel_id=1, source_target_pairs={{4,8},{8,4},{5,9},{9,5},{6,10},{10,6},{7,11},{11,7},{20,24},{24,20... | collective-permute-start | bytes 589832 | tf_op jit(solution)/shard_map/ppermute | solution.py:246
  10.6 23.6 %collective-permute-start = (f16[6,64,256]{2,1,0:T(8,128)(2,1)}, f16[6,64,256]{2,1,0:T(8,128)(2,1)}, u32[]{:S(2)}, u32[]{:S(2)}) collective-permute-start(f16[6,64,256]{2,1,0:T(8,128)(2,1)} %convert_element_type.36), channel_id=1, source_target_pairs={{0,4},{4,0},{8,12},{12,8},{1,5},{5,1},{9,13},{13,9},{2,6},{6,2},{1... | collective-permute-start | bytes 589832 | tf_op jit(solution)/shard_map/ppermute | solution.py:246
  15.4 4.0 %collective-permute-start.7 = (bf16[1,3,64,256]{3,2,1,0:T(8,128)(2,1)S(1)}, bf16[1,3,64,256]{3,2,1,0:T(8,128)(2,1)S(1)}, u32[]{:S(2)}, u32[]{:S(2)}) collective-permute-start(bf16[1,3,64,256]{3,2,1,0:T(8,128)(2,1)S(1)} %collective-permute-done.4.refs_1_), channel_id=1, source_target_pairs={{4,8},{8,4},{5,9},{9,5},{6,10},{10,6},{7,11},{11,7},{20,24},{24,20... | collective-permute-start | bytes 294920 | tf_op jit(solution)/shard_map/ppermute | solution.py:246
  16.0 7.2 %collective-permute-start.6 = (bf16[1,3,64,256]{3,2,1,0:T(8,128)(2,1)S(1)}, bf16[1,3,64,256]{3,2,1,0:T(8,128)(2,1)}, u32[]{:S(2)}, u32[]{:S(2)}) collective-permute-start(bf16[1,3,64,256]{3,2,1,0:T(8,128)(2,1)S(1)} %collective-permute-done.5.refs_2_), channel_id=1, source_target_pairs={{0,4},{4,0},{8,12},{12,8},{1,5},{5,1},{9,13},{13,9},{2,6},{6,2},{1... | collective-permute-start | bytes 294920 | tf_op jit(solution)/shard_map/ppermute | solution.py:246
  19.4 17.0 %collective-permute-start.3 = (f32[6,8,256]{2,1,0:T(8,128)}, f32[6,8,256]{2,1,0:T(8,128)S(1)}, u32[]{:S(2)}, u32[]{:S(2)}) collective-permute-start(f32[6,8,256]{2,1,0:T(8,128)} %copy-done.6), channel_id=1, source_target_pairs={{1,2},{2,1},{5,6},{6,5},{9,10},{10,9},{13,14},{14,13},{17,18},{18,... | collective-permute-start | bytes 147464 | tf_op jit(solution)/shard_map/ppermute | solution.py:252
  23.3 12.0 %collective-permute-start.8 = (bf16[1,3,64,256]{3,2,1,0:T(8,128)(2,1)S(1)}, bf16[1,3,64,256]{3,2,1,0:T(8,128)(2,1)}, u32[]{:S(2)}, u32[]{:S(2)}) collective-permute-start(bf16[1,3,64,256]{3,2,1,0:T(8,128)(2,1)S(1)} %collective-permute-done.7.refs_4_), channel_id=1, source_target_pairs={{0,4},{4,0},{8,12},{12,8},{1,5},{5,1},{9,13},{13,9},{2,6},{6,2},{1... | collective-permute-start | bytes 294920 | tf_op jit(solution)/shard_map/ppermute | solution.py:246
  27.3 7.9 %collective-permute-start.9 = (bf16[1,3,64,256]{3,2,1,0:T(8,128)(2,1)}, bf16[1,3,64,256]{3,2,1,0:T(8,128)(2,1)}, u32[]{:S(2)}, u32[]{:S(2)}) collective-permute-start(bf16[1,3,64,256]{3,2,1,0:T(8,128)(2,1)} %collective-permute-done.6.refs_3_), channel_id=1, source_target_pairs={{4,8},{8,4},{5,9},{9,5},{6,10},{10,6},{7,11},{11,7},{20,24},{24,20... | collective-permute-start | bytes 294920 | tf_op jit(solution)/shard_map/ppermute | solution.py:246
  30.2 5.1 %copy-start.5 = (bf16[1,3,64,256]{3,2,1,0:T(8,128)(2,1)S(1)}, bf16[1,3,64,256]{3,2,1,0:T(8,128)(2,1)}, u32[]{:S(2)}) copy-start(bf16[1,3,64,256]{3,2,1,0:T(8,128)(2,1)} %refs_0_.1) | copy-start | bytes 294916
  37.5 10.1 %collective-permute-start.11 = (f16[3,64,256]{2,1,0:T(8,128)(2,1)S(1)}, f16[3,64,256]{2,1,0:T(8,128)(2,1)S(1)}, u32[]{:S(2)}, u32[]{:S(2)}) collective-permute-start(f16[3,64,256]{2,1,0:T(8,128)(2,1)S(1)} %convert_element_type.42), channel_id=1, source_target_pairs={{4,8},{8,4},{5,9},{9,5},{6,10},{10,6},{7,11},{11,7},{20,24},{24,20... | collective-permute-start | bytes 294920 | tf_op jit(solution)/shard_map/ppermute | solution.py:246
  38.2 9.4 %collective-permute-start.10 = (f16[3,64,256]{2,1,0:T(8,128)(2,1)S(1)}, f16[3,64,256]{2,1,0:T(8,128)(2,1)S(1)}, u32[]{:S(2)}, u32[]{:S(2)}) collective-permute-start(f16[3,64,256]{2,1,0:T(8,128)(2,1)S(1)} %convert_element_type.40), channel_id=1, source_target_pairs={{0,4},{4,0},{8,12},{12,8},{1,5},{5,1},{9,13},{13,9},{2,6},{6,2},{1... | collective-permute-start | bytes 294920 | tf_op jit(solution)/shard_map/ppermute | solution.py:246
  41.7 6.0 %collective-permute-start.12 = (f32[3,8,256]{2,1,0:T(8,128)S(1)}, f32[3,8,256]{2,1,0:T(8,128)S(1)}, u32[]{:S(2)}, u32[]{:S(2)}) collective-permute-start(f32[3,8,256]{2,1,0:T(8,128)S(1)} %get-tuple-element.26), channel_id=1, source_target_pairs={{0,1},{1,0},{2,3},{3,2},{4,5},{5,4},{6,7},{7,6},{8,9},{9,8},{10,11... | collective-permute-start | bytes 73736 | tf_op jit(solution)/shard_map/ppermute | solution.py:252
  41.7 6.0 %collective-permute-start.13 = (f32[3,8,256]{2,1,0:T(8,128)S(1)}, f32[3,8,256]{2,1,0:T(8,128)S(1)}, u32[]{:S(2)}, u32[]{:S(2)}) collective-permute-start(f32[3,8,256]{2,1,0:T(8,128)S(1)} %get-tuple-element.27), channel_id=1, source_target_pairs={{1,2},{2,1},{5,6},{6,5},{9,10},{10,9},{13,14},{14,13},{17,18},{18,... | collective-permute-start | bytes 73736 | tf_op jit(solution)/shard_map/ppermute | solution.py:252
  48.5 8.7 %collective-permute-start.15 = (f16[3,64,256]{2,1,0:T(8,128)(2,1)S(1)}, f16[3,64,256]{2,1,0:T(8,128)(2,1)S(1)}, u32[]{:S(2)}, u32[]{:S(2)}) collective-permute-start(f16[3,64,256]{2,1,0:T(8,128)(2,1)S(1)} %convert_element_type.46), channel_id=1, source_target_pairs={{4,8},{8,4},{5,9},{9,5},{6,10},{10,6},{7,11},{11,7},{20,24},{24,20... | collective-permute-start | bytes 294920 | tf_op jit(solution)/shard_map/ppermute | solution.py:246
  49.2 8.0 %collective-permute-start.14 = (f16[3,64,256]{2,1,0:T(8,128)(2,1)S(1)}, f16[3,64,256]{2,1,0:T(8,128)(2,1)S(1)}, u32[]{:S(2)}, u32[]{:S(2)}) collective-permute-start(f16[3,64,256]{2,1,0:T(8,128)(2,1)S(1)} %convert_element_type.44), channel_id=1, source_target_pairs={{0,4},{4,0},{8,12},{12,8},{1,5},{5,1},{9,13},{13,9},{2,6},{6,2},{1... | collective-permute-start | bytes 294920 | tf_op jit(solution)/shard_map/ppermute | solution.py:246
  50.9 6.3 %collective-permute-start.16 = (f32[3,8,256]{2,1,0:T(8,128)S(1)}, f32[3,8,256]{2,1,0:T(8,128)S(1)}, u32[]{:S(2)}, u32[]{:S(2)}) collective-permute-start(f32[3,8,256]{2,1,0:T(8,128)S(1)} %get-tuple-element.31), channel_id=1, source_target_pairs={{0,1},{1,0},{2,3},{3,2},{4,5},{5,4},{6,7},{7,6},{8,9},{9,8},{10,11... | collective-permute-start | bytes 73736 | tf_op jit(solution)/shard_map/ppermute | solution.py:252
  50.9 6.4 %collective-permute-start.17 = (f32[3,8,256]{2,1,0:T(8,128)S(1)}, f32[3,8,256]{2,1,0:T(8,128)S(1)}, u32[]{:S(2)}, u32[]{:S(2)}) collective-permute-start(f32[3,8,256]{2,1,0:T(8,128)S(1)} %get-tuple-element.32), channel_id=1, source_target_pairs={{1,2},{2,1},{5,6},{6,5},{9,10},{10,9},{13,14},{14,13},{17,18},{18,... | collective-permute-start | bytes 73736 | tf_op jit(solution)/shard_map/ppermute | solution.py:252

commit v2 on v0

v2 whole, which is shorter than its diff:
```python
import functools

import jax
import jax.numpy as jnp
from jax import lax
from jax.experimental import pallas as pl
from jax.experimental.pallas import tpu as pltpu
from jax.sharding import PartitionSpec as P

time_step = 0.2
viscous = 0.1
slope = 0.5 * time_step

LANES = 128
ROWS = 8
VMEM = pl.BlockSpec(memory_space=pltpu.VMEM)
SMEM = pl.BlockSpec(memory_space=pltpu.SMEM)
HBM = pl.BlockSpec(memory_space=pl.ANY)
FIXED_HBM = pl.BlockSpec(memory_space=pltpu.HBM)
VMEM_LIMIT = 8 * 1024 * 1024
f32 = jnp.float32
f16 = jnp.float16

velocity_scale = 2.0**13
field_scales = (2.0**13, 2.0**10, 2.0**8)


def in_vmem(x):
    return pltpu.with_memory_space_constraint(x, pltpu.VMEM)


def in_hbm(x):
    return pltpu.with_memory_space_constraint(x, pltpu.HBM)


def call(kernel, outs, *args, smem=1, aliases=None, cost=None, hbm_out=False, scratch=()):
    specs = [SMEM] * smem + [VMEM] * (len(args) - smem)
    args = args[:smem] + tuple(in_vmem(a) for a in args[smem:])
    shapes = [pltpu.VMEM(o.shape, o.dtype) for o in outs]
    out_specs = [VMEM] * len(outs)
    if hbm_out:
        shapes[-1], out_specs[-1] = outs[-1], HBM
    return pl.pallas_call(
        kernel,
        out_shape=shapes,
        in_specs=specs,
        out_specs=out_specs,
        scratch_shapes=scratch,
        input_output_aliases=aliases or {},
        compiler_params=pltpu.CompilerParams(vmem_limit_bytes=VMEM_LIMIT),
        cost_estimate=pl.CostEstimate(flops=cost, bytes_accessed=cost // 4, transcendentals=0) if cost else None,
    )(*args)


def pack_planes(pos, field, out_refs):
    even = pos[0] == 0
    last = field.shape[1] - 1
    toward_first = jnp.where(even, last, 0)
    for out, plane in ((out_refs[0], toward_first), (out_refs[1], last - toward_first)):
        for c in range(3):
            out[c] = field[c, plane]


def pack_rows(pos, field, out_refs, first=0):
    even = pos[1] == 0
    for c in range(3):
        low = field[c, :, 0, :]
        high = field[c, :, field.shape[2] - 1, :]
        out_refs[0][first + c] = jnp.where(even, high, low)
        out_refs[1][first + c] = jnp.where(even, low, high)


def pack_planes_kernel(pos, w, v, x1, x2, sems):
    planes = w.shape[1]
    toward_first = jnp.where(pos[0] == 0, planes - 1, 0)
    copies = []
    for first, field in ((0, w), (3, v)):
        for out, plane in ((x1, toward_first), (x2, planes - 1 - toward_first)):
            one = pltpu.make_async_copy(field.at[:, plane], out.at[pl.ds(first, 3)], sems.at[len(copies)])
            one.start()
            copies.append(one)
    for one in copies:
        one.wait()


def pack_rows_kernel(pos, w, v, y1, y2):
    pack_rows(pos, w, (y1, y2), 0)
    pack_rows(pos, v, (y1, y2), 3)


def gather_kernel(slots, slot, order, pos, azimuth, incidence, field, *refs):
    *parts, table, out, py1, py2 = refs
    per = sum(part.shape[0] for part in parts) // len(order)
    places = [p * per + b for p in order for b in range(per)]
    for part in parts:
        for b in range(part.shape[0]):
            table[places.pop(0)] = part[b].astype(f32) * time_step
    table[table.shape[0] - 1] = jnp.zeros(table.shape[1:], f32)

    def deposit(x, _):
        where = [slot(pos, azimuth, incidence, 0, x, k) for k in range(slots)]
        for c in range(3):
            total = field[c, x]
            for block in where:
                total += table[block, c]
            out[c, x] = total
        return 0

    lax.fori_loop(0, out.shape[1], deposit, 0)
    pack_rows(pos, out, (py1, py2))


def slot_of_table(blocks, per, pos, azimuth, incidence, step, plane, k):
    plane = jnp.clip(pos[2] + plane, 0, incidence.shape[2] - 1)
    block = incidence[azimuth[step], k, plane]
    owner = block // per if per > 1 else block
    slot = (owner ^ pos[3]) * per + block % per if per > 1 else owner ^ pos[3]
    return jnp.where((block >= 0) & (block < blocks), slot, blocks)


def shifted(parts, lane, up):
    out = []
    for i, part in enumerate(parts):
        other = i + 1 if up else i - 1
        edge = pltpu.roll(parts[other], LANES - 1 if up else 1, 1) if 0 <= other < len(parts) else 0.0
        own = pltpu.roll(part, LANES - 1 if up else 1, 1)
        out.append(jnp.where(lane == (LANES - 1 if up else 0), edge, own))
    return out


def local_kernel(step, slots, slot, pos, azimuth, incidence, w, v, *refs):
    if step:
        table, grad, out = refs
    else:
        out, grad = refs
    planes, rows, depth = w.shape[1:]
    slabs = range(depth // LANES)
    chunks = rows // ROWS
    lane = lax.broadcasted_iota(jnp.int32, (ROWS, LANES), 1)
    sub = lax.broadcasted_iota(jnp.int32, (ROWS, LANES), 0)
    comps = range(3)

    def plane_body(x, _):
        before = jnp.maximum(x - 1, 0)
        after = jnp.minimum(x + 1, planes - 1)
        low = jnp.where(x > 0, slope, 0.0)
        high = jnp.where(x < planes - 1, slope, 0.0)
        deposits = [slot(pos, azimuth, incidence, step, x, k) for k in range(slots)] if step else []

        def place(j, s):
            return slice(j * ROWS, (j + 1) * ROWS), slice(s * LANES, (s + 1) * LANES)

        def load(ref, plane, j):
            return [[ref[(c, plane, *place(j, s))] for s in slabs] for c in comps]

        def along_y(prv, cur, nxt):
            up = pltpu.roll(jnp.where(sub == 0, 0.0 if nxt is None else nxt, cur), ROWS - 1, 0)
            down = pltpu.roll(jnp.where(sub == ROWS - 1, 0.0 if prv is None else prv, cur), 1, 0)
            return up, down

        def pick(window, c, s):
            return [None if a is None else a[c][s] for a in window]

        fld = [None, None, load(w, x, 0)]
        vel = [None, None, load(v, x, 0)]
        for j in range(chunks):
            fld = fld[1:] + [load(w, x, j + 1) if j + 1 < chunks else None]
            vel = vel[1:] + [load(v, x, j + 1) if j + 1 < chunks else None]
            up_z = [shifted(fld[1][c], lane, True) for c in comps]
            down_z = [shifted(fld[1][c], lane, False) for c in comps]
            if not step:
                vel_up_z = [shifted(vel[1][c], lane, True) for c in comps]
                vel_down_z = [shifted(vel[1][c], lane, False) for c in comps]
            for s in slabs:
                v0, v1, v2 = (vel[1][c][s] for c in comps)
                x_up = high - high * v0
                x_down = low + low * v0
                p1, p2 = slope * v1, slope * v2
                y_up, y_down = slope - p1, slope + p1
                z_up, z_down = slope - p2, slope + p2
                w0, w1, w2 = (fld[1][c][s] for c in comps)
                for c in comps:
                    here = place(j, s)
                    if step:
                        g0, g1, g2 = (grad[(3 * i + c, x, *here)] for i in range(3))
                    else:
                        g0 = high * v[(c, after, *here)] - low * v[(c, before, *here)]
                        vuy, vdy = along_y(*pick(vel, c, s))
                        g1 = slope * (vuy - vdy)
                        g2 = slope * (vel_up_z[c][s] - vel_down_z[c][s])
                        for i, g in enumerate((g0, g1, g2)):
                            grad[(3 * i + c, x, *here)] = g
                    wuy, wdy = along_y(*pick(fld, c, s))
                    total = (1.0 - 6.0 * viscous) * fld[1][c][s]
                    total += (x_up * w[(c, after, *here)] + x_down * w[(c, before, *here)]) + (y_up * wuy + y_down * wdy)
                    total += (z_up * up_z[c][s] + z_down * down_z[c][s]) + (w0 * g0 + w1 * g1)
                    total += w2 * g2
                    for block in deposits:
                        total += table[(block, c, *here)]
                    out[(c, x, *here)] = total
        return 0

    lax.fori_loop(0, planes, plane_body, 0)


def fix_kernel(step, slots, slot, final, *refs):
    pos, azimuth, incidence, new, *refs = refs
    if step:
        if step == 1:
            table, *refs = refs
        v, x1, x2, y1, y2, out, *sends = refs
    else:
        grad, w, v, x1, x2, y1, y2, out, full, *sends = refs
    planes, rows = new.shape[1:3]
    last = planes - 1

    for low in (True, False):
        row = 0 if low else rows - 1
        there = jnp.where(pos[6 if low else 7] > 0, slope, 0.0)
        sign = there if low else -there
        first = (pos[1] == 0) if not low else (pos[1] != 0)
        coef = there + sign * v[1, :, row, :]
        for c in range(3):
            total = new[c, :, row, :] + coef * jnp.where(first, y1[c], y2[c])
            if not step:
                change = -sign * jnp.where(first, y1[3 + c], y2[3 + c])
                full[3 + c, :, row, :] = grad[3 + c, :, row, :] + change
                total += w[1, :, row, :] * change
            out[c, :, row, :] = total

    if final:
        result, sems = sends
        copies = [
            pltpu.make_async_copy(out.at[c, pl.ds(1, planes - 2)], result.at[c, pl.ds(1, planes - 2)], sems.at[c])
            for c in range(3)
        ]
        for one in copies:
            one.start()

    toward_first = jnp.where(pos[0] == 0, last, 0)
    unscale = 1.0 / field_scales[step]
    for which, halo, plane in ((0, x1, toward_first), (1, x2, last - toward_first)):
        there = jnp.where(pos[4 + which] > 0, slope, 0.0)
        sign = jnp.where(plane > 0, -there, there)
        if step == 1:
            beyond = jnp.where(plane > 0, planes, -1)
            blocks = [slot(pos, azimuth, incidence, 0, beyond, k) for k in range(slots)]
            coef = there + sign * v[0, plane]
        else:
            coef = (there * unscale) + (sign * unscale) * v[0, plane]
        for c in range(3):
            value = halo[c]
            if step == 1:
                value = value * unscale
                for block in blocks:
                    value += table[block, c]
            total = out[c, plane] + coef * value
            if not step:
                change = (-sign / velocity_scale) * halo[3 + c]
                full[c, plane] = grad[c, plane] + change
                total += w[0, plane] * change
            out[c, plane] = total

    if final:
        for i, plane in enumerate((0, last)):
            one = pltpu.make_async_copy(out.at[:, plane], result.at[:, plane], sems.at[3 + i])
            one.start()
            copies.append(one)
        for one in copies:
            one.wait()
    else:
        pack_planes(pos, out, sends[:2])
        if step:
            pack_rows(pos, out, sends[2:])


def swaps(axis, wrap):
    count = lax.axis_size(axis)
    pairs = []
    for start in (0, 1):
        both = []
        for i in range(count):
            other = ((i - start) ^ 1) + start
            if not 0 <= other < count:
                other = count - 1 - i if wrap and start and count % 2 == 0 else i
            both.append((i, other))
        pairs.append(both)
    return pairs


def gather_blocks(sources):
    count = lax.axis_size("xz")
    if count & (count - 1):
        return [lax.all_gather(sources, "xz", axis=0, tiled=True)], list(range(count))
    parts, order, stage = [sources], [0], count // 2
    while stage:
        payload = parts[0] if len(parts) == 1 else jnp.concatenate(parts, axis=0)
        parts.append(lax.ppermute(payload, "xz", [(i, i ^ stage) for i in range(count)]))
        order += [p ^ stage for p in order]
        stage //= 2
    return parts, order


def per_device(vorticity, velocity, sources, incidence, azimuth):
    planes, rows, depth = vorticity.shape[1:]
    steps = azimuth.shape[0]
    slots = incidence.shape[2]
    count, side_count = lax.axis_size("xz"), lax.axis_size("gy")
    per = sources.shape[0]
    blocks = count * per
    z = lax.axis_index("xz")
    y = lax.axis_index("gy")
    low_z, high_z = z > 0, z < count - 1
    pos = jnp.stack(
        [
            z % 2,
            y % 2,
            z * planes,
            0 if count & (count - 1) else z,
            jnp.where(z % 2 == 0, high_z, low_z),
            jnp.where(z % 2 == 0, low_z, high_z),
            y > 0,
            y < side_count - 1,
        ]
    ).astype(jnp.int32)
    incidence = jnp.transpose(incidence, (0, 2, 1))
    x_pairs, y_pairs = swaps("xz", False), swaps("gy", True)
    where = functools.partial(slot_of_table, blocks, per)

    def shape(*dims, dtype=f32):
        return jax.ShapeDtypeStruct(dims, dtype)

    def swap_planes(pair, scale):
        return [lax.ppermute((a * scale).astype(f16), "xz", x_pairs[i]).astype(f32) for i, a in enumerate(pair)]

    def swap_rows(pair):
        return [lax.ppermute(a, "gy", y_pairs[i]) for i, a in enumerate(pair)]

    work = 3 * planes * rows * depth * 40
    whole = shape(3, planes, rows, depth)
    parts, order = gather_blocks(sources)
    planes_out = pl.pallas_call(
        pack_planes_kernel,
        out_shape=[pltpu.VMEM((6, rows, depth), f32)] * 2,
        in_specs=[SMEM, FIXED_HBM, FIXED_HBM],
        out_specs=[VMEM] * 2,
        scratch_shapes=[pltpu.SemaphoreType.DMA((4,))],
        compiler_params=pltpu.CompilerParams(vmem_limit_bytes=VMEM_LIMIT),
    )(pos, in_hbm(vorticity), in_hbm(velocity))
    rows_out = call(pack_rows_kernel, [shape(6, planes, depth)] * 2, pos, vorticity, velocity)
    scale = jnp.array([field_scales[0]] * 3 + [velocity_scale] * 3, f32)[:, None, None]
    halo = swap_planes(planes_out, scale)
    side = swap_rows(rows_out)
    field = vorticity
    small = (pos, azimuth, incidence)
    grads = shape(9, planes, rows, depth)
    for step in range(steps):
        final = step == steps - 1
        local = functools.partial(local_kernel, step, slots, where)
        fix = functools.partial(fix_kernel, step, slots, where, final)
        send_x, send_y = [shape(3, rows, depth)] * 2, [shape(3, planes, depth)] * 2
        if step:
            (new,) = call(local, [whole], *small, field, velocity, table, grad, smem=3, cost=work)
            extra = [table] if step == 1 else []
            result = call(
                fix,
                [whole, whole] if final else [whole] + send_x + send_y,
                *small,
                new,
                *extra,
                velocity,
                *halo,
                *side,
                smem=3,
                aliases={3: 0},
                cost=work // 10,
                hbm_out=final,
                scratch=[pltpu.SemaphoreType.DMA((5,))] if final else (),
            )
            if final:
                return result[1]
            field = result[0]
            halo = swap_planes(result[1:3], field_scales[step + 1])
            side = swap_rows(result[3:5])
        else:
            new, grad = call(local, [whole, grads], *small, field, velocity, smem=3, cost=work)
            args = (new, grad, field, velocity, *halo, *side)
            new, grad, *ready = call(
                fix, [whole, grads] + send_x, *small, *args, smem=3, aliases={3: 0, 4: 1}, cost=work // 10
            )
            halo = swap_planes(ready, field_scales[1])
            table, field, *ready = call(
                functools.partial(gather_kernel, slots, where, order),
                [shape(blocks + 1, 3, rows, depth), whole] + send_y,
                *small,
                new,
                *parts,
                smem=3,
                aliases={3: 1},
                cost=work // 10,
            )
            side = swap_rows(ready)


def solution(mesh):
    in_specs = (
        P(None, ("groups", "xz"), "gy", None),
        P(None, ("groups", "xz"), "gy", None),
        P(("groups", "xz"), None, "gy", None),
        P("groups", None, None),
        P("groups"),
    )
    out_specs = P(None, ("groups", "xz"), "gy", None)
    return jax.shard_map(
        per_device, mesh=mesh, in_specs=in_specs, out_specs=out_specs, check_vma=False
    )
```

time: 134 us -> 36.2 us (0.27)
  other arithmetic: 46.1 us -> 0.29 us
  starting transfers between devices: 43.4 us -> 17.5 us
  Pallas kernels: 0 us -> 15 us
  blocking collectives: 14.4 us -> 0 us
  waiting for transfers between devices: 16.2 us -> 2.37 us
  local copies, waits for them, and re-layouts: 9.57 us -> 0.11 us
  matrix products: 2.76 us -> 0 us
    ppermute x16 -> x14, starting transfers between devices: 43.4 us -> 17.5 us  [the longest x6 7.37 us: swap_planes(): lax.ppermute((a * scale).astype(f16), 'xz', x_pairs[i]).astype(f32)]
    add x3 -> x0, other arithmetic: 22.5 us -> none  [advance(): center + time_step * (stretched - carried + source) + viscous * laplace]
    concatenate x8 -> x1, other arithmetic: 20.8 us -> 0.02 us  [gather_blocks(): payload = parts[0] if len(parts) == 1 else jnp.concatenate(parts, axis=0)]
    pallas_call x0 -> x9, Pallas kernels: none -> 15 us  [the longest x8 12.9 us: call(): pl.pallas_call(kernel, out_shape=shapes, in_specs=specs, out_specs=out_sp...]
    all_gather x1 -> x0, blocking collectives: 14.4 us -> none  [per_device(): gathered = lax.all_gather(sources, 'xz', axis=0, tiled=True)]
    ppermute x16 -> x14, waiting for transfers between devices: 16.2 us -> 2.37 us  [the longest x2 1.83 us: gather_blocks(): lax.ppermute(payload, 'xz', [(i, i ^ stage) for i in range(count)])]
    slice x8 -> x0, local copies, waits for them, and re-layouts: 5.18 us -> none  [the longest x5 3.39 us: with_halo(): lax.slice_in_dim(cells, cells.shape[dim] - width, cells.shape[dim], axis=...]
    dot_general x1 -> x0, matrix products: 2.76 us -> none  [per_device(): jnp.dot(counts, gathered.reshape(blocks, -1), preferred_element_type=jnp....]
  transfers between devices with their start and end apart: 16 -> 14, of which waited for: 6 -> 2; matrix products, arithmetic and copies ran while one was open for 13% -> 1% of each run, Pallas kernels for 0% -> 29%
where the time goes in v2:
time: 36.2 us; the launch traced here: 35.6 us
  starting transfers between devices  17.5 us (48%)
  Pallas kernels  15 us (41%)
  waiting for transfers between devices  2.37 us (7%)
    pallas_call x8, Pallas kernels, call(): pl.pallas_call(kernel, out_shape=shapes, in_specs=specs, out_specs=out_sp...  12.9 us
    ppermute x6, starting transfers between devices, swap_planes(): lax.ppermute((a * scale).astype(f16), 'xz', x_pairs[i]).astype(f32)  7.37 us
    ppermute x6, starting transfers between devices, swap_rows(): return [lax.ppermute(a, 'gy', y_pairs[i]) for i, a in enumerate(pair)]  5.92 us
    ppermute x2, starting transfers between devices, gather_blocks(): lax.ppermute(payload, 'xz', [(i, i ^ stage) for i in range(count)])  4.23 us
    pallas_call x1, Pallas kernels, per_device(): pl.pallas_call(pack_planes_kernel, out_shape=[pltpu.VMEM((6, rows, depth)...  2.08 us
    ppermute x2, waiting for transfers between devices, gather_blocks(): lax.ppermute(payload, 'xz', [(i, i ^ stage) for i in range(count)])  1.83 us
  transfers between devices with their start and end apart: 14, of which 2 were waited for; matrix products, arithmetic and copies ran while one was open for 1% of the time, Pallas kernels for 29%

profile of v2, /device:TPU:1, one launch (start us, length us, event | category | flops | bytes accessed | tf_op | source)
XLA Modules:
  0.0 35.6 jit_solution(10100184174882164514)
XLA Ops:
  0.0 0.1 stack.51.pos.refs_0_
  0.1 0.0 copy-start.2
  0.1 0.0 copy-start
  0.1 0.0 copy-start.1
  0.1 2.1 %shard_map.65 = (f32[6,64,256]{2,1,0:T(8,128)S(1)}, f32[6,64,256]{2,1,0:T(8,128)S(1)}) custom-call(s32[8]{0:T(128)S(1)} %stack.51.pos.refs_0_, f32[3,8,64,256]{3,2,1,0:T(8,128)} %refs_5_.2, f32[3,8,64,256]{3,2,1,0:T(8,128)} %refs_4_.1), custom_call_target="tpu_custom_call" | custom-call | tf_op jit(solution)/shard_map/pallas_call | solution.py:342
  2.2 2.2 %collective-permute-start = (f16[6,64,256]{2,1,0:T(8,128)(2,1)S(1)}, f16[6,64,256]{2,1,0:T(8,128)(2,1)S(1)}, u32[]{:S(2)}, u32[]{:S(2)}) collective-permute-start(f16[6,64,256]{2,1,0:T(8,128)(2,1)S(1)} %multiply_convert_fusion.1), channel_id=1, source_target_pairs={{0,4},{4,0},{8,12},{12,8},{1,5},{5,1},{9,13},{13,9},{2,6},{6,2},{1... | collective-permute-start | bytes 589832 | tf_op jit(solution)/shard_map/ppermute | solution.py:334
  4.4 0.0 copy-done.2
  4.4 2.3 %collective-permute-start.4 = (bf16[1,3,64,256]{3,2,1,0:T(8,128)(2,1)S(1)}, bf16[1,3,64,256]{3,2,1,0:T(8,128)(2,1)S(1)}, u32[]{:S(2)}, u32[]{:S(2)}) collective-permute-start(bf16[1,3,64,256]{3,2,1,0:T(8,128)(2,1)S(1)} %copy-done.2), channel_id=1, source_target_pairs={{0,8},{4,12},{8,0},{12,4},{1,9},{5,13},{9,1},{13,5},{2,10},{6,14},... | collective-permute-start | bytes 294920 | tf_op jit(solution)/shard_map/ppermute | solution.py:298
  6.8 0.0 copy-start.3
  6.8 0.0 copy-start.4
  6.8 0.7 %collective-permute-start.1 = (f16[6,64,256]{2,1,0:T(8,128)(2,1)S(1)}, f16[6,64,256]{2,1,0:T(8,128)(2,1)S(1)}, u32[]{:S(2)}, u32[]{:S(2)}) collective-permute-start(f16[6,64,256]{2,1,0:T(8,128)(2,1)S(1)} %multiply_convert_fusion), channel_id=1, source_target_pairs={{0,0},{4,8},{8,4},{12,12},{1,1},{5,9},{9,5},{13,13},{2,2},{6,10},{... | collective-permute-start | bytes 589832 | tf_op jit(solution)/shard_map/ppermute | solution.py:334
  7.5 0.0 copy-done
  7.5 0.0 copy-done.1
  7.5 0.6 %shard_map.66 = (f32[6,8,256]{2,1,0:T(8,128)S(1)}, f32[6,8,256]{2,1,0:T(8,128)S(1)}) custom-call(s32[8]{0:T(128)S(1)} %stack.51.pos.refs_0_, f32[3,8,64,256]{3,2,1,0:T(8,128)S(1)} %copy-done.1, f32[3,8,64,256]{3,2,1,0:T(8,128)S(1)} %copy-done), custom_call_target="tpu_custom_call" | custom-call | tf_op jit(solution)/shard_map/pallas_call | solution.py:43
  8.1 1.3 %collective-permute-start.2 = (f32[6,8,256]{2,1,0:T(8,128)S(1)}, f32[6,8,256]{2,1,0:T(8,128)S(1)}, u32[]{:S(2)}, u32[]{:S(2)}) collective-permute-start(f32[6,8,256]{2,1,0:T(8,128)S(1)} %get-tuple-element.29), channel_id=1, source_target_pairs={{0,1},{1,0},{2,3},{3,2},{4,5},{5,4},{6,7},{7,6},{8,9},{9,8},{10,11... | collective-permute-start | bytes 147464 | tf_op jit(solution)/shard_map/ppermute | solution.py:337
  9.4 1.2 %collective-permute-start.3 = (f32[6,8,256]{2,1,0:T(8,128)S(1)}, f32[6,8,256]{2,1,0:T(8,128)S(1)}, u32[]{:S(2)}, u32[]{:S(2)}) collective-permute-start(f32[6,8,256]{2,1,0:T(8,128)S(1)} %get-tuple-element.30), channel_id=1, source_target_pairs={{0,3},{1,2},{2,1},{3,0},{4,7},{5,6},{6,5},{7,4},{8,11},{9,10},{10,... | collective-permute-start | bytes 147464 | tf_op jit(solution)/shard_map/ppermute | solution.py:337
  10.6 0.0 copy-done.3
  10.6 0.0 copy-done.4
  10.6 2.9 %shard_map.64 = (f32[3,8,64,256]{3,2,1,0:T(8,128)S(1)}, f32[9,8,64,256]{3,2,1,0:T(8,128)S(1)}) custom-call(s32[8]{0:T(128)S(1)} %stack.51.pos.refs_0_, s32[3]{0:T(128)S(1)} %copy-done.4, s32[4,2,32]{2,1,0:T(2,128)S(1)} %bitcast.9, f32[3,8,64,256]{3,2,1,0:T(8,128)S(1)} %copy-done.1, f32[3,8,64,256]{3,2,1,0:T(8,128)S(1)} %copy-done), custom_call_target="tpu_custom_call" | custom-call | flops 15728640 | bytes 3932160 | tf_op jit(solution)/shard_map/pallas_call | solution.py:43
  13.5 0.0 collective-permute-done.4.refs_1_
  13.6 1.9 %collective-permute-start.5 = (bf16[2,3,64,256]{3,2,1,0:T(8,128)(2,1)S(1)}, bf16[2,3,64,256]{3,2,1,0:T(8,128)(2,1)S(1)}, u32[]{:S(2)}, u32[]{:S(2)}) collective-permute-start(bf16[2,3,64,256]{3,2,1,0:T(8,128)(2,1)S(1)} %pad_maximum_fusion), channel_id=1, source_target_pairs={{0,4},{4,0},{8,12},{12,8},{1,5},{5,1},{9,13},{13,9},{2,6},{6,2},{1... | collective-permute-start | bytes 589832 | tf_op jit(solution)/shard_map/ppermute | solution.py:298
  15.5 0.0 collective-permute-done
  15.5 0.0 collective-permute-done.1
  15.6 0.0 collective-permute-done.2.refs_9_
  15.6 0.0 collective-permute-done.3.refs_10_
  15.6 0.9 %shard_map.67 = (f32[3,8,64,256]{3,2,1,0:T(8,128)S(1)}, f32[9,8,64,256]{3,2,1,0:T(8,128)S(1)}, f32[3,64,256]{2,1,0:T(8,128)S(1)}, f32[3,64,256]{2,1,0:T(8,128)S(1)}) custom-call(s32[8]{0:T(128)S(1)} %stack.51.pos.refs_0_, s32[3]{0:T(128)S(1)} %copy-done.4, s32[4,2,32]{2,1,0:T(2,128)S(1)} %bitcast.10, ...), custom_call_target="tpu_custom_call", output_to_operand_aliasing={{0}: (3, {}), {1}: (4, {})} | custom-call | flops 1572864 | bytes 393216 | tf_op jit(solution)/shard_map/pallas_call | solution.py:43
  16.5 1.3 %collective-permute-start.6 = (f16[3,64,256]{2,1,0:T(8,128)(2,1)S(1)}, f16[3,64,256]{2,1,0:T(8,128)(2,1)S(1)}, u32[]{:S(2)}, u32[]{:S(2)}) collective-permute-start(f16[3,64,256]{2,1,0:T(8,128)(2,1)S(1)} %multiply_convert_fusion.5), channel_id=1, source_target_pairs={{0,4},{4,0},{8,12},{12,8},{1,5},{5,1},{9,13},{13,9},{2,6},{6,2},{1... | collective-permute-start | bytes 294920 | tf_op jit(solution)/shard_map/ppermute | solution.py:334
  17.9 0.7 %collective-permute-start.7 = (f16[3,64,256]{2,1,0:T(8,128)(2,1)S(1)}, f16[3,64,256]{2,1,0:T(8,128)(2,1)S(1)}, u32[]{:S(2)}, u32[]{:S(2)}) collective-permute-start(f16[3,64,256]{2,1,0:T(8,128)(2,1)S(1)} %multiply_convert_fusion.4), channel_id=1, source_target_pairs={{0,0},{4,8},{8,4},{12,12},{1,1},{5,9},{9,5},{13,13},{2,2},{6,10},{... | collective-permute-start | bytes 294920 | tf_op jit(solution)/shard_map/ppermute | solution.py:334
  18.6 1.8 %collective-permute-done.5.refs_2_ = bf16[2,3,64,256]{3,2,1,0:T(8,128)(2,1)S(1)} collective-permute-done((bf16[2,3,64,256]{3,2,1,0:T(8,128)(2,1)S(1)}, bf16[2,3,64,256]{3,2,1,0:T(8,128)(2,1)S(1)}, u32[]{:S(2)}, u32[]{:S(2)}) %collective-permute-start.5) | collective-permute-done | bytes 196640 | tf_op jit(solution)/shard_map/ppermute | solution.py:298
  20.4 1.1 %shard_map.68 = (f32[5,3,64,256]{3,2,1,0:T(8,128)S(1)}, f32[3,8,64,256]{3,2,1,0:T(8,128)S(1)}, f32[3,8,256]{2,1,0:T(8,128)S(1)}, f32[3,8,256]{2,1,0:T(8,128)S(1)}) custom-call(s32[8]{0:T(128)S(1)} %stack.51.pos.refs_0_, s32[3]{0:T(128)S(1)} %copy-done.4, s32[4,2,32]{2,1,0:T(2,128)S(1)} %bitcast.11, ...), custom_call_target="tpu_custom_call", output_to_operand_aliasing={{1}: (3, {})} | custom-call | flops 1572864 | bytes 393216 | tf_op jit(solution)/shard_map/pallas_call | solution.py:43
  21.5 1.6 %collective-permute-start.8 = (f32[3,8,256]{2,1,0:T(8,128)S(1)}, f32[3,8,256]{2,1,0:T(8,128)S(1)}, u32[]{:S(2)}, u32[]{:S(2)}) collective-permute-start(f32[3,8,256]{2,1,0:T(8,128)S(1)} %get-tuple-element.37), channel_id=1, source_target_pairs={{0,1},{1,0},{2,3},{3,2},{4,5},{5,4},{6,7},{7,6},{8,9},{9,8},{10,11... | collective-permute-start | bytes 73736 | tf_op jit(solution)/shard_map/ppermute | solution.py:337
  23.1 0.3 collective-permute-start.9
  23.4 0.0 collective-permute-done.6
  23.4 0.0 collective-permute-done.7
  23.4 2.4 %shard_map.69.refs_3_ = f32[3,8,64,256]{3,2,1,0:T(8,128)S(1)} custom-call(s32[8]{0:T(128)S(1)} %stack.51.pos.refs_0_, s32[3]{0:T(128)S(1)} %copy-done.4, s32[4,2,32]{2,1,0:T(2,128)S(1)} %bitcast.12, f32[3,8,64,256]{3,2,1,0:T(8,128)S(1)} %get-tuple-element.32.w, f32[3,8,64,256]{3,2,1,0:T(8,128)S(1)} %copy-done, ...), custom_call_target="tpu_custom_call" | custom-call | flops 15728640 | bytes 3932160 | tf_op jit(solution)/shard_map/pallas_call | solution.py:43
  25.8 0.0 collective-permute-done.8.refs_8_
  25.8 0.5 %collective-permute-done.9.refs_9_ = f32[3,8,256]{2,1,0:T(8,128)S(1)} collective-permute-done((f32[3,8,256]{2,1,0:T(8,128)S(1)}, f32[3,8,256]{2,1,0:T(8,128)S(1)}, u32[]{:S(2)}, u32[]{:S(2)}) %collective-permute-start.9) | collective-permute-done | bytes 24608 | tf_op jit(solution)/shard_map/ppermute | solution.py:337
  26.3 0.8 %shard_map.70 = (f32[3,8,64,256]{3,2,1,0:T(8,128)S(1)}, f32[3,64,256]{2,1,0:T(8,128)S(1)}, f32[3,64,256]{2,1,0:T(8,128)S(1)}, f32[3,8,256]{2,1,0:T(8,128)S(1)}, f32[3,8,256]{2,1,0:T(8,128)S(1)}) custom-call(s32[8]{0:T(128)S(1)} %stack.51.pos.refs_0_, s32[3]{0:T(128)S(1)} %copy-done.4, s32[4,2,32]{2,1,0:T(2,128)S(1)} %bitcast.13, ...), custom_call_target="tpu_custom_call", output_to_operand_aliasing={{0}: (3, {})} | custom-call | flops 1572864 | bytes 393216 | tf_op jit(solution)/shard_map/pallas_call | solution.py:43
  27.2 1.8 %collective-permute-start.10 = (f16[3,64,256]{2,1,0:T(8,128)(2,1)S(1)}, f16[3,64,256]{2,1,0:T(8,128)(2,1)S(1)}, u32[]{:S(2)}, u32[]{:S(2)}) collective-permute-start(f16[3,64,256]{2,1,0:T(8,128)(2,1)S(1)} %multiply_convert_fusion.3), channel_id=1, source_target_pairs={{0,4},{4,0},{8,12},{12,8},{1,5},{5,1},{9,13},{13,9},{2,6},{6,2},{1... | collective-permute-start | bytes 294920 | tf_op jit(solution)/shard_map/ppermute | solution.py:334
  29.1 0.7 %collective-permute-start.11 = (f16[3,64,256]{2,1,0:T(8,128)(2,1)S(1)}, f16[3,64,256]{2,1,0:T(8,128)(2,1)S(1)}, u32[]{:S(2)}, u32[]{:S(2)}) collective-permute-start(f16[3,64,256]{2,1,0:T(8,128)(2,1)S(1)} %multiply_convert_fusion.2), channel_id=1, source_target_pairs={{0,0},{4,8},{8,4},{12,12},{1,1},{5,9},{9,5},{13,13},{2,2},{6,10},{... | collective-permute-start | bytes 294920 | tf_op jit(solution)/shard_map/ppermute | solution.py:334
  29.7 0.4 %collective-permute-start.12 = (f32[3,8,256]{2,1,0:T(8,128)S(1)}, f32[3,8,256]{2,1,0:T(8,128)S(1)}, u32[]{:S(2)}, u32[]{:S(2)}) collective-permute-start(f32[3,8,256]{2,1,0:T(8,128)S(1)} %get-tuple-element.42), channel_id=1, source_target_pairs={{0,1},{1,0},{2,3},{3,2},{4,5},{5,4},{6,7},{7,6},{8,9},{9,8},{10,11... | collective-permute-start | bytes 73736 | tf_op jit(solution)/shard_map/ppermute | solution.py:337
  30.1 1.1 %collective-permute-start.13 = (f32[3,8,256]{2,1,0:T(8,128)S(1)}, f32[3,8,256]{2,1,0:T(8,128)S(1)}, u32[]{:S(2)}, u32[]{:S(2)}) collective-permute-start(f32[3,8,256]{2,1,0:T(8,128)S(1)} %get-tuple-element.43), channel_id=1, source_target_pairs={{0,3},{1,2},{2,1},{3,0},{4,7},{5,6},{6,5},{7,4},{8,11},{9,10},{10,... | collective-permute-start | bytes 73736 | tf_op jit(solution)/shard_map/ppermute | solution.py:337
  31.3 2.4 %shard_map.71.refs_3_ = f32[3,8,64,256]{3,2,1,0:T(8,128)S(1)} custom-call(s32[8]{0:T(128)S(1)} %stack.51.pos.refs_0_, s32[3]{0:T(128)S(1)} %copy-done.4, s32[4,2,32]{2,1,0:T(2,128)S(1)} %bitcast.14, f32[3,8,64,256]{3,2,1,0:T(8,128)S(1)} %get-tuple-element.39.w, f32[3,8,64,256]{3,2,1,0:T(8,128)S(1)} %copy-done, ...), custom_call_target="tpu_custom_call" | custom-call | flops 15728640 | bytes 3932160 | tf_op jit(solution)/shard_map/pallas_call | solution.py:43
  33.6 0.0 collective-permute-done.10
  33.7 0.0 collective-permute-done.11
  33.7 0.0 collective-permute-done.12.refs_7_
  33.7 0.0 collective-permute-done.13.refs_8_
  33.7 1.9 %shard_map.72 = (f32[3,8,64,256]{3,2,1,0:T(8,128)S(1)}, f32[3,8,64,256]{3,2,1,0:T(8,128)}) custom-call(s32[8]{0:T(128)S(1)} %stack.51.pos.refs_0_, s32[3]{0:T(128)S(1)} %copy-done.4, s32[4,2,32]{2,1,0:T(2,128)S(1)} %bitcast.15, f32[3,8,64,256]{3,2,1,0:T(8,128)S(1)} %shard_map.71.refs_3_, ...), custom_call_target="tpu_custom_call", output_to_operand_aliasing={{0}: (3, {})} | custom-call | flops 1572864 | bytes 393216 | tf_op jit(solution)/shard_map/pallas_call | solution.py:43
  (13 shorter events, 0.3 us)
Async XLA Ops:
  0.1 4.3 %copy-start.2 = (bf16[1,3,64,256]{3,2,1,0:T(8,128)(2,1)S(1)}, bf16[1,3,64,256]{3,2,1,0:T(8,128)(2,1)}, u32[]{:S(2)}) copy-start(bf16[1,3,64,256]{3,2,1,0:T(8,128)(2,1)} %refs_0_.1) | copy-start | bytes 294916
  0.1 7.4 %copy-start = (f32[3,8,64,256]{3,2,1,0:T(8,128)S(1)}, f32[3,8,64,256]{3,2,1,0:T(8,128)}, u32[]{:S(2)}) copy-start(f32[3,8,64,256]{3,2,1,0:T(8,128)} %refs_4_.1) | copy-start | bytes 4718596
  0.1 7.4 %copy-start.1 = (f32[3,8,64,256]{3,2,1,0:T(8,128)S(1)}, f32[3,8,64,256]{3,2,1,0:T(8,128)}, u32[]{:S(2)}) copy-start(f32[3,8,64,256]{3,2,1,0:T(8,128)} %refs_5_.2) | copy-start | bytes 4718596
  2.2 13.3 %collective-permute-start = (f16[6,64,256]{2,1,0:T(8,128)(2,1)S(1)}, f16[6,64,256]{2,1,0:T(8,128)(2,1)S(1)}, u32[]{:S(2)}, u32[]{:S(2)}) collective-permute-start(f16[6,64,256]{2,1,0:T(8,128)(2,1)S(1)} %multiply_convert_fusion.1), channel_id=1, source_target_pairs={{0,4},{4,0},{8,12},{12,8},{1,5},{5,1},{9,13},{13,9},{2,6},{6,2},{1... | collective-permute-start | bytes 589832 | tf_op jit(solution)/shard_map/ppermute | solution.py:334
  4.4 9.1 %collective-permute-start.4 = (bf16[1,3,64,256]{3,2,1,0:T(8,128)(2,1)S(1)}, bf16[1,3,64,256]{3,2,1,0:T(8,128)(2,1)S(1)}, u32[]{:S(2)}, u32[]{:S(2)}) collective-permute-start(bf16[1,3,64,256]{3,2,1,0:T(8,128)(2,1)S(1)} %copy-done.2), channel_id=1, source_target_pairs={{0,8},{4,12},{8,0},{12,4},{1,9},{5,13},{9,1},{13,5},{2,10},{6,14},... | collective-permute-start | bytes 294920 | tf_op jit(solution)/shard_map/ppermute | solution.py:298
  6.8 3.8 %copy-start.3 = (s32[4,32,2]{1,2,0:T(2,128)S(1)}, s32[4,32,2]{1,2,0:T(2,128)}, u32[]{:S(2)}) copy-start(s32[4,32,2]{1,2,0:T(2,128)} %param.9) | copy-start | bytes 3076
  6.8 3.8 %copy-start.4 = (s32[3]{0:T(128)S(1)}, s32[3]{0:T(128)}, u32[]{:S(2)}) copy-start(s32[3]{0:T(128)} %refs_1_.5) | copy-start | bytes 40
  6.8 8.7 %collective-permute-start.1 = (f16[6,64,256]{2,1,0:T(8,128)(2,1)S(1)}, f16[6,64,256]{2,1,0:T(8,128)(2,1)S(1)}, u32[]{:S(2)}, u32[]{:S(2)}) collective-permute-start(f16[6,64,256]{2,1,0:T(8,128)(2,1)S(1)} %multiply_convert_fusion), channel_id=1, source_target_pairs={{0,0},{4,8},{8,4},{12,12},{1,1},{5,9},{9,5},{13,13},{2,2},{6,10},{... | collective-permute-start | bytes 589832 | tf_op jit(solution)/shard_map/ppermute | solution.py:334
  8.1 7.5 %collective-permute-start.2 = (f32[6,8,256]{2,1,0:T(8,128)S(1)}, f32[6,8,256]{2,1,0:T(8,128)S(1)}, u32[]{:S(2)}, u32[]{:S(2)}) collective-permute-start(f32[6,8,256]{2,1,0:T(8,128)S(1)} %get-tuple-element.29), channel_id=1, source_target_pairs={{0,1},{1,0},{2,3},{3,2},{4,5},{5,4},{6,7},{7,6},{8,9},{9,8},{10,11... | collective-permute-start | bytes 147464 | tf_op jit(solution)/shard_map/ppermute | solution.py:337
  9.4 6.2 %collective-permute-start.3 = (f32[6,8,256]{2,1,0:T(8,128)S(1)}, f32[6,8,256]{2,1,0:T(8,128)S(1)}, u32[]{:S(2)}, u32[]{:S(2)}) collective-permute-start(f32[6,8,256]{2,1,0:T(8,128)S(1)} %get-tuple-element.30), channel_id=1, source_target_pairs={{0,3},{1,2},{2,1},{3,0},{4,7},{5,6},{6,5},{7,4},{8,11},{9,10},{10,... | collective-permute-start | bytes 147464 | tf_op jit(solution)/shard_map/ppermute | solution.py:337
  13.6 6.8 %collective-permute-start.5 = (bf16[2,3,64,256]{3,2,1,0:T(8,128)(2,1)S(1)}, bf16[2,3,64,256]{3,2,1,0:T(8,128)(2,1)S(1)}, u32[]{:S(2)}, u32[]{:S(2)}) collective-permute-start(bf16[2,3,64,256]{3,2,1,0:T(8,128)(2,1)S(1)} %pad_maximum_fusion), channel_id=1, source_target_pairs={{0,4},{4,0},{8,12},{12,8},{1,5},{5,1},{9,13},{13,9},{2,6},{6,2},{1... | collective-permute-start | bytes 589832 | tf_op jit(solution)/shard_map/ppermute | solution.py:298
  16.5 6.8 %collective-permute-start.6 = (f16[3,64,256]{2,1,0:T(8,128)(2,1)S(1)}, f16[3,64,256]{2,1,0:T(8,128)(2,1)S(1)}, u32[]{:S(2)}, u32[]{:S(2)}) collective-permute-start(f16[3,64,256]{2,1,0:T(8,128)(2,1)S(1)} %multiply_convert_fusion.5), channel_id=1, source_target_pairs={{0,4},{4,0},{8,12},{12,8},{1,5},{5,1},{9,13},{13,9},{2,6},{6,2},{1... | collective-permute-start | bytes 294920 | tf_op jit(solution)/shard_map/ppermute | solution.py:334
  17.9 5.5 %collective-permute-start.7 = (f16[3,64,256]{2,1,0:T(8,128)(2,1)S(1)}, f16[3,64,256]{2,1,0:T(8,128)(2,1)S(1)}, u32[]{:S(2)}, u32[]{:S(2)}) collective-permute-start(f16[3,64,256]{2,1,0:T(8,128)(2,1)S(1)} %multiply_convert_fusion.4), channel_id=1, source_target_pairs={{0,0},{4,8},{8,4},{12,12},{1,1},{5,9},{9,5},{13,13},{2,2},{6,10},{... | collective-permute-start | bytes 294920 | tf_op jit(solution)/shard_map/ppermute | solution.py:334
  21.5 4.3 %collective-permute-start.8 = (f32[3,8,256]{2,1,0:T(8,128)S(1)}, f32[3,8,256]{2,1,0:T(8,128)S(1)}, u32[]{:S(2)}, u32[]{:S(2)}) collective-permute-start(f32[3,8,256]{2,1,0:T(8,128)S(1)} %get-tuple-element.37), channel_id=1, source_target_pairs={{0,1},{1,0},{2,3},{3,2},{4,5},{5,4},{6,7},{7,6},{8,9},{9,8},{10,11... | collective-permute-start | bytes 73736 | tf_op jit(solution)/shard_map/ppermute | solution.py:337
  23.1 3.3 %collective-permute-start.9 = (f32[3,8,256]{2,1,0:T(8,128)S(1)}, f32[3,8,256]{2,1,0:T(8,128)S(1)}, u32[]{:S(2)}, u32[]{:S(2)}) collective-permute-start(f32[3,8,256]{2,1,0:T(8,128)S(1)} %get-tuple-element.38), channel_id=1, source_target_pairs={{0,3},{1,2},{2,1},{3,0},{4,7},{5,6},{6,5},{7,4},{8,11},{9,10},{10,... | collective-permute-start | bytes 73736 | tf_op jit(solution)/shard_map/ppermute | solution.py:337
  27.2 6.5 %collective-permute-start.10 = (f16[3,64,256]{2,1,0:T(8,128)(2,1)S(1)}, f16[3,64,256]{2,1,0:T(8,128)(2,1)S(1)}, u32[]{:S(2)}, u32[]{:S(2)}) collective-permute-start(f16[3,64,256]{2,1,0:T(8,128)(2,1)S(1)} %multiply_convert_fusion.3), channel_id=1, source_target_pairs={{0,4},{4,0},{8,12},{12,8},{1,5},{5,1},{9,13},{13,9},{2,6},{6,2},{1... | collective-permute-start | bytes 294920 | tf_op jit(solution)/shard_map/ppermute | solution.py:334
  29.1 4.6 %collective-permute-start.11 = (f16[3,64,256]{2,1,0:T(8,128)(2,1)S(1)}, f16[3,64,256]{2,1,0:T(8,128)(2,1)S(1)}, u32[]{:S(2)}, u32[]{:S(2)}) collective-permute-start(f16[3,64,256]{2,1,0:T(8,128)(2,1)S(1)} %multiply_convert_fusion.2), channel_id=1, source_target_pairs={{0,0},{4,8},{8,4},{12,12},{1,1},{5,9},{9,5},{13,13},{2,2},{6,10},{... | collective-permute-start | bytes 294920 | tf_op jit(solution)/shard_map/ppermute | solution.py:334
  29.7 4.0 %collective-permute-start.12 = (f32[3,8,256]{2,1,0:T(8,128)S(1)}, f32[3,8,256]{2,1,0:T(8,128)S(1)}, u32[]{:S(2)}, u32[]{:S(2)}) collective-permute-start(f32[3,8,256]{2,1,0:T(8,128)S(1)} %get-tuple-element.42), channel_id=1, source_target_pairs={{0,1},{1,0},{2,3},{3,2},{4,5},{5,4},{6,7},{7,6},{8,9},{9,8},{10,11... | collective-permute-start | bytes 73736 | tf_op jit(solution)/shard_map/ppermute | solution.py:337
  30.1 3.6 %collective-permute-start.13 = (f32[3,8,256]{2,1,0:T(8,128)S(1)}, f32[3,8,256]{2,1,0:T(8,128)S(1)}, u32[]{:S(2)}, u32[]{:S(2)}) collective-permute-start(f32[3,8,256]{2,1,0:T(8,128)S(1)} %get-tuple-element.43), channel_id=1, source_target_pairs={{0,3},{1,2},{2,1},{3,0},{4,7},{5,6},{6,5},{7,4},{8,11},{9,10},{10,... | collective-permute-start | bytes 73736 | tf_op jit(solution)/shard_map/ppermute | solution.py:337

commit v3 on v2

--- a/solution.py
+++ b/solution.py
@@ -188,11 +188,13 @@
                         vuy, vdy = along_y(*pick(vel, c, s))
                         g1 = slope * (vuy - vdy)
                         g2 = slope * (vel_up_z[c][s] - vel_down_z[c][s])
-                        for i, g in enumerate((g0, g1, g2)):
+                        terms = [g0, g1, g2]
+                        terms[c] += 1.0 - 6.0 * viscous
+                        g0, g1, g2 = terms
+                        for i, g in enumerate(terms):
                             grad[(3 * i + c, x, *here)] = g
                     wuy, wdy = along_y(*pick(fld, c, s))
-                    total = (1.0 - 6.0 * viscous) * fld[1][c][s]
-                    total += (x_up * w[(c, after, *here)] + x_down * w[(c, before, *here)]) + (y_up * wuy + y_down * wdy)
+                    total = (x_up * w[(c, after, *here)] + x_down * w[(c, before, *here)]) + (y_up * wuy + y_down * wdy)
                     total += (z_up * up_z[c][s] + z_down * down_z[c][s]) + (w0 * g0 + w1 * g1)
                     total += w2 * g2
                     for block in deposits:
@@ -213,6 +215,18 @@
         grad, w, v, x1, x2, y1, y2, out, full, *sends = refs
     planes, rows = new.shape[1:3]
     last = planes - 1
+    inner = pl.ds(1, planes - 2)
+    copies = []
+
+    def write(source, target):
+        copies.append(pltpu.make_async_copy(source, target, sems.at[len(copies)]))
+        copies[-1].start()
+
+    if final:
+        result, sems = sends
+        middle = pl.ds(ROWS, rows - 2 * ROWS)
+        for c in range(3):
+            write(out.at[c, inner, middle], result.at[c, inner, middle])
 
     for low in (True, False):
         row = 0 if low else rows - 1
@@ -229,13 +243,9 @@
             out[c, :, row, :] = total
 
     if final:
-        result, sems = sends
-        copies = [
-            pltpu.make_async_copy(out.at[c, pl.ds(1, planes - 2)], result.at[c, pl.ds(1, planes - 2)], sems.at[c])
-            for c in range(3)
-        ]
-        for one in copies:
-            one.start()
+        for c in range(3):
+            for tile in (0, rows - ROWS):
+                write(out.at[c, inner, pl.ds(tile, ROWS)], result.at[c, inner, pl.ds(tile, ROWS)])
 
     toward_first = jnp.where(pos[0] == 0, last, 0)
     unscale = 1.0 / field_scales[step]
@@ -262,10 +272,8 @@
             out[c, plane] = total
 
     if final:
-        for i, plane in enumerate((0, last)):
-            one = pltpu.make_async_copy(out.at[:, plane], result.at[:, plane], sems.at[3 + i])
-            one.start()
-            copies.append(one)
+        for plane in (0, last):
+            write(out.at[:, plane], result.at[:, plane])
         for one in copies:
             one.wait()
     else:
@@ -331,7 +339,8 @@
         return jax.ShapeDtypeStruct(dims, dtype)
 
     def swap_planes(pair, scale):
-        return [lax.ppermute((a * scale).astype(f16), "xz", x_pairs[i]).astype(f32) for i, a in enumerate(pair)]
+        second, first = [lax.ppermute((pair[i] * scale).astype(f16), "xz", x_pairs[i]) for i in (1, 0)]
+        return first, second
 
     def swap_rows(pair):
         return [lax.ppermute(a, "gy", y_pairs[i]) for i, a in enumerate(pair)]
@@ -347,6 +356,7 @@
         scratch_shapes=[pltpu.SemaphoreType.DMA((4,))],
         compiler_params=pltpu.CompilerParams(vmem_limit_bytes=VMEM_LIMIT),
     )(pos, in_hbm(vorticity), in_hbm(velocity))
+    vorticity, velocity, planes_out = lax.optimization_barrier((vorticity, velocity, planes_out))
     rows_out = call(pack_rows_kernel, [shape(6, planes, depth)] * 2, pos, vorticity, velocity)
     scale = jnp.array([field_scales[0]] * 3 + [velocity_scale] * 3, f32)[:, None, None]
     halo = swap_planes(planes_out, scale)
@@ -361,6 +371,11 @@
         send_x, send_y = [shape(3, rows, depth)] * 2, [shape(3, planes, depth)] * 2
         if step:
             (new,) = call(local, [whole], *small, field, velocity, table, grad, smem=3, cost=work)
+            if step == 1:
+                one, *side = lax.optimization_barrier((jnp.ones((1, 1, depth), f32), *side))
+                halo = [a.astype(f32) * one for a in halo]
+            else:
+                halo = [a.astype(f32) for a in halo]
             extra = [table] if step == 1 else []
             result = call(
                 fix,
@@ -375,7 +390,7 @@
                 aliases={3: 0},
                 cost=work // 10,
                 hbm_out=final,
-                scratch=[pltpu.SemaphoreType.DMA((5,))] if final else (),
+                scratch=[pltpu.SemaphoreType.DMA((11,))] if final else (),
             )
             if final:
                 return result[1]
@@ -383,8 +398,9 @@
             halo = swap_planes(result[1:3], field_scales[step + 1])
             side = swap_rows(result[3:5])
         else:
-            new, grad = call(local, [whole, grads], *small, field, velocity, smem=3, cost=work)
-            args = (new, grad, field, velocity, *halo, *side)
+            gate, parts[1] = lax.optimization_barrier((pos, parts[1]))
+            new, grad = call(local, [whole, grads], gate, azimuth, incidence, field, velocity, smem=3, cost=work)
+            args = (new, grad, field, velocity, *[a.astype(f32) for a in halo], *side)
             new, grad, *ready = call(
                 fix, [whole, grads] + send_x, *small, *args, smem=3, aliases={3: 0, 4: 1}, cost=work // 10
             )

time: 36.2 us -> 34.8 us (0.961)
  waiting for transfers between devices: 2.37 us -> 0.17 us
  starting transfers between devices: 17.5 us -> 18.6 us
    ppermute x2, waiting for transfers between devices: 1.83 us -> 0.09 us  [gather_blocks(): lax.ppermute(payload, 'xz', [(i, i ^ stage) for i in range(count)])]
    ppermute x2, starting transfers between devices: 4.23 us -> 5.06 us  [gather_blocks(): lax.ppermute(payload, 'xz', [(i, i ^ stage) for i in range(count)])]
    ppermute x6, waiting for transfers between devices: 0.52 us -> 0.07 us  [swap_rows(): return [lax.ppermute(a, 'gy', y_pairs[i]) for i, a in enumerate(pair)]]
    ppermute x6, starting transfers between devices: 7.37 us -> 7.8 us  [swap_planes(): lax.ppermute((pair[i] * scale).astype(f16), 'xz', x_pairs[i])]
  transfers between devices with their start and end apart: 14 -> 14, of which waited for: 2 -> 2; matrix products, arithmetic and copies ran while one was open for 1% -> 1% of each run, Pallas kernels for 29% -> 35%
where the time goes in v3:
time: 34.8 us; the launch traced here: 34.3 us
  starting transfers between devices  18.6 us (53%)
  Pallas kernels  14.8 us (43%)
    pallas_call x8, Pallas kernels, call(): pl.pallas_call(kernel, out_shape=shapes, in_specs=specs, out_specs=out_sp...  12.7 us
    ppermute x6, starting transfers between devices, swap_planes(): lax.ppermute((pair[i] * scale).astype(f16), 'xz', x_pairs[i])  7.8 us
    ppermute x6, starting transfers between devices, swap_rows(): return [lax.ppermute(a, 'gy', y_pairs[i]) for i, a in enumerate(pair)]  5.77 us
    ppermute x2, starting transfers between devices, gather_blocks(): lax.ppermute(payload, 'xz', [(i, i ^ stage) for i in range(count)])  5.06 us
    pallas_call x1, Pallas kernels, per_device(): pl.pallas_call(pack_planes_kernel, out_shape=[pltpu.VMEM((6, rows, depth)...  2.06 us
  transfers between devices with their start and end apart: 14, of which 2 were waited for; matrix products, arithmetic and copies ran while one was open for 1% of the time, Pallas kernels for 35%

profile of v3, /device:TPU:1, one launch (start us, length us, event | category | flops | bytes accessed | tf_op | source)
XLA Modules:
  0.0 34.3 jit_solution(7047464492727602665)
XLA Ops:
  0.0 3.1 %collective-permute-start = (bf16[1,3,64,256]{3,2,1,0:T(8,128)(2,1)}, bf16[1,3,64,256]{3,2,1,0:T(8,128)(2,1)S(1)}, u32[]{:S(2)}, u32[]{:S(2)}) collective-permute-start(bf16[1,3,64,256]{3,2,1,0:T(8,128)(2,1)} %refs_0_.1), channel_id=1, source_target_pairs={{0,8},{4,12},{8,0},{12,4},{1,9},{5,13},{9,1},{13,5},{2,10},{6,14},... | collective-permute-start | bytes 294920 | tf_op jit(solution)/shard_map/ppermute | solution.py:306
  3.1 0.1 stack.51.pos.refs_0_
  3.2 0.0 copy-start
  3.2 0.0 copy-start.1
  3.2 2.1 %shard_map.64 = (f32[6,64,256]{2,1,0:T(8,128)S(1)}, f32[6,64,256]{2,1,0:T(8,128)S(1)}) custom-call(s32[8]{0:T(128)S(1)} %stack.51.pos.refs_0_, f32[3,8,64,256]{3,2,1,0:T(8,128)} %refs_5_, f32[3,8,64,256]{3,2,1,0:T(8,128)} %refs_4_), custom_call_target="tpu_custom_call" | custom-call | tf_op jit(solution)/shard_map/pallas_call | solution.py:351
  5.3 1.4 %collective-permute-start.1 = (f16[6,64,256]{2,1,0:T(8,128)(2,1)S(1)}, f16[6,64,256]{2,1,0:T(8,128)(2,1)S(1)}, u32[]{:S(2)}, u32[]{:S(2)}) collective-permute-start(f16[6,64,256]{2,1,0:T(8,128)(2,1)S(1)} %multiply_convert_fusion.1), channel_id=1, source_target_pairs={{0,4},{4,0},{8,12},{12,8},{1,5},{5,1},{9,13},{13,9},{2,6},{6,2},{1... | collective-permute-start | bytes 589832 | tf_op jit(solution)/shard_map/ppermute | solution.py:342
  6.7 0.0 copy-start.2
  6.8 0.0 copy-start.3
  6.8 0.0 copy-start.4
  6.8 0.8 %collective-permute-start.2 = (f16[6,64,256]{2,1,0:T(8,128)(2,1)S(1)}, f16[6,64,256]{2,1,0:T(8,128)(2,1)S(1)}, u32[]{:S(2)}, u32[]{:S(2)}) collective-permute-start(f16[6,64,256]{2,1,0:T(8,128)(2,1)S(1)} %multiply_convert_fusion), channel_id=1, source_target_pairs={{0,0},{4,8},{8,4},{12,12},{1,1},{5,9},{9,5},{13,13},{2,2},{6,10},{... | collective-permute-start | bytes 589832 | tf_op jit(solution)/shard_map/ppermute | solution.py:342
  7.6 0.0 copy-done
  7.6 0.0 copy-done.1
  7.6 0.6 %shard_map.66 = (f32[6,8,256]{2,1,0:T(8,128)S(1)}, f32[6,8,256]{2,1,0:T(8,128)S(1)}) custom-call(s32[8]{0:T(128)S(1)} %stack.51.pos.refs_0_, f32[3,8,64,256]{3,2,1,0:T(8,128)S(1)} %copy-done.1, f32[3,8,64,256]{3,2,1,0:T(8,128)S(1)} %copy-done), custom_call_target="tpu_custom_call" | custom-call | tf_op jit(solution)/shard_map/pallas_call | solution.py:43
  8.2 1.3 %collective-permute-start.3 = (f32[6,8,256]{2,1,0:T(8,128)S(1)}, f32[6,8,256]{2,1,0:T(8,128)S(1)}, u32[]{:S(2)}, u32[]{:S(2)}) collective-permute-start(f32[6,8,256]{2,1,0:T(8,128)S(1)} %get-tuple-element.43), channel_id=1, source_target_pairs={{0,1},{1,0},{2,3},{3,2},{4,5},{5,4},{6,7},{7,6},{8,9},{9,8},{10,11... | collective-permute-start | bytes 147464 | tf_op jit(solution)/shard_map/ppermute | solution.py:346
  9.5 1.2 %collective-permute-start.4 = (f32[6,8,256]{2,1,0:T(8,128)S(1)}, f32[6,8,256]{2,1,0:T(8,128)S(1)}, u32[]{:S(2)}, u32[]{:S(2)}) collective-permute-start(f32[6,8,256]{2,1,0:T(8,128)S(1)} %get-tuple-element.44), channel_id=1, source_target_pairs={{0,3},{1,2},{2,1},{3,0},{4,7},{5,6},{6,5},{7,4},{8,11},{9,10},{10,... | collective-permute-start | bytes 147464 | tf_op jit(solution)/shard_map/ppermute | solution.py:346
  10.7 0.0 collective-permute-done.refs_1_
  10.7 0.0 copy-done.2
  10.7 1.9 %collective-permute-start.5 = (bf16[2,3,64,256]{3,2,1,0:T(8,128)(2,1)S(1)}, bf16[2,3,64,256]{3,2,1,0:T(8,128)(2,1)S(1)}, u32[]{:S(2)}, u32[]{:S(2)}) collective-permute-start(bf16[2,3,64,256]{3,2,1,0:T(8,128)(2,1)S(1)} %pad_maximum_fusion), channel_id=1, source_target_pairs={{0,4},{4,0},{8,12},{12,8},{1,5},{5,1},{9,13},{13,9},{2,6},{6,2},{1... | collective-permute-start | bytes 589832 | tf_op jit(solution)/shard_map/ppermute | solution.py:306
  12.6 0.0 copy-done.3
  12.6 0.0 copy-done.4
  12.6 2.9 %shard_map.65 = (f32[3,8,64,256]{3,2,1,0:T(8,128)S(1)}, f32[9,8,64,256]{3,2,1,0:T(8,128)S(1)}) custom-call(s32[8]{0:T(128)S(1)} %stack.51.pos.refs_0_, s32[3]{0:T(128)S(1)} %copy-done.4, s32[4,2,32]{2,1,0:T(2,128)S(1)} %bitcast.10, f32[3,8,64,256]{3,2,1,0:T(8,128)S(1)} %copy-done.1, f32[3,8,64,256]{3,2,1,0:T(8,128)S(1)} %copy-done), custom_call_target="tpu_custom_call" | custom-call | flops 15728640 | bytes 3932160 | tf_op jit(solution)/shard_map/pallas_call | solution.py:43
  15.6 0.0 collective-permute-done.1
  15.6 0.0 collective-permute-done.2
  15.7 0.0 collective-permute-done.3.refs_9_
  15.7 0.0 collective-permute-done.4.refs_10_
  15.7 0.9 %shard_map.67 = (f32[3,8,64,256]{3,2,1,0:T(8,128)S(1)}, f32[9,8,64,256]{3,2,1,0:T(8,128)S(1)}, f32[3,64,256]{2,1,0:T(8,128)S(1)}, f32[3,64,256]{2,1,0:T(8,128)S(1)}) custom-call(s32[8]{0:T(128)S(1)} %stack.51.pos.refs_0_, s32[3]{0:T(128)S(1)} %copy-done.4, s32[4,2,32]{2,1,0:T(2,128)S(1)} %bitcast.11, ...), custom_call_target="tpu_custom_call", output_to_operand_aliasing={{0}: (3, {}), {1}: (4, {})} | custom-call | flops 1572864 | bytes 393216 | tf_op jit(solution)/shard_map/pallas_call | solution.py:43
  16.7 0.1 collective-permute-start.6
  16.8 0.7 %collective-permute-start.9 = (f16[3,64,256]{2,1,0:T(8,128)(2,1)S(1)}, f16[3,64,256]{2,1,0:T(8,128)(2,1)S(1)}, u32[]{:S(2)}, u32[]{:S(2)}) collective-permute-start(f16[3,64,256]{2,1,0:T(8,128)(2,1)S(1)} %multiply_convert_fusion.4), channel_id=1, source_target_pairs={{0,0},{4,8},{8,4},{12,12},{1,1},{5,9},{9,5},{13,13},{2,2},{6,10},{... | collective-permute-start | bytes 294920 | tf_op jit(solution)/shard_map/ppermute | solution.py:342
  17.4 0.1 collective-permute-done.5.refs_2_
  17.5 1.1 %shard_map.68 = (f32[5,3,64,256]{3,2,1,0:T(8,128)S(1)}, f32[3,8,64,256]{3,2,1,0:T(8,128)S(1)}, f32[3,8,256]{2,1,0:T(8,128)S(1)}, f32[3,8,256]{2,1,0:T(8,128)S(1)}) custom-call(s32[8]{0:T(128)S(1)} %stack.51.pos.refs_0_, s32[3]{0:T(128)S(1)} %copy-done.4, s32[4,2,32]{2,1,0:T(2,128)S(1)} %bitcast.12, ...), custom_call_target="tpu_custom_call", output_to_operand_aliasing={{1}: (3, {})} | custom-call | flops 1572864 | bytes 393216 | tf_op jit(solution)/shard_map/pallas_call | solution.py:43
  18.6 1.0 %collective-permute-start.7 = (f32[3,8,256]{2,1,0:T(8,128)S(1)}, f32[3,8,256]{2,1,0:T(8,128)S(1)}, u32[]{:S(2)}, u32[]{:S(2)}) collective-permute-start(f32[3,8,256]{2,1,0:T(8,128)S(1)} %get-tuple-element.51), channel_id=1, source_target_pairs={{0,1},{1,0},{2,3},{3,2},{4,5},{5,4},{6,7},{7,6},{8,9},{9,8},{10,11... | collective-permute-start | bytes 73736 | tf_op jit(solution)/shard_map/ppermute | solution.py:346
  19.7 1.0 %collective-permute-start.8 = (f32[3,8,256]{2,1,0:T(8,128)S(1)}, f32[3,8,256]{2,1,0:T(8,128)S(1)}, u32[]{:S(2)}, u32[]{:S(2)}) collective-permute-start(f32[3,8,256]{2,1,0:T(8,128)S(1)} %get-tuple-element.52), channel_id=1, source_target_pairs={{0,3},{1,2},{2,1},{3,0},{4,7},{5,6},{6,5},{7,4},{8,11},{9,10},{10,... | collective-permute-start | bytes 73736 | tf_op jit(solution)/shard_map/ppermute | solution.py:346
  20.7 2.3 %shard_map.69.refs_3_ = f32[3,8,64,256]{3,2,1,0:T(8,128)S(1)} custom-call(s32[8]{0:T(128)S(1)} %stack.51.pos.refs_0_, s32[3]{0:T(128)S(1)} %copy-done.4, s32[4,2,32]{2,1,0:T(2,128)S(1)} %bitcast.13, f32[3,8,64,256]{3,2,1,0:T(8,128)S(1)} %get-tuple-element.47.w, f32[3,8,64,256]{3,2,1,0:T(8,128)S(1)} %copy-done, ...), custom_call_target="tpu_custom_call" | custom-call | flops 15728640 | bytes 3932160 | tf_op jit(solution)/shard_map/pallas_call | solution.py:43
  23.0 0.0 collective-permute-done.7.refs_8_
  23.0 0.0 collective-permute-done.8.refs_9_
  23.0 0.0 collective-permute-done.6
  23.0 0.0 collective-permute-done.9
  23.1 0.8 %shard_map.70 = (f32[3,8,64,256]{3,2,1,0:T(8,128)S(1)}, f32[3,64,256]{2,1,0:T(8,128)S(1)}, f32[3,64,256]{2,1,0:T(8,128)S(1)}, f32[3,8,256]{2,1,0:T(8,128)S(1)}, f32[3,8,256]{2,1,0:T(8,128)S(1)}) custom-call(s32[8]{0:T(128)S(1)} %stack.51.pos.refs_0_, s32[3]{0:T(128)S(1)} %copy-done.4, s32[4,2,32]{2,1,0:T(2,128)S(1)} %bitcast.14, ...), custom_call_target="tpu_custom_call", output_to_operand_aliasing={{0}: (3, {})} | custom-call | flops 1572864 | bytes 393216 | tf_op jit(solution)/shard_map/pallas_call | solution.py:43
  23.9 4.2 %collective-permute-start.10 = (f16[3,64,256]{2,1,0:T(8,128)(2,1)S(1)}, f16[3,64,256]{2,1,0:T(8,128)(2,1)S(1)}, u32[]{:S(2)}, u32[]{:S(2)}) collective-permute-start(f16[3,64,256]{2,1,0:T(8,128)(2,1)S(1)} %multiply_convert_fusion.3), channel_id=1, source_target_pairs={{0,4},{4,0},{8,12},{12,8},{1,5},{5,1},{9,13},{13,9},{2,6},{6,2},{1... | collective-permute-start | bytes 294920 | tf_op jit(solution)/shard_map/ppermute | solution.py:342
  28.1 0.7 %collective-permute-start.11 = (f16[3,64,256]{2,1,0:T(8,128)(2,1)S(1)}, f16[3,64,256]{2,1,0:T(8,128)(2,1)S(1)}, u32[]{:S(2)}, u32[]{:S(2)}) collective-permute-start(f16[3,64,256]{2,1,0:T(8,128)(2,1)S(1)} %multiply_convert_fusion.2), channel_id=1, source_target_pairs={{0,0},{4,8},{8,4},{12,12},{1,1},{5,9},{9,5},{13,13},{2,2},{6,10},{... | collective-permute-start | bytes 294920 | tf_op jit(solution)/shard_map/ppermute | solution.py:342
  28.8 0.4 %collective-permute-start.12 = (f32[3,8,256]{2,1,0:T(8,128)S(1)}, f32[3,8,256]{2,1,0:T(8,128)S(1)}, u32[]{:S(2)}, u32[]{:S(2)}) collective-permute-start(f32[3,8,256]{2,1,0:T(8,128)S(1)} %get-tuple-element.60), channel_id=1, source_target_pairs={{0,1},{1,0},{2,3},{3,2},{4,5},{5,4},{6,7},{7,6},{8,9},{9,8},{10,11... | collective-permute-start | bytes 73736 | tf_op jit(solution)/shard_map/ppermute | solution.py:346
  29.2 0.8 %collective-permute-start.13 = (f32[3,8,256]{2,1,0:T(8,128)S(1)}, f32[3,8,256]{2,1,0:T(8,128)S(1)}, u32[]{:S(2)}, u32[]{:S(2)}) collective-permute-start(f32[3,8,256]{2,1,0:T(8,128)S(1)} %get-tuple-element.61), channel_id=1, source_target_pairs={{0,3},{1,2},{2,1},{3,0},{4,7},{5,6},{6,5},{7,4},{8,11},{9,10},{10,... | collective-permute-start | bytes 73736 | tf_op jit(solution)/shard_map/ppermute | solution.py:346
  30.1 2.3 %shard_map.71.refs_3_ = f32[3,8,64,256]{3,2,1,0:T(8,128)S(1)} custom-call(s32[8]{0:T(128)S(1)} %stack.51.pos.refs_0_, s32[3]{0:T(128)S(1)} %copy-done.4, s32[4,2,32]{2,1,0:T(2,128)S(1)} %bitcast.15, f32[3,8,64,256]{3,2,1,0:T(8,128)S(1)} %get-tuple-element.57.w, f32[3,8,64,256]{3,2,1,0:T(8,128)S(1)} %copy-done, ...), custom_call_target="tpu_custom_call" | custom-call | flops 15728640 | bytes 3932160 | tf_op jit(solution)/shard_map/pallas_call | solution.py:43
  32.3 0.0 collective-permute-done.10
  32.4 0.0 collective-permute-done.11
  32.4 0.0 collective-permute-done.12.refs_7_
  32.4 0.1 collective-permute-done.13.refs_8_
  32.5 1.8 %shard_map.72 = (f32[3,8,64,256]{3,2,1,0:T(8,128)S(1)}, f32[3,8,64,256]{3,2,1,0:T(8,128)}) custom-call(s32[8]{0:T(128)S(1)} %stack.51.pos.refs_0_, s32[3]{0:T(128)S(1)} %copy-done.4, s32[4,2,32]{2,1,0:T(2,128)S(1)} %bitcast.16, f32[3,8,64,256]{3,2,1,0:T(8,128)S(1)} %shard_map.71.refs_3_, ...), custom_call_target="tpu_custom_call", output_to_operand_aliasing={{0}: (3, {})} | custom-call | flops 1572864 | bytes 393216 | tf_op jit(solution)/shard_map/pallas_call | solution.py:43
  (13 shorter events, 0.3 us)
Async XLA Ops:
  0.0 10.7 %collective-permute-start = (bf16[1,3,64,256]{3,2,1,0:T(8,128)(2,1)}, bf16[1,3,64,256]{3,2,1,0:T(8,128)(2,1)S(1)}, u32[]{:S(2)}, u32[]{:S(2)}) collective-permute-start(bf16[1,3,64,256]{3,2,1,0:T(8,128)(2,1)} %refs_0_.1), channel_id=1, source_target_pairs={{0,8},{4,12},{8,0},{12,4},{1,9},{5,13},{9,1},{13,5},{2,10},{6,14},... | collective-permute-start | bytes 294920 | tf_op jit(solution)/shard_map/ppermute | solution.py:306
  3.2 4.4 %copy-start = (f32[3,8,64,256]{3,2,1,0:T(8,128)S(1)}, f32[3,8,64,256]{3,2,1,0:T(8,128)}, u32[]{:S(2)}) copy-start(f32[3,8,64,256]{3,2,1,0:T(8,128)} %refs_4_) | copy-start | bytes 4718596
  3.2 4.4 %copy-start.1 = (f32[3,8,64,256]{3,2,1,0:T(8,128)S(1)}, f32[3,8,64,256]{3,2,1,0:T(8,128)}, u32[]{:S(2)}) copy-start(f32[3,8,64,256]{3,2,1,0:T(8,128)} %refs_5_) | copy-start | bytes 4718596
  5.3 10.3 %collective-permute-start.1 = (f16[6,64,256]{2,1,0:T(8,128)(2,1)S(1)}, f16[6,64,256]{2,1,0:T(8,128)(2,1)S(1)}, u32[]{:S(2)}, u32[]{:S(2)}) collective-permute-start(f16[6,64,256]{2,1,0:T(8,128)(2,1)S(1)} %multiply_convert_fusion.1), channel_id=1, source_target_pairs={{0,4},{4,0},{8,12},{12,8},{1,5},{5,1},{9,13},{13,9},{2,6},{6,2},{1... | collective-permute-start | bytes 589832 | tf_op jit(solution)/shard_map/ppermute | solution.py:342
  6.7 4.0 %copy-start.2 = (bf16[1,3,64,256]{3,2,1,0:T(8,128)(2,1)S(1)}, bf16[1,3,64,256]{3,2,1,0:T(8,128)(2,1)}, u32[]{:S(2)}) copy-start(bf16[1,3,64,256]{3,2,1,0:T(8,128)(2,1)} %refs_0_.1) | copy-start | bytes 294916
  6.8 5.9 %copy-start.3 = (s32[4,32,2]{1,2,0:T(2,128)S(1)}, s32[4,32,2]{1,2,0:T(2,128)}, u32[]{:S(2)}) copy-start(s32[4,32,2]{1,2,0:T(2,128)} %param.9) | copy-start | bytes 3076
  6.8 5.9 %copy-start.4 = (s32[3]{0:T(128)S(1)}, s32[3]{0:T(128)}, u32[]{:S(2)}) copy-start(s32[3]{0:T(128)} %refs_1_.5) | copy-start | bytes 40
  6.8 8.9 %collective-permute-start.2 = (f16[6,64,256]{2,1,0:T(8,128)(2,1)S(1)}, f16[6,64,256]{2,1,0:T(8,128)(2,1)S(1)}, u32[]{:S(2)}, u32[]{:S(2)}) collective-permute-start(f16[6,64,256]{2,1,0:T(8,128)(2,1)S(1)} %multiply_convert_fusion), channel_id=1, source_target_pairs={{0,0},{4,8},{8,4},{12,12},{1,1},{5,9},{9,5},{13,13},{2,2},{6,10},{... | collective-permute-start | bytes 589832 | tf_op jit(solution)/shard_map/ppermute | solution.py:342
  8.2 7.5 %collective-permute-start.3 = (f32[6,8,256]{2,1,0:T(8,128)S(1)}, f32[6,8,256]{2,1,0:T(8,128)S(1)}, u32[]{:S(2)}, u32[]{:S(2)}) collective-permute-start(f32[6,8,256]{2,1,0:T(8,128)S(1)} %get-tuple-element.43), channel_id=1, source_target_pairs={{0,1},{1,0},{2,3},{3,2},{4,5},{5,4},{6,7},{7,6},{8,9},{9,8},{10,11... | collective-permute-start | bytes 147464 | tf_op jit(solution)/shard_map/ppermute | solution.py:346
  9.5 6.2 %collective-permute-start.4 = (f32[6,8,256]{2,1,0:T(8,128)S(1)}, f32[6,8,256]{2,1,0:T(8,128)S(1)}, u32[]{:S(2)}, u32[]{:S(2)}) collective-permute-start(f32[6,8,256]{2,1,0:T(8,128)S(1)} %get-tuple-element.44), channel_id=1, source_target_pairs={{0,3},{1,2},{2,1},{3,0},{4,7},{5,6},{6,5},{7,4},{8,11},{9,10},{10,... | collective-permute-start | bytes 147464 | tf_op jit(solution)/shard_map/ppermute | solution.py:346
  10.7 6.8 %collective-permute-start.5 = (bf16[2,3,64,256]{3,2,1,0:T(8,128)(2,1)S(1)}, bf16[2,3,64,256]{3,2,1,0:T(8,128)(2,1)S(1)}, u32[]{:S(2)}, u32[]{:S(2)}) collective-permute-start(bf16[2,3,64,256]{3,2,1,0:T(8,128)(2,1)S(1)} %pad_maximum_fusion), channel_id=1, source_target_pairs={{0,4},{4,0},{8,12},{12,8},{1,5},{5,1},{9,13},{13,9},{2,6},{6,2},{1... | collective-permute-start | bytes 589832 | tf_op jit(solution)/shard_map/ppermute | solution.py:306
  16.7 6.3 %collective-permute-start.6 = (f16[3,64,256]{2,1,0:T(8,128)(2,1)S(1)}, f16[3,64,256]{2,1,0:T(8,128)(2,1)S(1)}, u32[]{:S(2)}, u32[]{:S(2)}) collective-permute-start(f16[3,64,256]{2,1,0:T(8,128)(2,1)S(1)} %multiply_convert_fusion.5), channel_id=1, source_target_pairs={{0,4},{4,0},{8,12},{12,8},{1,5},{5,1},{9,13},{13,9},{2,6},{6,2},{1... | collective-permute-start | bytes 294920 | tf_op jit(solution)/shard_map/ppermute | solution.py:342
  16.8 6.2 %collective-permute-start.9 = (f16[3,64,256]{2,1,0:T(8,128)(2,1)S(1)}, f16[3,64,256]{2,1,0:T(8,128)(2,1)S(1)}, u32[]{:S(2)}, u32[]{:S(2)}) collective-permute-start(f16[3,64,256]{2,1,0:T(8,128)(2,1)S(1)} %multiply_convert_fusion.4), channel_id=1, source_target_pairs={{0,0},{4,8},{8,4},{12,12},{1,1},{5,9},{9,5},{13,13},{2,2},{6,10},{... | collective-permute-start | bytes 294920 | tf_op jit(solution)/shard_map/ppermute | solution.py:342
  18.6 4.3 %collective-permute-start.7 = (f32[3,8,256]{2,1,0:T(8,128)S(1)}, f32[3,8,256]{2,1,0:T(8,128)S(1)}, u32[]{:S(2)}, u32[]{:S(2)}) collective-permute-start(f32[3,8,256]{2,1,0:T(8,128)S(1)} %get-tuple-element.51), channel_id=1, source_target_pairs={{0,1},{1,0},{2,3},{3,2},{4,5},{5,4},{6,7},{7,6},{8,9},{9,8},{10,11... | collective-permute-start | bytes 73736 | tf_op jit(solution)/shard_map/ppermute | solution.py:346
  19.7 3.3 %collective-permute-start.8 = (f32[3,8,256]{2,1,0:T(8,128)S(1)}, f32[3,8,256]{2,1,0:T(8,128)S(1)}, u32[]{:S(2)}, u32[]{:S(2)}) collective-permute-start(f32[3,8,256]{2,1,0:T(8,128)S(1)} %get-tuple-element.52), channel_id=1, source_target_pairs={{0,3},{1,2},{2,1},{3,0},{4,7},{5,6},{6,5},{7,4},{8,11},{9,10},{10,... | collective-permute-start | bytes 73736 | tf_op jit(solution)/shard_map/ppermute | solution.py:346
  23.9 8.4 %collective-permute-start.10 = (f16[3,64,256]{2,1,0:T(8,128)(2,1)S(1)}, f16[3,64,256]{2,1,0:T(8,128)(2,1)S(1)}, u32[]{:S(2)}, u32[]{:S(2)}) collective-permute-start(f16[3,64,256]{2,1,0:T(8,128)(2,1)S(1)} %multiply_convert_fusion.3), channel_id=1, source_target_pairs={{0,4},{4,0},{8,12},{12,8},{1,5},{5,1},{9,13},{13,9},{2,6},{6,2},{1... | collective-permute-start | bytes 294920 | tf_op jit(solution)/shard_map/ppermute | solution.py:342
  28.1 4.2 %collective-permute-start.11 = (f16[3,64,256]{2,1,0:T(8,128)(2,1)S(1)}, f16[3,64,256]{2,1,0:T(8,128)(2,1)S(1)}, u32[]{:S(2)}, u32[]{:S(2)}) collective-permute-start(f16[3,64,256]{2,1,0:T(8,128)(2,1)S(1)} %multiply_convert_fusion.2), channel_id=1, source_target_pairs={{0,0},{4,8},{8,4},{12,12},{1,1},{5,9},{9,5},{13,13},{2,2},{6,10},{... | collective-permute-start | bytes 294920 | tf_op jit(solution)/shard_map/ppermute | solution.py:342
  28.8 3.6 %collective-permute-start.12 = (f32[3,8,256]{2,1,0:T(8,128)S(1)}, f32[3,8,256]{2,1,0:T(8,128)S(1)}, u32[]{:S(2)}, u32[]{:S(2)}) collective-permute-start(f32[3,8,256]{2,1,0:T(8,128)S(1)} %get-tuple-element.60), channel_id=1, source_target_pairs={{0,1},{1,0},{2,3},{3,2},{4,5},{5,4},{6,7},{7,6},{8,9},{9,8},{10,11... | collective-permute-start | bytes 73736 | tf_op jit(solution)/shard_map/ppermute | solution.py:346
  29.2 3.3 %collective-permute-start.13 = (f32[3,8,256]{2,1,0:T(8,128)S(1)}, f32[3,8,256]{2,1,0:T(8,128)S(1)}, u32[]{:S(2)}, u32[]{:S(2)}) collective-permute-start(f32[3,8,256]{2,1,0:T(8,128)S(1)} %get-tuple-element.61), channel_id=1, source_target_pairs={{0,3},{1,2},{2,1},{3,0},{4,7},{5,6},{6,5},{7,4},{8,11},{9,10},{10,... | collective-permute-start | bytes 73736 | tf_op jit(solution)/shard_map/ppermute | solution.py:346

commit v4 on v3

--- a/solution.py
+++ b/solution.py
@@ -33,7 +33,7 @@
     return pltpu.with_memory_space_constraint(x, pltpu.HBM)
 
 
-def call(kernel, outs, *args, smem=1, aliases=None, cost=None, hbm_out=False, scratch=()):
+def call(kernel, outs, *args, smem=0, aliases=None, cost=None, hbm_out=False, scratch=()):
     specs = [SMEM] * smem + [VMEM] * (len(args) - smem)
     args = args[:smem] + tuple(in_vmem(a) for a in args[smem:])
     shapes = [pltpu.VMEM(o.shape, o.dtype) for o in outs]
@@ -52,13 +52,13 @@
     )(*args)
 
 
-def pack_planes(pos, field, out_refs):
+def pack_planes(pos, field, out_refs, first=0):
     even = pos[0] == 0
     last = field.shape[1] - 1
     toward_first = jnp.where(even, last, 0)
     for out, plane in ((out_refs[0], toward_first), (out_refs[1], last - toward_first)):
         for c in range(3):
-            out[c] = field[c, plane]
+            out[first + c] = field[c, plane]
 
 
 def pack_rows(pos, field, out_refs, first=0):
@@ -70,26 +70,35 @@
         out_refs[1][first + c] = jnp.where(even, low, high)
 
 
-def pack_planes_kernel(pos, w, v, x1, x2, sems):
-    planes = w.shape[1]
-    toward_first = jnp.where(pos[0] == 0, planes - 1, 0)
+def load_kernel(position, w_in, v_in, w, v, x1, x2, y1, y2, sems):
+    pos = position()
+    last = w.shape[1] - 1
     copies = []
-    for first, field in ((0, w), (3, v)):
-        for out, plane in ((x1, toward_first), (x2, planes - 1 - toward_first)):
-            one = pltpu.make_async_copy(field.at[:, plane], out.at[pl.ds(first, 3)], sems.at[len(copies)])
-            one.start()
-            copies.append(one)
-    for one in copies:
+
+    def load(source, target):
+        copies.append(pltpu.make_async_copy(source, target, sems.at[len(copies)]))
+        copies[-1].start()
+
+    for source, target in ((w_in, w), (v_in, v)):
+        for plane in (0, last):
+            load(source.at[:, plane], target.at[:, plane])
+    inner = pl.ds(1, last - 1)
+    for source, target in ((w_in, w), (v_in, v)):
+        for c in range(3):
+            load(source.at[c, inner], target.at[c, inner])
+    for one in copies[:4]:
         one.wait()
-
-
-def pack_rows_kernel(pos, w, v, y1, y2):
-    pack_rows(pos, w, (y1, y2), 0)
-    pack_rows(pos, v, (y1, y2), 3)
-
-
-def gather_kernel(slots, slot, order, pos, azimuth, incidence, field, *refs):
+    pack_planes(pos, w, (x1, x2), 0)
+    pack_planes(pos, v, (x1, x2), 3)
+    for i, field in enumerate((w, v)):
+        for one in copies[4 + 3 * i : 7 + 3 * i]:
+            one.wait()
+        pack_rows(pos, field, (y1, y2), 3 * i)
+
+
+def gather_kernel(slots, slot, order, position, azimuth, incidence, field, *refs):
     *parts, table, out, py1, py2 = refs
+    pos = position()
     per = sum(part.shape[0] for part in parts) // len(order)
     places = [p * per + b for p in order for b in range(per)]
     for part in parts:
@@ -128,11 +137,12 @@
     return out
 
 
-def local_kernel(step, slots, slot, pos, azimuth, incidence, w, v, *refs):
+def local_kernel(step, slots, slot, position, *refs):
     if step:
-        table, grad, out = refs
+        azimuth, incidence, w, v, table, grad, out = refs
+        pos = position()
     else:
-        out, grad = refs
+        w, v, out, grad = refs
     planes, rows, depth = w.shape[1:]
     slabs = range(depth // LANES)
     chunks = rows // ROWS
@@ -205,8 +215,11 @@
     lax.fori_loop(0, planes, plane_body, 0)
 
 
-def fix_kernel(step, slots, slot, final, *refs):
-    pos, azimuth, incidence, new, *refs = refs
+def fix_kernel(step, slots, slot, position, final, *refs):
+    if step == 1:
+        azimuth, incidence, *refs = refs
+    pos = position()
+    new, *refs = refs
     if step:
         if step == 1:
             table, *refs = refs
@@ -316,21 +329,22 @@
     count, side_count = lax.axis_size("xz"), lax.axis_size("gy")
     per = sources.shape[0]
     blocks = count * per
-    z = lax.axis_index("xz")
-    y = lax.axis_index("gy")
-    low_z, high_z = z > 0, z < count - 1
-    pos = jnp.stack(
-        [
+
+    def position():
+        z, y = lax.axis_index("xz"), lax.axis_index("gy")
+        even = z % 2 == 0
+        low, high = (z > 0).astype(jnp.int32), (z < count - 1).astype(jnp.int32)
+        return [
             z % 2,
             y % 2,
             z * planes,
             0 if count & (count - 1) else z,
-            jnp.where(z % 2 == 0, high_z, low_z),
-            jnp.where(z % 2 == 0, low_z, high_z),
-            y > 0,
-            y < side_count - 1,
+            jnp.where(even, high, low),
+            jnp.where(even, low, high),
+            (y > 0).astype(jnp.int32),
+            (y < side_count - 1).astype(jnp.int32),
         ]
-    ).astype(jnp.int32)
+
     incidence = jnp.transpose(incidence, (0, 2, 1))
     x_pairs, y_pairs = swaps("xz", False), swaps("gy", True)
     where = functools.partial(slot_of_table, blocks, per)
@@ -348,46 +362,46 @@
     work = 3 * planes * rows * depth * 40
     whole = shape(3, planes, rows, depth)
     parts, order = gather_blocks(sources)
-    planes_out = pl.pallas_call(
-        pack_planes_kernel,
-        out_shape=[pltpu.VMEM((6, rows, depth), f32)] * 2,
-        in_specs=[SMEM, FIXED_HBM, FIXED_HBM],
-        out_specs=[VMEM] * 2,
-        scratch_shapes=[pltpu.SemaphoreType.DMA((4,))],
+    vorticity, velocity, *sends = pl.pallas_call(
+        functools.partial(load_kernel, position),
+        out_shape=[pltpu.VMEM(whole.shape, f32)] * 2
+        + [pltpu.VMEM((6, rows, depth), f32)] * 2
+        + [pltpu.VMEM((6, planes, depth), f32)] * 2,
+        in_specs=[FIXED_HBM, FIXED_HBM],
+        out_specs=[VMEM] * 6,
+        scratch_shapes=[pltpu.SemaphoreType.DMA((10,))],
         compiler_params=pltpu.CompilerParams(vmem_limit_bytes=VMEM_LIMIT),
-    )(pos, in_hbm(vorticity), in_hbm(velocity))
-    vorticity, velocity, planes_out = lax.optimization_barrier((vorticity, velocity, planes_out))
-    rows_out = call(pack_rows_kernel, [shape(6, planes, depth)] * 2, pos, vorticity, velocity)
+    )(in_hbm(vorticity), in_hbm(velocity))
     scale = jnp.array([field_scales[0]] * 3 + [velocity_scale] * 3, f32)[:, None, None]
-    halo = swap_planes(planes_out, scale)
-    side = swap_rows(rows_out)
+    halo = swap_planes(sends[:2], scale)
+    side = swap_rows(sends[2:])
     field = vorticity
-    small = (pos, azimuth, incidence)
+    small = (azimuth, incidence)
     grads = shape(9, planes, rows, depth)
+    send_x, send_y = [shape(3, rows, depth)] * 2, [shape(3, planes, depth)] * 2
     for step in range(steps):
         final = step == steps - 1
-        local = functools.partial(local_kernel, step, slots, where)
-        fix = functools.partial(fix_kernel, step, slots, where, final)
-        send_x, send_y = [shape(3, rows, depth)] * 2, [shape(3, planes, depth)] * 2
+        local = functools.partial(local_kernel, step, slots, where, position)
+        fix = functools.partial(fix_kernel, step, slots, where, position, final)
         if step:
-            (new,) = call(local, [whole], *small, field, velocity, table, grad, smem=3, cost=work)
-            if step == 1:
+            (new,) = call(local, [whole], *small, field, velocity, table, grad, smem=2, cost=work)
+            first = step == 1
+            if first:
                 one, *side = lax.optimization_barrier((jnp.ones((1, 1, depth), f32), *side))
                 halo = [a.astype(f32) * one for a in halo]
             else:
                 halo = [a.astype(f32) for a in halo]
-            extra = [table] if step == 1 else []
             result = call(
                 fix,
                 [whole, whole] if final else [whole] + send_x + send_y,
-                *small,
+                *(small if first else ()),
                 new,
-                *extra,
+                *([table] if first else []),
                 velocity,
                 *halo,
                 *side,
-                smem=3,
-                aliases={3: 0},
+                smem=2 if first else 0,
+                aliases={2 if first else 0: 0},
                 cost=work // 10,
                 hbm_out=final,
                 scratch=[pltpu.SemaphoreType.DMA((11,))] if final else (),
@@ -398,21 +412,19 @@
             halo = swap_planes(result[1:3], field_scales[step + 1])
             side = swap_rows(result[3:5])
         else:
-            gate, parts[1] = lax.optimization_barrier((pos, parts[1]))
-            new, grad = call(local, [whole, grads], gate, azimuth, incidence, field, velocity, smem=3, cost=work)
+            held, parts[1] = lax.optimization_barrier((field, parts[1]))
+            new, grad = call(local, [whole, grads], held, velocity, cost=work)
             args = (new, grad, field, velocity, *[a.astype(f32) for a in halo], *side)
-            new, grad, *ready = call(
-                fix, [whole, grads] + send_x, *small, *args, smem=3, aliases={3: 0, 4: 1}, cost=work // 10
-            )
+            new, grad, *ready = call(fix, [whole, grads] + send_x, *args, aliases={0: 0, 1: 1}, cost=work // 10)
             halo = swap_planes(ready, field_scales[1])
             table, field, *ready = call(
-                functools.partial(gather_kernel, slots, where, order),
+                functools.partial(gather_kernel, slots, where, order, position),
                 [shape(blocks + 1, 3, rows, depth), whole] + send_y,
                 *small,
                 new,
                 *parts,
-                smem=3,
-                aliases={3: 1},
+                smem=2,
+                aliases={2: 1},
                 cost=work // 10,
             )
             side = swap_rows(ready)

time: 34.8 us -> 32.1 us (0.922)
  the two profiles are of different devices: /device:TPU:1 before, /device:TPU:9 now
where the time goes in v4:
time: 32.1 us; the launch traced here: 32 us
  starting transfers between devices  18 us (56%)
  Pallas kernels  12.2 us (38%)
  waiting for transfers between devices  1.18 us (4%)
    pallas_call x7, Pallas kernels, call(): pl.pallas_call(kernel, out_shape=shapes, in_specs=specs, out_specs=out_sp...  10.1 us
    ppermute x6, starting transfers between devices, swap_planes(): lax.ppermute((pair[i] * scale).astype(f16), 'xz', x_pairs[i])  9.58 us
    ppermute x6, starting transfers between devices, swap_rows(): return [lax.ppermute(a, 'gy', y_pairs[i]) for i, a in enumerate(pair)]  6.07 us
    ppermute x2, starting transfers between devices, gather_blocks(): lax.ppermute(payload, 'xz', [(i, i ^ stage) for i in range(count)])  2.38 us
    pallas_call x1, Pallas kernels, per_device(): pl.pallas_call(functools.partial(load_kernel, position), out_shape=[pltpu...  2.05 us
    ppermute x6, waiting for transfers between devices, swap_rows(): return [lax.ppermute(a, 'gy', y_pairs[i]) for i, a in enumerate(pair)]  1.16 us
  transfers between devices with their start and end apart: 14, of which 3 were waited for; matrix products, arithmetic and copies ran while one was open for 1% of the time, Pallas kernels for 32%

profile of v4, /device:TPU:9, one launch (start us, length us, event | category | flops | bytes accessed | tf_op | source)
XLA Modules:
  0.0 32.0 jit_solution(3622087611229910753)
XLA Ops:
  0.0 0.0 copy-start
  0.0 2.3 %collective-permute-start = (bf16[1,3,64,256]{3,2,1,0:T(8,128)(2,1)}, bf16[1,3,64,256]{3,2,1,0:T(8,128)(2,1)S(1)}, u32[]{:S(2)}, u32[]{:S(2)}) collective-permute-start(bf16[1,3,64,256]{3,2,1,0:T(8,128)(2,1)} %refs_0_.4), channel_id=1, source_target_pairs={{0,8},{4,12},{8,0},{12,4},{1,9},{5,13},{9,1},{13,5},{2,10},{6,14},... | collective-permute-start | bytes 294920 | tf_op jit(solution)/shard_map/ppermute | solution.py:319
  2.3 2.1 %shard_map.64 = (f32[3,8,64,256]{3,2,1,0:T(8,128)S(1)}, f32[3,8,64,256]{3,2,1,0:T(8,128)S(1)}, f32[6,64,256]{2,1,0:T(8,128)S(1)}, f32[6,64,256]{2,1,0:T(8,128)S(...) custom-call(f32[3,8,64,256]{3,2,1,0:T(8,128)} %w_in.1, f32[3,8,64,256]{3,2,1,0:T(8,128)} %v_in.1), custom_call_target="tpu_custom_call" | custom-call | tf_op jit(solution)/shard_map/pallas_call | solution.py:365
  4.4 0.2 collective-permute-start.1
  4.7 2.1 %collective-permute-start.2 = (f16[6,64,256]{2,1,0:T(8,128)(2,1)S(1)}, f16[6,64,256]{2,1,0:T(8,128)(2,1)S(1)}, u32[]{:S(2)}, u32[]{:S(2)}) collective-permute-start(f16[6,64,256]{2,1,0:T(8,128)(2,1)S(1)} %multiply_convert_fusion), channel_id=1, source_target_pairs={{0,0},{4,8},{8,4},{12,12},{1,1},{5,9},{9,5},{13,13},{2,2},{6,10},{... | collective-permute-start | bytes 589832 | tf_op jit(solution)/shard_map/ppermute | solution.py:356
  6.8 1.6 %collective-permute-start.3 = (f32[6,8,256]{2,1,0:T(8,128)S(1)}, f32[6,8,256]{2,1,0:T(8,128)S(1)}, u32[]{:S(2)}, u32[]{:S(2)}) collective-permute-start(f32[6,8,256]{2,1,0:T(8,128)S(1)} %get-tuple-element.39), channel_id=1, source_target_pairs={{0,1},{1,0},{2,3},{3,2},{4,5},{5,4},{6,7},{7,6},{8,9},{9,8},{10,11... | collective-permute-start | bytes 147464 | tf_op jit(solution)/shard_map/ppermute | solution.py:360
  8.4 1.2 %collective-permute-start.4 = (f32[6,8,256]{2,1,0:T(8,128)S(1)}, f32[6,8,256]{2,1,0:T(8,128)S(1)}, u32[]{:S(2)}, u32[]{:S(2)}) collective-permute-start(f32[6,8,256]{2,1,0:T(8,128)S(1)} %get-tuple-element.40), channel_id=1, source_target_pairs={{0,3},{1,2},{2,1},{3,0},{4,7},{5,6},{6,5},{7,4},{8,11},{9,10},{10,... | collective-permute-start | bytes 147464 | tf_op jit(solution)/shard_map/ppermute | solution.py:360
  9.5 0.0 collective-permute-done.refs_1_
  9.5 0.0 copy-done
  9.6 0.1 collective-permute-start.5
  9.6 2.2 %shard_map.65 = (f32[3,8,64,256]{3,2,1,0:T(8,128)S(1)}, f32[9,8,64,256]{3,2,1,0:T(8,128)S(1)}) custom-call(f32[3,8,64,256]{3,2,1,0:T(8,128)S(1)} %get-tuple-element.33.refs_0_.refs_2_, f32[3,8,64,256]{3,2,1,0:T(8,128)S(1)} %get-tuple-element.34.refs_1_.refs_3_.refs_4_), custom_call_target="tpu_custom_call" | custom-call | flops 15728640 | bytes 3932160 | tf_op jit(solution)/shard_map/pallas_call | solution.py:43
  11.9 0.0 collective-permute-done.1
  11.9 0.0 collective-permute-done.2
  12.0 0.0 collective-permute-done.3.refs_6_
  12.0 0.2 collective-permute-done.4.refs_7_
  12.2 0.0 copy-start.1
  12.2 0.0 copy-start.2
  12.2 0.3 shard_map.66
  12.5 1.4 %collective-permute-start.6 = (f16[3,64,256]{2,1,0:T(8,128)(2,1)S(1)}, f16[3,64,256]{2,1,0:T(8,128)(2,1)S(1)}, u32[]{:S(2)}, u32[]{:S(2)}) collective-permute-start(f16[3,64,256]{2,1,0:T(8,128)(2,1)S(1)} %multiply_convert_fusion.5), channel_id=1, source_target_pairs={{0,4},{4,0},{8,12},{12,8},{1,5},{5,1},{9,13},{13,9},{2,6},{6,2},{1... | collective-permute-start | bytes 294920 | tf_op jit(solution)/shard_map/ppermute | solution.py:356
  13.9 3.2 %collective-permute-start.9 = (f16[3,64,256]{2,1,0:T(8,128)(2,1)S(1)}, f16[3,64,256]{2,1,0:T(8,128)(2,1)S(1)}, u32[]{:S(2)}, u32[]{:S(2)}) collective-permute-start(f16[3,64,256]{2,1,0:T(8,128)(2,1)S(1)} %multiply_convert_fusion.4), channel_id=1, source_target_pairs={{0,0},{4,8},{8,4},{12,12},{1,1},{5,9},{9,5},{13,13},{2,2},{6,10},{... | collective-permute-start | bytes 294920 | tf_op jit(solution)/shard_map/ppermute | solution.py:356
  17.1 0.0 collective-permute-done.5.refs_2_
  17.1 0.0 copy-done.1
  17.1 0.0 copy-done.2
  17.1 1.1 %shard_map.67 = (f32[5,3,64,256]{3,2,1,0:T(8,128)S(1)}, f32[3,8,64,256]{3,2,1,0:T(8,128)S(1)}, f32[3,8,256]{2,1,0:T(8,128)S(1)}, f32[3,8,256]{2,1,0:T(8,128)S(1)}) custom-call(s32[3]{0:T(128)S(1)} %copy-done.2, s32[4,2,32]{2,1,0:T(2,128)S(1)} %bitcast.2, f32[3,8,64,256]{3,2,1,0:T(8,128)S(1)} %get-tuple-element.41.field, ...), custom_call_target="tpu_custom_call", output_to_operand_aliasing={{1}: (2, {})} | custom-call | flops 1572864 | bytes 393216 | tf_op jit(solution)/shard_map/pallas_call | solution.py:43
  18.2 1.4 %collective-permute-start.7 = (f32[3,8,256]{2,1,0:T(8,128)S(1)}, f32[3,8,256]{2,1,0:T(8,128)S(1)}, u32[]{:S(2)}, u32[]{:S(2)}) collective-permute-start(f32[3,8,256]{2,1,0:T(8,128)S(1)} %get-tuple-element.47), channel_id=1, source_target_pairs={{0,1},{1,0},{2,3},{3,2},{4,5},{5,4},{6,7},{7,6},{8,9},{9,8},{10,11... | collective-permute-start | bytes 73736 | tf_op jit(solution)/shard_map/ppermute | solution.py:360
  19.5 0.4 %collective-permute-start.8 = (f32[3,8,256]{2,1,0:T(8,128)S(1)}, f32[3,8,256]{2,1,0:T(8,128)S(1)}, u32[]{:S(2)}, u32[]{:S(2)}) collective-permute-start(f32[3,8,256]{2,1,0:T(8,128)S(1)} %get-tuple-element.48), channel_id=1, source_target_pairs={{0,3},{1,2},{2,1},{3,0},{4,7},{5,6},{6,5},{7,4},{8,11},{9,10},{10,... | collective-permute-start | bytes 73736 | tf_op jit(solution)/shard_map/ppermute | solution.py:360
  19.9 2.3 %shard_map.68.refs_2_ = f32[3,8,64,256]{3,2,1,0:T(8,128)S(1)} custom-call(s32[3]{0:T(128)S(1)} %copy-done.2, s32[4,2,32]{2,1,0:T(2,128)S(1)} %bitcast.3, f32[3,8,64,256]{3,2,1,0:T(8,128)S(1)} %get-tuple-element.43.refs_2_, f32[3,8,64,256]{3,2,1,0:T(8,128)S(1)} %get-tuple-element.34.refs_1_.refs_3_.refs_4_, ...), custom_call_target="tpu_custom_call" | custom-call | flops 15728640 | bytes 3932160 | tf_op jit(solution)/shard_map/pallas_call | solution.py:43
  22.2 0.0 collective-permute-done.7.refs_7_
  22.2 0.6 %collective-permute-done.8.refs_8_ = f32[3,8,256]{2,1,0:T(8,128)S(1)} collective-permute-done((f32[3,8,256]{2,1,0:T(8,128)S(1)}, f32[3,8,256]{2,1,0:T(8,128)S(1)}, u32[]{:S(2)}, u32[]{:S(2)}) %collective-permute-start.8) | collective-permute-done | bytes 24608 | tf_op jit(solution)/shard_map/ppermute | solution.py:360
  22.8 0.0 collective-permute-done.6
  22.8 0.0 collective-permute-done.9
  22.9 0.8 %shard_map.69 = (f32[3,8,64,256]{3,2,1,0:T(8,128)S(1)}, f32[3,64,256]{2,1,0:T(8,128)S(1)}, f32[3,64,256]{2,1,0:T(8,128)S(1)}, f32[3,8,256]{2,1,0:T(8,128)S(1)}, f32[3,8,256]{2,1,0:T(8,128)S(1)}) custom-call(s32[3]{0:T(128)S(1)} %copy-done.2, s32[4,2,32]{2,1,0:T(2,128)S(1)} %bitcast.4, ...), custom_call_target="tpu_custom_call", output_to_operand_aliasing={{0}: (2, {})} | custom-call | flops 1572864 | bytes 393216 | tf_op jit(solution)/shard_map/pallas_call | solution.py:43
  23.7 0.1 collective-permute-start.10
  23.8 2.6 %collective-permute-start.11 = (f16[3,64,256]{2,1,0:T(8,128)(2,1)S(1)}, f16[3,64,256]{2,1,0:T(8,128)(2,1)S(1)}, u32[]{:S(2)}, u32[]{:S(2)}) collective-permute-start(f16[3,64,256]{2,1,0:T(8,128)(2,1)S(1)} %multiply_convert_fusion.2), channel_id=1, source_target_pairs={{0,0},{4,8},{8,4},{12,12},{1,1},{5,9},{9,5},{13,13},{2,2},{6,10},{... | collective-permute-start | bytes 294920 | tf_op jit(solution)/shard_map/ppermute | solution.py:356
  26.4 1.0 %collective-permute-start.12 = (f32[3,8,256]{2,1,0:T(8,128)S(1)}, f32[3,8,256]{2,1,0:T(8,128)S(1)}, u32[]{:S(2)}, u32[]{:S(2)}) collective-permute-start(f32[3,8,256]{2,1,0:T(8,128)S(1)} %get-tuple-element.56), channel_id=1, source_target_pairs={{0,1},{1,0},{2,3},{3,2},{4,5},{5,4},{6,7},{7,6},{8,9},{9,8},{10,11... | collective-permute-start | bytes 73736 | tf_op jit(solution)/shard_map/ppermute | solution.py:360
  27.5 0.6 %collective-permute-start.13 = (f32[3,8,256]{2,1,0:T(8,128)S(1)}, f32[3,8,256]{2,1,0:T(8,128)S(1)}, u32[]{:S(2)}, u32[]{:S(2)}) collective-permute-start(f32[3,8,256]{2,1,0:T(8,128)S(1)} %get-tuple-element.57), channel_id=1, source_target_pairs={{0,3},{1,2},{2,1},{3,0},{4,7},{5,6},{6,5},{7,4},{8,11},{9,10},{10,... | collective-permute-start | bytes 73736 | tf_op jit(solution)/shard_map/ppermute | solution.py:360
  28.0 2.3 %shard_map.70.refs_0_ = f32[3,8,64,256]{3,2,1,0:T(8,128)S(1)} custom-call(s32[3]{0:T(128)S(1)} %copy-done.2, s32[4,2,32]{2,1,0:T(2,128)S(1)} %bitcast.5, f32[3,8,64,256]{3,2,1,0:T(8,128)S(1)} %get-tuple-element.53.refs_2_, f32[3,8,64,256]{3,2,1,0:T(8,128)S(1)} %get-tuple-element.34.refs_1_.refs_3_.refs_4_, ...), custom_call_target="tpu_custom_call" | custom-call | flops 15728640 | bytes 3932160 | tf_op jit(solution)/shard_map/pallas_call | solution.py:43
  30.3 0.0 collective-permute-done.10
  30.3 0.0 collective-permute-done.11
  30.4 0.0 collective-permute-done.12.refs_4_
  30.4 0.3 %collective-permute-done.13.refs_5_ = f32[3,8,256]{2,1,0:T(8,128)S(1)} collective-permute-done((f32[3,8,256]{2,1,0:T(8,128)S(1)}, f32[3,8,256]{2,1,0:T(8,128)S(1)}, u32[]{:S(2)}, u32[]{:S(2)}) %collective-permute-start.13) | collective-permute-done | bytes 24608 | tf_op jit(solution)/shard_map/ppermute | solution.py:360
  30.7 1.2 %shard_map.71 = (f32[3,8,64,256]{3,2,1,0:T(8,128)S(1)}, f32[3,8,64,256]{3,2,1,0:T(8,128)}) custom-call(f32[3,8,64,256]{3,2,1,0:T(8,128)S(1)} %shard_map.70.refs_0_, f32[3,8,64,256]{3,2,1,0:T(8,128)S(1)} %get-tuple-element.34.refs_1_.refs_3_.refs_4_, f32[3,64,256]{2,1,0:T(8,128)S(1)} %convert_element_type.45.refs_2_, ...), custom_call_target="tpu_custom_call", output_to_operand_aliasing={{0}: (0, {})} | custom-call | flops 1572864 | bytes 393216 | tf_op jit(solution)/shard_map/pallas_call | solution.py:43
  (13 shorter events, 0.3 us)
Async XLA Ops:
  0.0 9.5 %copy-start = (bf16[1,3,64,256]{3,2,1,0:T(8,128)(2,1)S(1)}, bf16[1,3,64,256]{3,2,1,0:T(8,128)(2,1)}, u32[]{:S(2)}) copy-start(bf16[1,3,64,256]{3,2,1,0:T(8,128)(2,1)} %refs_0_.4) | copy-start | bytes 294916
  0.0 9.5 %collective-permute-start = (bf16[1,3,64,256]{3,2,1,0:T(8,128)(2,1)}, bf16[1,3,64,256]{3,2,1,0:T(8,128)(2,1)S(1)}, u32[]{:S(2)}, u32[]{:S(2)}) collective-permute-start(bf16[1,3,64,256]{3,2,1,0:T(8,128)(2,1)} %refs_0_.4), channel_id=1, source_target_pairs={{0,8},{4,12},{8,0},{12,4},{1,9},{5,13},{9,1},{13,5},{2,10},{6,14},... | collective-permute-start | bytes 294920 | tf_op jit(solution)/shard_map/ppermute | solution.py:319
  4.4 7.5 %collective-permute-start.1 = (f16[6,64,256]{2,1,0:T(8,128)(2,1)S(1)}, f16[6,64,256]{2,1,0:T(8,128)(2,1)S(1)}, u32[]{:S(2)}, u32[]{:S(2)}) collective-permute-start(f16[6,64,256]{2,1,0:T(8,128)(2,1)S(1)} %multiply_convert_fusion.1), channel_id=1, source_target_pairs={{0,4},{4,0},{8,12},{12,8},{1,5},{5,1},{9,13},{13,9},{2,6},{6,2},{1... | collective-permute-start | bytes 589832 | tf_op jit(solution)/shard_map/ppermute | solution.py:356
  4.7 7.2 %collective-permute-start.2 = (f16[6,64,256]{2,1,0:T(8,128)(2,1)S(1)}, f16[6,64,256]{2,1,0:T(8,128)(2,1)S(1)}, u32[]{:S(2)}, u32[]{:S(2)}) collective-permute-start(f16[6,64,256]{2,1,0:T(8,128)(2,1)S(1)} %multiply_convert_fusion), channel_id=1, source_target_pairs={{0,0},{4,8},{8,4},{12,12},{1,1},{5,9},{9,5},{13,13},{2,2},{6,10},{... | collective-permute-start | bytes 589832 | tf_op jit(solution)/shard_map/ppermute | solution.py:356
  6.8 5.2 %collective-permute-start.3 = (f32[6,8,256]{2,1,0:T(8,128)S(1)}, f32[6,8,256]{2,1,0:T(8,128)S(1)}, u32[]{:S(2)}, u32[]{:S(2)}) collective-permute-start(f32[6,8,256]{2,1,0:T(8,128)S(1)} %get-tuple-element.39), channel_id=1, source_target_pairs={{0,1},{1,0},{2,3},{3,2},{4,5},{5,4},{6,7},{7,6},{8,9},{9,8},{10,11... | collective-permute-start | bytes 147464 | tf_op jit(solution)/shard_map/ppermute | solution.py:360
  8.4 3.8 %collective-permute-start.4 = (f32[6,8,256]{2,1,0:T(8,128)S(1)}, f32[6,8,256]{2,1,0:T(8,128)S(1)}, u32[]{:S(2)}, u32[]{:S(2)}) collective-permute-start(f32[6,8,256]{2,1,0:T(8,128)S(1)} %get-tuple-element.40), channel_id=1, source_target_pairs={{0,3},{1,2},{2,1},{3,0},{4,7},{5,6},{6,5},{7,4},{8,11},{9,10},{10,... | collective-permute-start | bytes 147464 | tf_op jit(solution)/shard_map/ppermute | solution.py:360
  9.6 7.5 %collective-permute-start.5 = (bf16[2,3,64,256]{3,2,1,0:T(8,128)(2,1)S(1)}, bf16[2,3,64,256]{3,2,1,0:T(8,128)(2,1)S(1)}, u32[]{:S(2)}, u32[]{:S(2)}) collective-permute-start(bf16[2,3,64,256]{3,2,1,0:T(8,128)(2,1)S(1)} %pad_maximum_fusion), channel_id=1, source_target_pairs={{0,4},{4,0},{8,12},{12,8},{1,5},{5,1},{9,13},{13,9},{2,6},{6,2},{1... | collective-permute-start | bytes 589832 | tf_op jit(solution)/shard_map/ppermute | solution.py:319
  12.2 4.9 %copy-start.1 = (s32[4,32,2]{1,2,0:T(2,128)S(1)}, s32[4,32,2]{1,2,0:T(2,128)}, u32[]{:S(2)}) copy-start(s32[4,32,2]{1,2,0:T(2,128)} %param.9) | copy-start | bytes 3076
  12.2 4.9 %copy-start.2 = (s32[3]{0:T(128)S(1)}, s32[3]{0:T(128)}, u32[]{:S(2)}) copy-start(s32[3]{0:T(128)} %refs_0_.7) | copy-start | bytes 40
  12.5 10.3 %collective-permute-start.6 = (f16[3,64,256]{2,1,0:T(8,128)(2,1)S(1)}, f16[3,64,256]{2,1,0:T(8,128)(2,1)S(1)}, u32[]{:S(2)}, u32[]{:S(2)}) collective-permute-start(f16[3,64,256]{2,1,0:T(8,128)(2,1)S(1)} %multiply_convert_fusion.5), channel_id=1, source_target_pairs={{0,4},{4,0},{8,12},{12,8},{1,5},{5,1},{9,13},{13,9},{2,6},{6,2},{1... | collective-permute-start | bytes 294920 | tf_op jit(solution)/shard_map/ppermute | solution.py:356
  13.9 8.9 %collective-permute-start.9 = (f16[3,64,256]{2,1,0:T(8,128)(2,1)S(1)}, f16[3,64,256]{2,1,0:T(8,128)(2,1)S(1)}, u32[]{:S(2)}, u32[]{:S(2)}) collective-permute-start(f16[3,64,256]{2,1,0:T(8,128)(2,1)S(1)} %multiply_convert_fusion.4), channel_id=1, source_target_pairs={{0,0},{4,8},{8,4},{12,12},{1,1},{5,9},{9,5},{13,13},{2,2},{6,10},{... | collective-permute-start | bytes 294920 | tf_op jit(solution)/shard_map/ppermute | solution.py:356
  18.2 4.0 %collective-permute-start.7 = (f32[3,8,256]{2,1,0:T(8,128)S(1)}, f32[3,8,256]{2,1,0:T(8,128)S(1)}, u32[]{:S(2)}, u32[]{:S(2)}) collective-permute-start(f32[3,8,256]{2,1,0:T(8,128)S(1)} %get-tuple-element.47), channel_id=1, source_target_pairs={{0,1},{1,0},{2,3},{3,2},{4,5},{5,4},{6,7},{7,6},{8,9},{9,8},{10,11... | collective-permute-start | bytes 73736 | tf_op jit(solution)/shard_map/ppermute | solution.py:360
  19.5 3.3 %collective-permute-start.8 = (f32[3,8,256]{2,1,0:T(8,128)S(1)}, f32[3,8,256]{2,1,0:T(8,128)S(1)}, u32[]{:S(2)}, u32[]{:S(2)}) collective-permute-start(f32[3,8,256]{2,1,0:T(8,128)S(1)} %get-tuple-element.48), channel_id=1, source_target_pairs={{0,3},{1,2},{2,1},{3,0},{4,7},{5,6},{6,5},{7,4},{8,11},{9,10},{10,... | collective-permute-start | bytes 73736 | tf_op jit(solution)/shard_map/ppermute | solution.py:360
  23.7 6.6 %collective-permute-start.10 = (f16[3,64,256]{2,1,0:T(8,128)(2,1)S(1)}, f16[3,64,256]{2,1,0:T(8,128)(2,1)S(1)}, u32[]{:S(2)}, u32[]{:S(2)}) collective-permute-start(f16[3,64,256]{2,1,0:T(8,128)(2,1)S(1)} %multiply_convert_fusion.3), channel_id=1, source_target_pairs={{0,4},{4,0},{8,12},{12,8},{1,5},{5,1},{9,13},{13,9},{2,6},{6,2},{1... | collective-permute-start | bytes 294920 | tf_op jit(solution)/shard_map/ppermute | solution.py:356
  23.8 6.5 %collective-permute-start.11 = (f16[3,64,256]{2,1,0:T(8,128)(2,1)S(1)}, f16[3,64,256]{2,1,0:T(8,128)(2,1)S(1)}, u32[]{:S(2)}, u32[]{:S(2)}) collective-permute-start(f16[3,64,256]{2,1,0:T(8,128)(2,1)S(1)} %multiply_convert_fusion.2), channel_id=1, source_target_pairs={{0,0},{4,8},{8,4},{12,12},{1,1},{5,9},{9,5},{13,13},{2,2},{6,10},{... | collective-permute-start | bytes 294920 | tf_op jit(solution)/shard_map/ppermute | solution.py:356
  26.4 3.9 %collective-permute-start.12 = (f32[3,8,256]{2,1,0:T(8,128)S(1)}, f32[3,8,256]{2,1,0:T(8,128)S(1)}, u32[]{:S(2)}, u32[]{:S(2)}) collective-permute-start(f32[3,8,256]{2,1,0:T(8,128)S(1)} %get-tuple-element.56), channel_id=1, source_target_pairs={{0,1},{1,0},{2,3},{3,2},{4,5},{5,4},{6,7},{7,6},{8,9},{9,8},{10,11... | collective-permute-start | bytes 73736 | tf_op jit(solution)/shard_map/ppermute | solution.py:360
  27.5 3.3 %collective-permute-start.13 = (f32[3,8,256]{2,1,0:T(8,128)S(1)}, f32[3,8,256]{2,1,0:T(8,128)S(1)}, u32[]{:S(2)}, u32[]{:S(2)}) collective-permute-start(f32[3,8,256]{2,1,0:T(8,128)S(1)} %get-tuple-element.57), channel_id=1, source_target_pairs={{0,3},{1,2},{2,1},{3,0},{4,7},{5,6},{6,5},{7,4},{8,11},{9,10},{10,... | collective-permute-start | bytes 73736 | tf_op jit(solution)/shard_map/ppermute | solution.py:360

commit v5 on v4

--- a/solution.py
+++ b/solution.py
@@ -97,8 +97,14 @@
 
 
 def gather_kernel(slots, slot, order, position, azimuth, incidence, field, *refs):
-    *parts, table, out, py1, py2 = refs
+    *parts, table, out, py1, py2, words = refs
     pos = position()
+    planes, blocks = out.shape[1], table.shape[0] - 1
+    start = 0
+    for step, those in ((1, range(planes)), (2, range(planes)), (0, (-1, planes))):
+        entries = [slot(pos, azimuth, incidence, step, x, k) for x in those for k in range(slots)]
+        put_slots(words, start, entries, blocks)
+        start += words_for(len(entries), blocks)
     per = sum(part.shape[0] for part in parts) // len(order)
     places = [p * per + b for p in order for b in range(per)]
     for part in parts:
@@ -125,6 +131,35 @@
     owner = block // per if per > 1 else block
     slot = (owner ^ pos[3]) * per + block % per if per > 1 else owner ^ pos[3]
     return jnp.where((block >= 0) & (block < blocks), slot, blocks)
+
+
+def code_of(blocks):
+    bits = blocks.bit_length()
+    return bits, 24 // bits
+
+
+def words_for(entries, blocks):
+    return -(-entries // code_of(blocks)[1])
+
+
+def put_slots(ref, start, entries, blocks):
+    bits, per = code_of(blocks)
+    for i in range(0, len(entries), per):
+        word = sum(entry << (bits * j) for j, entry in enumerate(entries[i : i + per]))
+        ref[start + i // per] = jnp.full(ref.shape[1:], word.astype(f32))
+
+
+def slot_reader(ref, start, entries, blocks):
+    bits, per = code_of(blocks)
+    words = [jnp.max(ref[start + i]).astype(jnp.int32) for i in range(words_for(entries, blocks))]
+
+    def read(entry):
+        word = words[0]
+        for i, other in enumerate(words[1:], 1):
+            word = jnp.where(entry // per == i, other, word)
+        return (word >> (entry % per * bits)) & (2**bits - 1)
+
+    return read
 
 
 def shifted(parts, lane, up):
@@ -137,10 +172,9 @@
     return out
 
 
-def local_kernel(step, slots, slot, position, *refs):
+def local_kernel(step, slots, *refs):
     if step:
-        azimuth, incidence, w, v, table, grad, out = refs
-        pos = position()
+        w, v, table, words, grad, out = refs
     else:
         w, v, out, grad = refs
     planes, rows, depth = w.shape[1:]
@@ -149,13 +183,16 @@
     lane = lax.broadcasted_iota(jnp.int32, (ROWS, LANES), 1)
     sub = lax.broadcasted_iota(jnp.int32, (ROWS, LANES), 0)
     comps = range(3)
+    if step:
+        entries, blocks = planes * slots, table.shape[0] - 1
+        read = slot_reader(words, (step - 1) * words_for(entries, blocks), entries, blocks)
 
     def plane_body(x, _):
         before = jnp.maximum(x - 1, 0)
         after = jnp.minimum(x + 1, planes - 1)
         low = jnp.where(x > 0, slope, 0.0)
         high = jnp.where(x < planes - 1, slope, 0.0)
-        deposits = [slot(pos, azimuth, incidence, step, x, k) for k in range(slots)] if step else []
+        deposits = [read(x * slots + k) for k in range(slots)] if step else []
 
         def place(j, s):
             return slice(j * ROWS, (j + 1) * ROWS), slice(s * LANES, (s + 1) * LANES)
@@ -215,14 +252,12 @@
     lax.fori_loop(0, planes, plane_body, 0)
 
 
-def fix_kernel(step, slots, slot, position, final, *refs):
-    if step == 1:
-        azimuth, incidence, *refs = refs
+def fix_kernel(step, slots, position, final, *refs):
     pos = position()
     new, *refs = refs
     if step:
         if step == 1:
-            table, *refs = refs
+            table, words, *refs = refs
         v, x1, x2, y1, y2, out, *sends = refs
     else:
         grad, w, v, x1, x2, y1, y2, out, full, *sends = refs
@@ -230,6 +265,9 @@
     last = planes - 1
     inner = pl.ds(1, planes - 2)
     copies = []
+    if step == 1:
+        blocks = table.shape[0] - 1
+        read = slot_reader(words, 2 * words_for(planes * slots, blocks), 2 * slots, blocks)
 
     def write(source, target):
         copies.append(pltpu.make_async_copy(source, target, sems.at[len(copies)]))
@@ -266,8 +304,7 @@
         there = jnp.where(pos[4 + which] > 0, slope, 0.0)
         sign = jnp.where(plane > 0, -there, there)
         if step == 1:
-            beyond = jnp.where(plane > 0, planes, -1)
-            blocks = [slot(pos, azimuth, incidence, 0, beyond, k) for k in range(slots)]
+            beyond = [read(jnp.where(plane > 0, slots + k, k)) for k in range(slots)]
             coef = there + sign * v[0, plane]
         else:
             coef = (there * unscale) + (sign * unscale) * v[0, plane]
@@ -275,7 +312,7 @@
             value = halo[c]
             if step == 1:
                 value = value * unscale
-                for block in blocks:
+                for block in beyond:
                     value += table[block, c]
             total = out[c, plane] + coef * value
             if not step:
@@ -377,14 +414,15 @@
     side = swap_rows(sends[2:])
     field = vorticity
     small = (azimuth, incidence)
+    n_words = 2 * words_for(planes * slots, blocks) + words_for(2 * slots, blocks)
     grads = shape(9, planes, rows, depth)
     send_x, send_y = [shape(3, rows, depth)] * 2, [shape(3, planes, depth)] * 2
     for step in range(steps):
         final = step == steps - 1
-        local = functools.partial(local_kernel, step, slots, where, position)
-        fix = functools.partial(fix_kernel, step, slots, where, position, final)
+        local = functools.partial(local_kernel, step, slots)
+        fix = functools.partial(fix_kernel, step, slots, position, final)
         if step:
-            (new,) = call(local, [whole], *small, field, velocity, table, grad, smem=2, cost=work)
+            (new,) = call(local, [whole], field, velocity, table, words, grad, cost=work)
             first = step == 1
             if first:
                 one, *side = lax.optimization_barrier((jnp.ones((1, 1, depth), f32), *side))
@@ -394,14 +432,12 @@
             result = call(
                 fix,
                 [whole, whole] if final else [whole] + send_x + send_y,
-                *(small if first else ()),
                 new,
-                *([table] if first else []),
+                *([table, words] if first else []),
                 velocity,
                 *halo,
                 *side,
-                smem=2 if first else 0,
-                aliases={2 if first else 0: 0},
+                aliases={0: 0},
                 cost=work // 10,
                 hbm_out=final,
                 scratch=[pltpu.SemaphoreType.DMA((11,))] if final else (),
@@ -417,9 +453,9 @@
             args = (new, grad, field, velocity, *[a.astype(f32) for a in halo], *side)
             new, grad, *ready = call(fix, [whole, grads] + send_x, *args, aliases={0: 0, 1: 1}, cost=work // 10)
             halo = swap_planes(ready, field_scales[1])
-            table, field, *ready = call(
+            table, field, *ready, words = call(
                 functools.partial(gather_kernel, slots, where, order, position),
-                [shape(blocks + 1, 3, rows, depth), whole] + send_y,
+                [shape(blocks + 1, 3, rows, depth), whole] + send_y + [shape(n_words, ROWS, LANES)],
                 *small,
                 new,
                 *parts,

time: 32.1 us -> 31.5 us (0.981)
  the two profiles are of different devices: /device:TPU:9 before, /device:TPU:1 now
where the time goes in v5:
time: 31.5 us; the launch traced here: 31.1 us
  starting transfers between devices  17.3 us (55%)
  Pallas kernels  10.8 us (34%)
  waiting for transfers between devices  2.39 us (8%)
    pallas_call x7, Pallas kernels, call(): pl.pallas_call(kernel, out_shape=shapes, in_specs=specs, out_specs=out_sp...  8.76 us
    ppermute x6, starting transfers between devices, swap_planes(): lax.ppermute((pair[i] * scale).astype(f16), 'xz', x_pairs[i])  6.16 us
    ppermute x6, starting transfers between devices, swap_rows(): return [lax.ppermute(a, 'gy', y_pairs[i]) for i, a in enumerate(pair)]  6.07 us
    ppermute x2, starting transfers between devices, gather_blocks(): lax.ppermute(payload, 'xz', [(i, i ^ stage) for i in range(count)])  5.06 us
    pallas_call x1, Pallas kernels, per_device(): pl.pallas_call(functools.partial(load_kernel, position), out_shape=[pltpu...  2.05 us
    ppermute x2, waiting for transfers between devices, gather_blocks(): lax.ppermute(payload, 'xz', [(i, i ^ stage) for i in range(count)])  1.44 us
    ppermute x6, waiting for transfers between devices, swap_rows(): return [lax.ppermute(a, 'gy', y_pairs[i]) for i, a in enumerate(pair)]  0.93 us
  transfers between devices with their start and end apart: 14, of which 2 were waited for; matrix products, arithmetic and copies ran while one was open for 1% of the time, Pallas kernels for 30%

profile of v5, /device:TPU:1, one launch (start us, length us, event | category | flops | bytes accessed | tf_op | source)
XLA Modules:
  0.0 31.1 jit_solution(2473001280843874810)
XLA Ops:
  0.0 0.0 copy-start
  0.0 3.1 %collective-permute-start = (bf16[1,3,64,256]{3,2,1,0:T(8,128)(2,1)}, bf16[1,3,64,256]{3,2,1,0:T(8,128)(2,1)S(1)}, u32[]{:S(2)}, u32[]{:S(2)}) collective-permute-start(bf16[1,3,64,256]{3,2,1,0:T(8,128)(2,1)} %refs_0_.1), channel_id=1, source_target_pairs={{0,8},{4,12},{8,0},{12,4},{1,9},{5,13},{9,1},{13,5},{2,10},{6,14},... | collective-permute-start | bytes 294920 | tf_op jit(solution)/shard_map/ppermute | solution.py:356
  3.1 2.1 %shard_map.64 = (f32[3,8,64,256]{3,2,1,0:T(8,128)S(1)}, f32[3,8,64,256]{3,2,1,0:T(8,128)S(1)}, f32[6,64,256]{2,1,0:T(8,128)S(1)}, f32[6,64,256]{2,1,0:T(8,128)S(...) custom-call(f32[3,8,64,256]{3,2,1,0:T(8,128)} %w_in.1, f32[3,8,64,256]{3,2,1,0:T(8,128)} %v_in.1), custom_call_target="tpu_custom_call" | custom-call | tf_op jit(solution)/shard_map/pallas_call | solution.py:402
  5.2 1.4 %collective-permute-start.1 = (f16[6,64,256]{2,1,0:T(8,128)(2,1)S(1)}, f16[6,64,256]{2,1,0:T(8,128)(2,1)S(1)}, u32[]{:S(2)}, u32[]{:S(2)}) collective-permute-start(f16[6,64,256]{2,1,0:T(8,128)(2,1)S(1)} %multiply_convert_fusion.1), channel_id=1, source_target_pairs={{0,4},{4,0},{8,12},{12,8},{1,5},{5,1},{9,13},{13,9},{2,6},{6,2},{1... | collective-permute-start | bytes 589832 | tf_op jit(solution)/shard_map/ppermute | solution.py:393
  6.6 0.7 %collective-permute-start.2 = (f16[6,64,256]{2,1,0:T(8,128)(2,1)S(1)}, f16[6,64,256]{2,1,0:T(8,128)(2,1)S(1)}, u32[]{:S(2)}, u32[]{:S(2)}) collective-permute-start(f16[6,64,256]{2,1,0:T(8,128)(2,1)S(1)} %multiply_convert_fusion), channel_id=1, source_target_pairs={{0,0},{4,8},{8,4},{12,12},{1,1},{5,9},{9,5},{13,13},{2,2},{6,10},{... | collective-permute-start | bytes 589832 | tf_op jit(solution)/shard_map/ppermute | solution.py:393
  7.3 1.3 %collective-permute-start.3 = (f32[6,8,256]{2,1,0:T(8,128)S(1)}, f32[6,8,256]{2,1,0:T(8,128)S(1)}, u32[]{:S(2)}, u32[]{:S(2)}) collective-permute-start(f32[6,8,256]{2,1,0:T(8,128)S(1)} %get-tuple-element.40), channel_id=1, source_target_pairs={{0,1},{1,0},{2,3},{3,2},{4,5},{5,4},{6,7},{7,6},{8,9},{9,8},{10,11... | collective-permute-start | bytes 147464 | tf_op jit(solution)/shard_map/ppermute | solution.py:397
  8.6 1.2 %collective-permute-start.4 = (f32[6,8,256]{2,1,0:T(8,128)S(1)}, f32[6,8,256]{2,1,0:T(8,128)S(1)}, u32[]{:S(2)}, u32[]{:S(2)}) collective-permute-start(f32[6,8,256]{2,1,0:T(8,128)S(1)} %get-tuple-element.41), channel_id=1, source_target_pairs={{0,3},{1,2},{2,1},{3,0},{4,7},{5,6},{6,5},{7,4},{8,11},{9,10},{10,... | collective-permute-start | bytes 147464 | tf_op jit(solution)/shard_map/ppermute | solution.py:397
  9.8 0.0 collective-permute-done.refs_1_
  9.8 0.0 copy-done
  9.8 1.9 %collective-permute-start.5 = (bf16[2,3,64,256]{3,2,1,0:T(8,128)(2,1)S(1)}, bf16[2,3,64,256]{3,2,1,0:T(8,128)(2,1)S(1)}, u32[]{:S(2)}, u32[]{:S(2)}) collective-permute-start(bf16[2,3,64,256]{3,2,1,0:T(8,128)(2,1)S(1)} %pad_maximum_fusion), channel_id=1, source_target_pairs={{0,4},{4,0},{8,12},{12,8},{1,5},{5,1},{9,13},{13,9},{2,6},{6,2},{1... | collective-permute-start | bytes 589832 | tf_op jit(solution)/shard_map/ppermute | solution.py:356
  11.8 2.2 %shard_map.65 = (f32[3,8,64,256]{3,2,1,0:T(8,128)S(1)}, f32[9,8,64,256]{3,2,1,0:T(8,128)S(1)}) custom-call(f32[3,8,64,256]{3,2,1,0:T(8,128)S(1)} %get-tuple-element.34.refs_0_.refs_2_, f32[3,8,64,256]{3,2,1,0:T(8,128)S(1)} %get-tuple-element.35.refs_1_.refs_3_), custom_call_target="tpu_custom_call" | custom-call | flops 15728640 | bytes 3932160 | tf_op jit(solution)/shard_map/pallas_call | solution.py:43
  14.0 0.0 collective-permute-done.1
  14.0 0.0 collective-permute-done.2
  14.1 0.0 collective-permute-done.3.refs_6_
  14.1 0.0 collective-permute-done.4.refs_7_
  14.1 0.0 copy-start.1
  14.1 0.0 copy-start.2
  14.1 0.3 shard_map.66
  14.5 0.2 collective-permute-start.6
  14.7 0.7 %collective-permute-start.9 = (f16[3,64,256]{2,1,0:T(8,128)(2,1)S(1)}, f16[3,64,256]{2,1,0:T(8,128)(2,1)S(1)}, u32[]{:S(2)}, u32[]{:S(2)}) collective-permute-start(f16[3,64,256]{2,1,0:T(8,128)(2,1)S(1)} %multiply_convert_fusion.4), channel_id=1, source_target_pairs={{0,0},{4,8},{8,4},{12,12},{1,1},{5,9},{9,5},{13,13},{2,2},{6,10},{... | collective-permute-start | bytes 294920 | tf_op jit(solution)/shard_map/ppermute | solution.py:393
  15.4 1.4 %collective-permute-done.5.refs_2_ = bf16[2,3,64,256]{3,2,1,0:T(8,128)(2,1)S(1)} collective-permute-done((bf16[2,3,64,256]{3,2,1,0:T(8,128)(2,1)S(1)}, bf16[2,3,64,256]{3,2,1,0:T(8,128)(2,1)S(1)}, u32[]{:S(2)}, u32[]{:S(2)}) %collective-permute-start.5) | collective-permute-done | bytes 196640 | tf_op jit(solution)/shard_map/ppermute | solution.py:356
  16.8 0.0 copy-done.1
  16.8 0.0 copy-done.2
  16.8 1.2 %shard_map.67 = (f32[5,3,64,256]{3,2,1,0:T(8,128)S(1)}, f32[3,8,64,256]{3,2,1,0:T(8,128)S(1)}, f32[3,8,256]{2,1,0:T(8,128)S(1)}, f32[3,8,256]{2,1,0:T(8,128)S(1)}, f32[5,8,128]{2,1,0:T(8,128)S(1)}) custom-call(s32[3]{0:T(128)S(1)} %copy-done.2, s32[4,2,32]{2,1,0:T(2,128)S(1)} %bitcast.2, ...), custom_call_target="tpu_custom_call", output_to_operand_aliasing={{1}: (2, {})} | custom-call | flops 1572864 | bytes 393216 | tf_op jit(solution)/shard_map/pallas_call | solution.py:43
  18.0 1.0 %collective-permute-start.7 = (f32[3,8,256]{2,1,0:T(8,128)S(1)}, f32[3,8,256]{2,1,0:T(8,128)S(1)}, u32[]{:S(2)}, u32[]{:S(2)}) collective-permute-start(f32[3,8,256]{2,1,0:T(8,128)S(1)} %get-tuple-element.49), channel_id=1, source_target_pairs={{0,1},{1,0},{2,3},{3,2},{4,5},{5,4},{6,7},{7,6},{8,9},{9,8},{10,11... | collective-permute-start | bytes 73736 | tf_op jit(solution)/shard_map/ppermute | solution.py:397
  19.0 1.7 %collective-permute-start.8 = (f32[3,8,256]{2,1,0:T(8,128)S(1)}, f32[3,8,256]{2,1,0:T(8,128)S(1)}, u32[]{:S(2)}, u32[]{:S(2)}) collective-permute-start(f32[3,8,256]{2,1,0:T(8,128)S(1)} %get-tuple-element.50), channel_id=1, source_target_pairs={{0,3},{1,2},{2,1},{3,0},{4,7},{5,6},{6,5},{7,4},{8,11},{9,10},{10,... | collective-permute-start | bytes 73736 | tf_op jit(solution)/shard_map/ppermute | solution.py:397
  20.7 1.8 %shard_map.68.refs_0_ = f32[3,8,64,256]{3,2,1,0:T(8,128)S(1)} custom-call(f32[3,8,64,256]{3,2,1,0:T(8,128)S(1)} %get-tuple-element.44.refs_0_, f32[3,8,64,256]{3,2,1,0:T(8,128)S(1)} %get-tuple-element.35.refs_1_.refs_3_, f32[5,3,64,256]{3,2,1,0:T(8,128)S(1)} %get-tuple-element.45.refs_2_.refs_1_, f32[5,8,128]{2,1,0:T(8,128)S(1)} %get-tuple-element.46.refs_3_.refs_2_, ...), custom_call_target="tpu_custom_call" | custom-call | flops 15728640 | bytes 3932160 | tf_op jit(solution)/shard_map/pallas_call | solution.py:43
  22.5 0.0 collective-permute-done.7.refs_6_
  22.5 0.0 collective-permute-done.8.refs_7_
  22.5 0.0 collective-permute-done.6
  22.6 0.0 collective-permute-done.9
  22.6 0.3 shard_map.69
  22.9 2.6 %collective-permute-start.10 = (f16[3,64,256]{2,1,0:T(8,128)(2,1)S(1)}, f16[3,64,256]{2,1,0:T(8,128)(2,1)S(1)}, u32[]{:S(2)}, u32[]{:S(2)}) collective-permute-start(f16[3,64,256]{2,1,0:T(8,128)(2,1)S(1)} %multiply_convert_fusion.3), channel_id=1, source_target_pairs={{0,4},{4,0},{8,12},{12,8},{1,5},{5,1},{9,13},{13,9},{2,6},{6,2},{1... | collective-permute-start | bytes 294920 | tf_op jit(solution)/shard_map/ppermute | solution.py:393
  25.5 0.7 %collective-permute-start.11 = (f16[3,64,256]{2,1,0:T(8,128)(2,1)S(1)}, f16[3,64,256]{2,1,0:T(8,128)(2,1)S(1)}, u32[]{:S(2)}, u32[]{:S(2)}) collective-permute-start(f16[3,64,256]{2,1,0:T(8,128)(2,1)S(1)} %multiply_convert_fusion.2), channel_id=1, source_target_pairs={{0,0},{4,8},{8,4},{12,12},{1,1},{5,9},{9,5},{13,13},{2,2},{6,10},{... | collective-permute-start | bytes 294920 | tf_op jit(solution)/shard_map/ppermute | solution.py:393
  26.2 0.4 %collective-permute-start.12 = (f32[3,8,256]{2,1,0:T(8,128)S(1)}, f32[3,8,256]{2,1,0:T(8,128)S(1)}, u32[]{:S(2)}, u32[]{:S(2)}) collective-permute-start(f32[3,8,256]{2,1,0:T(8,128)S(1)} %get-tuple-element.58), channel_id=1, source_target_pairs={{0,1},{1,0},{2,3},{3,2},{4,5},{5,4},{6,7},{7,6},{8,9},{9,8},{10,11... | collective-permute-start | bytes 73736 | tf_op jit(solution)/shard_map/ppermute | solution.py:397
  26.6 0.5 %collective-permute-start.13 = (f32[3,8,256]{2,1,0:T(8,128)S(1)}, f32[3,8,256]{2,1,0:T(8,128)S(1)}, u32[]{:S(2)}, u32[]{:S(2)}) collective-permute-start(f32[3,8,256]{2,1,0:T(8,128)S(1)} %get-tuple-element.59), channel_id=1, source_target_pairs={{0,3},{1,2},{2,1},{3,0},{4,7},{5,6},{6,5},{7,4},{8,11},{9,10},{10,... | collective-permute-start | bytes 73736 | tf_op jit(solution)/shard_map/ppermute | solution.py:397
  27.0 1.8 %shard_map.70.refs_0_ = f32[3,8,64,256]{3,2,1,0:T(8,128)S(1)} custom-call(f32[3,8,64,256]{3,2,1,0:T(8,128)S(1)} %get-tuple-element.55.refs_0_, f32[3,8,64,256]{3,2,1,0:T(8,128)S(1)} %get-tuple-element.35.refs_1_.refs_3_, f32[5,3,64,256]{3,2,1,0:T(8,128)S(1)} %get-tuple-element.45.refs_2_.refs_1_, f32[5,8,128]{2,1,0:T(8,128)S(1)} %get-tuple-element.46.refs_3_.refs_2_, ...), custom_call_target="tpu_custom_call" | custom-call | flops 15728640 | bytes 3932160 | tf_op jit(solution)/shard_map/pallas_call | solution.py:43
  28.8 0.0 collective-permute-done.10
  28.9 0.0 collective-permute-done.11
  28.9 0.0 collective-permute-done.12.refs_4_
  28.9 0.9 %collective-permute-done.13.refs_5_ = f32[3,8,256]{2,1,0:T(8,128)S(1)} collective-permute-done((f32[3,8,256]{2,1,0:T(8,128)S(1)}, f32[3,8,256]{2,1,0:T(8,128)S(1)}, u32[]{:S(2)}, u32[]{:S(2)}) %collective-permute-start.13) | collective-permute-done | bytes 24608 | tf_op jit(solution)/shard_map/ppermute | solution.py:397
  29.8 1.2 %shard_map.71 = (f32[3,8,64,256]{3,2,1,0:T(8,128)S(1)}, f32[3,8,64,256]{3,2,1,0:T(8,128)}) custom-call(f32[3,8,64,256]{3,2,1,0:T(8,128)S(1)} %shard_map.70.refs_0_, f32[3,8,64,256]{3,2,1,0:T(8,128)S(1)} %get-tuple-element.35.refs_1_.refs_3_, f32[3,64,256]{2,1,0:T(8,128)S(1)} %convert_element_type.45.refs_2_, ...), custom_call_target="tpu_custom_call", output_to_operand_aliasing={{0}: (0, {})} | custom-call | flops 1572864 | bytes 393216 | tf_op jit(solution)/shard_map/pallas_call | solution.py:43
  (13 shorter events, 0.3 us)
Async XLA Ops:
  0.0 9.8 %copy-start = (bf16[1,3,64,256]{3,2,1,0:T(8,128)(2,1)S(1)}, bf16[1,3,64,256]{3,2,1,0:T(8,128)(2,1)}, u32[]{:S(2)}) copy-start(bf16[1,3,64,256]{3,2,1,0:T(8,128)(2,1)} %refs_0_.1) | copy-start | bytes 294916
  0.0 9.8 %collective-permute-start = (bf16[1,3,64,256]{3,2,1,0:T(8,128)(2,1)}, bf16[1,3,64,256]{3,2,1,0:T(8,128)(2,1)S(1)}, u32[]{:S(2)}, u32[]{:S(2)}) collective-permute-start(bf16[1,3,64,256]{3,2,1,0:T(8,128)(2,1)} %refs_0_.1), channel_id=1, source_target_pairs={{0,8},{4,12},{8,0},{12,4},{1,9},{5,13},{9,1},{13,5},{2,10},{6,14},... | collective-permute-start | bytes 294920 | tf_op jit(solution)/shard_map/ppermute | solution.py:356
  5.2 8.8 %collective-permute-start.1 = (f16[6,64,256]{2,1,0:T(8,128)(2,1)S(1)}, f16[6,64,256]{2,1,0:T(8,128)(2,1)S(1)}, u32[]{:S(2)}, u32[]{:S(2)}) collective-permute-start(f16[6,64,256]{2,1,0:T(8,128)(2,1)S(1)} %multiply_convert_fusion.1), channel_id=1, source_target_pairs={{0,4},{4,0},{8,12},{12,8},{1,5},{5,1},{9,13},{13,9},{2,6},{6,2},{1... | collective-permute-start | bytes 589832 | tf_op jit(solution)/shard_map/ppermute | solution.py:393
  6.6 7.4 %collective-permute-start.2 = (f16[6,64,256]{2,1,0:T(8,128)(2,1)S(1)}, f16[6,64,256]{2,1,0:T(8,128)(2,1)S(1)}, u32[]{:S(2)}, u32[]{:S(2)}) collective-permute-start(f16[6,64,256]{2,1,0:T(8,128)(2,1)S(1)} %multiply_convert_fusion), channel_id=1, source_target_pairs={{0,0},{4,8},{8,4},{12,12},{1,1},{5,9},{9,5},{13,13},{2,2},{6,10},{... | collective-permute-start | bytes 589832 | tf_op jit(solution)/shard_map/ppermute | solution.py:393
  7.3 6.8 %collective-permute-start.3 = (f32[6,8,256]{2,1,0:T(8,128)S(1)}, f32[6,8,256]{2,1,0:T(8,128)S(1)}, u32[]{:S(2)}, u32[]{:S(2)}) collective-permute-start(f32[6,8,256]{2,1,0:T(8,128)S(1)} %get-tuple-element.40), channel_id=1, source_target_pairs={{0,1},{1,0},{2,3},{3,2},{4,5},{5,4},{6,7},{7,6},{8,9},{9,8},{10,11... | collective-permute-start | bytes 147464 | tf_op jit(solution)/shard_map/ppermute | solution.py:397
  8.6 5.5 %collective-permute-start.4 = (f32[6,8,256]{2,1,0:T(8,128)S(1)}, f32[6,8,256]{2,1,0:T(8,128)S(1)}, u32[]{:S(2)}, u32[]{:S(2)}) collective-permute-start(f32[6,8,256]{2,1,0:T(8,128)S(1)} %get-tuple-element.41), channel_id=1, source_target_pairs={{0,3},{1,2},{2,1},{3,0},{4,7},{5,6},{6,5},{7,4},{8,11},{9,10},{10,... | collective-permute-start | bytes 147464 | tf_op jit(solution)/shard_map/ppermute | solution.py:397
  9.8 7.0 %collective-permute-start.5 = (bf16[2,3,64,256]{3,2,1,0:T(8,128)(2,1)S(1)}, bf16[2,3,64,256]{3,2,1,0:T(8,128)(2,1)S(1)}, u32[]{:S(2)}, u32[]{:S(2)}) collective-permute-start(bf16[2,3,64,256]{3,2,1,0:T(8,128)(2,1)S(1)} %pad_maximum_fusion), channel_id=1, source_target_pairs={{0,4},{4,0},{8,12},{12,8},{1,5},{5,1},{9,13},{13,9},{2,6},{6,2},{1... | collective-permute-start | bytes 589832 | tf_op jit(solution)/shard_map/ppermute | solution.py:356
  14.1 2.7 %copy-start.1 = (s32[4,32,2]{1,2,0:T(2,128)S(1)}, s32[4,32,2]{1,2,0:T(2,128)}, u32[]{:S(2)}) copy-start(s32[4,32,2]{1,2,0:T(2,128)} %param.9) | copy-start | bytes 3076
  14.1 2.7 %copy-start.2 = (s32[3]{0:T(128)S(1)}, s32[3]{0:T(128)}, u32[]{:S(2)}) copy-start(s32[3]{0:T(128)} %azimuth.1) | copy-start | bytes 40
  14.5 8.1 %collective-permute-start.6 = (f16[3,64,256]{2,1,0:T(8,128)(2,1)S(1)}, f16[3,64,256]{2,1,0:T(8,128)(2,1)S(1)}, u32[]{:S(2)}, u32[]{:S(2)}) collective-permute-start(f16[3,64,256]{2,1,0:T(8,128)(2,1)S(1)} %multiply_convert_fusion.5), channel_id=1, source_target_pairs={{0,4},{4,0},{8,12},{12,8},{1,5},{5,1},{9,13},{13,9},{2,6},{6,2},{1... | collective-permute-start | bytes 294920 | tf_op jit(solution)/shard_map/ppermute | solution.py:393
  14.7 7.8 %collective-permute-start.9 = (f16[3,64,256]{2,1,0:T(8,128)(2,1)S(1)}, f16[3,64,256]{2,1,0:T(8,128)(2,1)S(1)}, u32[]{:S(2)}, u32[]{:S(2)}) collective-permute-start(f16[3,64,256]{2,1,0:T(8,128)(2,1)S(1)} %multiply_convert_fusion.4), channel_id=1, source_target_pairs={{0,0},{4,8},{8,4},{12,12},{1,1},{5,9},{9,5},{13,13},{2,2},{6,10},{... | collective-permute-start | bytes 294920 | tf_op jit(solution)/shard_map/ppermute | solution.py:393
  18.0 4.5 %collective-permute-start.7 = (f32[3,8,256]{2,1,0:T(8,128)S(1)}, f32[3,8,256]{2,1,0:T(8,128)S(1)}, u32[]{:S(2)}, u32[]{:S(2)}) collective-permute-start(f32[3,8,256]{2,1,0:T(8,128)S(1)} %get-tuple-element.49), channel_id=1, source_target_pairs={{0,1},{1,0},{2,3},{3,2},{4,5},{5,4},{6,7},{7,6},{8,9},{9,8},{10,11... | collective-permute-start | bytes 73736 | tf_op jit(solution)/shard_map/ppermute | solution.py:397
  19.0 3.5 %collective-permute-start.8 = (f32[3,8,256]{2,1,0:T(8,128)S(1)}, f32[3,8,256]{2,1,0:T(8,128)S(1)}, u32[]{:S(2)}, u32[]{:S(2)}) collective-permute-start(f32[3,8,256]{2,1,0:T(8,128)S(1)} %get-tuple-element.50), channel_id=1, source_target_pairs={{0,3},{1,2},{2,1},{3,0},{4,7},{5,6},{6,5},{7,4},{8,11},{9,10},{10,... | collective-permute-start | bytes 73736 | tf_op jit(solution)/shard_map/ppermute | solution.py:397
  22.9 5.9 %collective-permute-start.10 = (f16[3,64,256]{2,1,0:T(8,128)(2,1)S(1)}, f16[3,64,256]{2,1,0:T(8,128)(2,1)S(1)}, u32[]{:S(2)}, u32[]{:S(2)}) collective-permute-start(f16[3,64,256]{2,1,0:T(8,128)(2,1)S(1)} %multiply_convert_fusion.3), channel_id=1, source_target_pairs={{0,4},{4,0},{8,12},{12,8},{1,5},{5,1},{9,13},{13,9},{2,6},{6,2},{1... | collective-permute-start | bytes 294920 | tf_op jit(solution)/shard_map/ppermute | solution.py:393
  25.5 3.4 %collective-permute-start.11 = (f16[3,64,256]{2,1,0:T(8,128)(2,1)S(1)}, f16[3,64,256]{2,1,0:T(8,128)(2,1)S(1)}, u32[]{:S(2)}, u32[]{:S(2)}) collective-permute-start(f16[3,64,256]{2,1,0:T(8,128)(2,1)S(1)} %multiply_convert_fusion.2), channel_id=1, source_target_pairs={{0,0},{4,8},{8,4},{12,12},{1,1},{5,9},{9,5},{13,13},{2,2},{6,10},{... | collective-permute-start | bytes 294920 | tf_op jit(solution)/shard_map/ppermute | solution.py:393
  26.2 2.7 %collective-permute-start.12 = (f32[3,8,256]{2,1,0:T(8,128)S(1)}, f32[3,8,256]{2,1,0:T(8,128)S(1)}, u32[]{:S(2)}, u32[]{:S(2)}) collective-permute-start(f32[3,8,256]{2,1,0:T(8,128)S(1)} %get-tuple-element.58), channel_id=1, source_target_pairs={{0,1},{1,0},{2,3},{3,2},{4,5},{5,4},{6,7},{7,6},{8,9},{9,8},{10,11... | collective-permute-start | bytes 73736 | tf_op jit(solution)/shard_map/ppermute | solution.py:397
  26.6 3.3 %collective-permute-start.13 = (f32[3,8,256]{2,1,0:T(8,128)S(1)}, f32[3,8,256]{2,1,0:T(8,128)S(1)}, u32[]{:S(2)}, u32[]{:S(2)}) collective-permute-start(f32[3,8,256]{2,1,0:T(8,128)S(1)} %get-tuple-element.59), channel_id=1, source_target_pairs={{0,3},{1,2},{2,1},{3,0},{4,7},{5,6},{6,5},{7,4},{8,11},{9,10},{10,... | collective-permute-start | bytes 73736 | tf_op jit(solution)/shard_map/ppermute | solution.py:397

commit v6 on v5

--- a/solution.py
+++ b/solution.py
@@ -96,15 +96,22 @@
         pack_rows(pos, field, (y1, y2), 3 * i)
 
 
-def gather_kernel(slots, slot, order, position, azimuth, incidence, field, *refs):
-    *parts, table, out, py1, py2, words = refs
+def slots_kernel(slots, slot, planes, blocks, position, azimuth, incidence, *refs):
+    *refs, words = refs
     pos = position()
-    planes, blocks = out.shape[1], table.shape[0] - 1
     start = 0
-    for step, those in ((1, range(planes)), (2, range(planes)), (0, (-1, planes))):
+    for step, those in ((0, range(planes)), (1, range(planes)), (2, range(planes)), (0, (-1, planes))):
         entries = [slot(pos, azimuth, incidence, step, x, k) for x in those for k in range(slots)]
         put_slots(words, start, entries, blocks)
         start += words_for(len(entries), blocks)
+    local_kernel(0, slots, *refs)
+
+
+def gather_kernel(slots, order, position, field, words, *refs):
+    *parts, table, out, py1, py2 = refs
+    pos = position()
+    entries, blocks = out.shape[1] * slots, table.shape[0] - 1
+    read = slot_reader(words, 0, entries, blocks)
     per = sum(part.shape[0] for part in parts) // len(order)
     places = [p * per + b for p in order for b in range(per)]
     for part in parts:
@@ -113,7 +120,7 @@
     table[table.shape[0] - 1] = jnp.zeros(table.shape[1:], f32)
 
     def deposit(x, _):
-        where = [slot(pos, azimuth, incidence, 0, x, k) for k in range(slots)]
+        where = [read(x * slots + k) for k in range(slots)]
         for c in range(3):
             total = field[c, x]
             for block in where:
@@ -185,7 +192,7 @@
     comps = range(3)
     if step:
         entries, blocks = planes * slots, table.shape[0] - 1
-        read = slot_reader(words, (step - 1) * words_for(entries, blocks), entries, blocks)
+        read = slot_reader(words, step * words_for(entries, blocks), entries, blocks)
 
     def plane_body(x, _):
         before = jnp.maximum(x - 1, 0)
@@ -267,7 +274,7 @@
     copies = []
     if step == 1:
         blocks = table.shape[0] - 1
-        read = slot_reader(words, 2 * words_for(planes * slots, blocks), 2 * slots, blocks)
+        read = slot_reader(words, 3 * words_for(planes * slots, blocks), 2 * slots, blocks)
 
     def write(source, target):
         copies.append(pltpu.make_async_copy(source, target, sems.at[len(copies)]))
@@ -413,8 +420,7 @@
     halo = swap_planes(sends[:2], scale)
     side = swap_rows(sends[2:])
     field = vorticity
-    small = (azimuth, incidence)
-    n_words = 2 * words_for(planes * slots, blocks) + words_for(2 * slots, blocks)
+    n_words = 3 * words_for(planes * slots, blocks) + words_for(2 * slots, blocks)
     grads = shape(9, planes, rows, depth)
     send_x, send_y = [shape(3, rows, depth)] * 2, [shape(3, planes, depth)] * 2
     for step in range(steps):
@@ -449,18 +455,26 @@
             side = swap_rows(result[3:5])
         else:
             held, parts[1] = lax.optimization_barrier((field, parts[1]))
-            new, grad = call(local, [whole, grads], held, velocity, cost=work)
+            new, grad, words = call(
+                functools.partial(slots_kernel, slots, where, planes, blocks, position),
+                [whole, grads, shape(n_words, ROWS, LANES)],
+                azimuth,
+                incidence,
+                held,
+                velocity,
+                smem=2,
+                cost=work,
+            )
             args = (new, grad, field, velocity, *[a.astype(f32) for a in halo], *side)
             new, grad, *ready = call(fix, [whole, grads] + send_x, *args, aliases={0: 0, 1: 1}, cost=work // 10)
             halo = swap_planes(ready, field_scales[1])
-            table, field, *ready, words = call(
-                functools.partial(gather_kernel, slots, where, order, position),
-                [shape(blocks + 1, 3, rows, depth), whole] + send_y + [shape(n_words, ROWS, LANES)],
-                *small,
+            table, field, *ready = call(
+                functools.partial(gather_kernel, slots, order, position),
+                [shape(blocks + 1, 3, rows, depth), whole] + send_y,
                 new,
+                words,
                 *parts,
-                smem=2,
-                aliases={2: 1},
+                aliases={0: 1},
                 cost=work // 10,
             )
             side = swap_rows(ready)

time: 31.5 us -> 31.6 us (level)
  waiting for transfers between devices: 2.39 us -> 1.66 us
  starting transfers between devices: 17.3 us -> 17.9 us
  Pallas kernels: 10.8 us -> 11.2 us
    ppermute x6, starting transfers between devices: 6.16 us -> 7.25 us  [swap_planes(): lax.ppermute((pair[i] * scale).astype(f16), 'xz', x_pairs[i])]
    ppermute x2, waiting for transfers between devices: 1.44 us -> 0.65 us  [gather_blocks(): lax.ppermute(payload, 'xz', [(i, i ^ stage) for i in range(count)])]
    ppermute x6, starting transfers between devices: 6.07 us -> 5.57 us  [swap_rows(): return [lax.ppermute(a, 'gy', y_pairs[i]) for i, a in enumerate(pair)]]
    pallas_call x7, Pallas kernels: 8.76 us -> 9.14 us  [call(): pl.pallas_call(kernel, out_shape=shapes, in_specs=specs, out_specs=out_sp...]
  transfers between devices with their start and end apart: 14 -> 14, of which waited for: 2 -> 3; matrix products, arithmetic and copies ran while one was open for 1% -> 1% of each run, Pallas kernels for 30% -> 31%
where the time goes in v6:
time: 31.6 us; the launch traced here: 31.3 us
  starting transfers between devices  17.9 us (57%)
  Pallas kernels  11.2 us (35%)
  waiting for transfers between devices  1.66 us (5%)
    pallas_call x7, Pallas kernels, call(): pl.pallas_call(kernel, out_shape=shapes, in_specs=specs, out_specs=out_sp...  9.14 us
    ppermute x6, starting transfers between devices, swap_planes(): lax.ppermute((pair[i] * scale).astype(f16), 'xz', x_pairs[i])  7.25 us
    ppermute x6, starting transfers between devices, swap_rows(): return [lax.ppermute(a, 'gy', y_pairs[i]) for i, a in enumerate(pair)]  5.57 us
    ppermute x2, starting transfers between devices, gather_blocks(): lax.ppermute(payload, 'xz', [(i, i ^ stage) for i in range(count)])  5.06 us
    pallas_call x1, Pallas kernels, per_device(): pl.pallas_call(functools.partial(load_kernel, position), out_shape=[pltpu...  2.05 us
    ppermute x6, waiting for transfers between devices, swap_rows(): return [lax.ppermute(a, 'gy', y_pairs[i]) for i, a in enumerate(pair)]  0.99 us
    ppermute x2, waiting for transfers between devices, gather_blocks(): lax.ppermute(payload, 'xz', [(i, i ^ stage) for i in range(count)])  0.65 us
  transfers between devices with their start and end apart: 14, of which 3 were waited for; matrix products, arithmetic and copies ran while one was open for 1% of the time, Pallas kernels for 31%

profile of v6, /device:TPU:1, one launch (start us, length us, event | category | flops | bytes accessed | tf_op | source)
XLA Modules:
  0.0 31.3 jit_solution(8067295498457467483)
XLA Ops:
  0.0 0.0 copy-start
  0.0 3.1 %collective-permute-start = (bf16[1,3,64,256]{3,2,1,0:T(8,128)(2,1)}, bf16[1,3,64,256]{3,2,1,0:T(8,128)(2,1)S(1)}, u32[]{:S(2)}, u32[]{:S(2)}) collective-permute-start(bf16[1,3,64,256]{3,2,1,0:T(8,128)(2,1)} %refs_0_.1), channel_id=1, source_target_pairs={{0,8},{4,12},{8,0},{12,4},{1,9},{5,13},{9,1},{13,5},{2,10},{6,14},... | collective-permute-start | bytes 294920 | tf_op jit(solution)/shard_map/ppermute | solution.py:363
  3.1 2.1 %shard_map.64 = (f32[3,8,64,256]{3,2,1,0:T(8,128)S(1)}, f32[3,8,64,256]{3,2,1,0:T(8,128)S(1)}, f32[6,64,256]{2,1,0:T(8,128)S(1)}, f32[6,64,256]{2,1,0:T(8,128)S(...) custom-call(f32[3,8,64,256]{3,2,1,0:T(8,128)} %w_in.1, f32[3,8,64,256]{3,2,1,0:T(8,128)} %v_in.1), custom_call_target="tpu_custom_call" | custom-call | tf_op jit(solution)/shard_map/pallas_call | solution.py:409
  5.2 0.0 copy-start.1
  5.2 0.0 copy-start.2
  5.3 1.4 %collective-permute-start.1 = (f16[6,64,256]{2,1,0:T(8,128)(2,1)S(1)}, f16[6,64,256]{2,1,0:T(8,128)(2,1)S(1)}, u32[]{:S(2)}, u32[]{:S(2)}) collective-permute-start(f16[6,64,256]{2,1,0:T(8,128)(2,1)S(1)} %multiply_convert_fusion.1), channel_id=1, source_target_pairs={{0,4},{4,0},{8,12},{12,8},{1,5},{5,1},{9,13},{13,9},{2,6},{6,2},{1... | collective-permute-start | bytes 589832 | tf_op jit(solution)/shard_map/ppermute | solution.py:400
  6.7 0.7 %collective-permute-start.2 = (f16[6,64,256]{2,1,0:T(8,128)(2,1)S(1)}, f16[6,64,256]{2,1,0:T(8,128)(2,1)S(1)}, u32[]{:S(2)}, u32[]{:S(2)}) collective-permute-start(f16[6,64,256]{2,1,0:T(8,128)(2,1)S(1)} %multiply_convert_fusion), channel_id=1, source_target_pairs={{0,0},{4,8},{8,4},{12,12},{1,1},{5,9},{9,5},{13,13},{2,2},{6,10},{... | collective-permute-start | bytes 589832 | tf_op jit(solution)/shard_map/ppermute | solution.py:400
  7.4 1.3 %collective-permute-start.3 = (f32[6,8,256]{2,1,0:T(8,128)S(1)}, f32[6,8,256]{2,1,0:T(8,128)S(1)}, u32[]{:S(2)}, u32[]{:S(2)}) collective-permute-start(f32[6,8,256]{2,1,0:T(8,128)S(1)} %get-tuple-element.40), channel_id=1, source_target_pairs={{0,1},{1,0},{2,3},{3,2},{4,5},{5,4},{6,7},{7,6},{8,9},{9,8},{10,11... | collective-permute-start | bytes 147464 | tf_op jit(solution)/shard_map/ppermute | solution.py:404
  8.7 1.2 %collective-permute-start.4 = (f32[6,8,256]{2,1,0:T(8,128)S(1)}, f32[6,8,256]{2,1,0:T(8,128)S(1)}, u32[]{:S(2)}, u32[]{:S(2)}) collective-permute-start(f32[6,8,256]{2,1,0:T(8,128)S(1)} %get-tuple-element.41), channel_id=1, source_target_pairs={{0,3},{1,2},{2,1},{3,0},{4,7},{5,6},{6,5},{7,4},{8,11},{9,10},{10,... | collective-permute-start | bytes 147464 | tf_op jit(solution)/shard_map/ppermute | solution.py:404
  9.8 0.0 collective-permute-done.refs_1_
  9.8 0.0 copy-done
  9.9 1.9 %collective-permute-start.5 = (bf16[2,3,64,256]{3,2,1,0:T(8,128)(2,1)S(1)}, bf16[2,3,64,256]{3,2,1,0:T(8,128)(2,1)S(1)}, u32[]{:S(2)}, u32[]{:S(2)}) collective-permute-start(bf16[2,3,64,256]{3,2,1,0:T(8,128)(2,1)S(1)} %pad_maximum_fusion), channel_id=1, source_target_pairs={{0,4},{4,0},{8,12},{12,8},{1,5},{5,1},{9,13},{13,9},{2,6},{6,2},{1... | collective-permute-start | bytes 589832 | tf_op jit(solution)/shard_map/ppermute | solution.py:363
  11.8 0.0 copy-done.1
  11.8 0.0 copy-done.2
  11.8 3.1 %shard_map.65 = (f32[3,8,64,256]{3,2,1,0:T(8,128)S(1)}, f32[9,8,64,256]{3,2,1,0:T(8,128)S(1)}, f32[7,8,128]{2,1,0:T(8,128)S(1)}) custom-call(s32[3]{0:T(128)S(1)} %copy-done.2, s32[4,2,32]{2,1,0:T(2,128)S(1)} %bitcast.2, f32[3,8,64,256]{3,2,1,0:T(8,128)S(1)} %get-tuple-element.34.refs_0_.refs_2_, f32[3,8,64,256]{3,2,1,0:T(8,128)S(1)} %get-tuple-element.35.refs_1_.refs_3_), custom_call_target="tpu_custom_call" | custom-call | flops 15728640 | bytes 3932160 | tf_op jit(solution)/shard_map/pallas_call | solution.py:43
  14.9 0.0 collective-permute-done.1
  15.0 0.0 collective-permute-done.2
  15.0 0.0 collective-permute-done.3.refs_6_
  15.0 0.0 collective-permute-done.4.refs_7_
  15.0 0.3 shard_map.66
  15.4 0.1 collective-permute-start.6
  15.5 0.7 %collective-permute-start.9 = (f16[3,64,256]{2,1,0:T(8,128)(2,1)S(1)}, f16[3,64,256]{2,1,0:T(8,128)(2,1)S(1)}, u32[]{:S(2)}, u32[]{:S(2)}) collective-permute-start(f16[3,64,256]{2,1,0:T(8,128)(2,1)S(1)} %multiply_convert_fusion.4), channel_id=1, source_target_pairs={{0,0},{4,8},{8,4},{12,12},{1,1},{5,9},{9,5},{13,13},{2,2},{6,10},{... | collective-permute-start | bytes 294920 | tf_op jit(solution)/shard_map/ppermute | solution.py:400
  16.2 0.7 %collective-permute-done.5.refs_2_ = bf16[2,3,64,256]{3,2,1,0:T(8,128)(2,1)S(1)} collective-permute-done((bf16[2,3,64,256]{3,2,1,0:T(8,128)(2,1)S(1)}, bf16[2,3,64,256]{3,2,1,0:T(8,128)(2,1)S(1)}, u32[]{:S(2)}, u32[]{:S(2)}) %collective-permute-start.5) | collective-permute-done | bytes 196640 | tf_op jit(solution)/shard_map/ppermute | solution.py:363
  16.8 0.5 %shard_map.67 = (f32[5,3,64,256]{3,2,1,0:T(8,128)S(1)}, f32[3,8,64,256]{3,2,1,0:T(8,128)S(1)}, f32[3,8,256]{2,1,0:T(8,128)S(1)}, f32[3,8,256]{2,1,0:T(8,128)S(1)}) custom-call(f32[3,8,64,256]{3,2,1,0:T(8,128)S(1)} %get-tuple-element.42.field, f32[7,8,128]{2,1,0:T(8,128)S(1)} %get-tuple-element.43.words.refs_3_.refs_2_, ...), custom_call_target="tpu_custom_call", output_to_operand_aliasing={{1}: (0, {})} | custom-call | flops 1572864 | bytes 393216 | tf_op jit(solution)/shard_map/pallas_call | solution.py:43
  17.3 1.0 %collective-permute-start.7 = (f32[3,8,256]{2,1,0:T(8,128)S(1)}, f32[3,8,256]{2,1,0:T(8,128)S(1)}, u32[]{:S(2)}, u32[]{:S(2)}) collective-permute-start(f32[3,8,256]{2,1,0:T(8,128)S(1)} %get-tuple-element.49), channel_id=1, source_target_pairs={{0,1},{1,0},{2,3},{3,2},{4,5},{5,4},{6,7},{7,6},{8,9},{9,8},{10,11... | collective-permute-start | bytes 73736 | tf_op jit(solution)/shard_map/ppermute | solution.py:404
  18.3 1.2 %collective-permute-start.8 = (f32[3,8,256]{2,1,0:T(8,128)S(1)}, f32[3,8,256]{2,1,0:T(8,128)S(1)}, u32[]{:S(2)}, u32[]{:S(2)}) collective-permute-start(f32[3,8,256]{2,1,0:T(8,128)S(1)} %get-tuple-element.50), channel_id=1, source_target_pairs={{0,3},{1,2},{2,1},{3,0},{4,7},{5,6},{6,5},{7,4},{8,11},{9,10},{10,... | collective-permute-start | bytes 73736 | tf_op jit(solution)/shard_map/ppermute | solution.py:404
  19.5 1.9 %shard_map.68.refs_0_ = f32[3,8,64,256]{3,2,1,0:T(8,128)S(1)} custom-call(f32[3,8,64,256]{3,2,1,0:T(8,128)S(1)} %get-tuple-element.45.refs_0_, f32[3,8,64,256]{3,2,1,0:T(8,128)S(1)} %get-tuple-element.35.refs_1_.refs_3_, f32[5,3,64,256]{3,2,1,0:T(8,128)S(1)} %get-tuple-element.46.refs_2_.refs_1_, f32[7,8,128]{2,1,0:T(8,128)S(1)} %get-tuple-element.43.words.refs_3_.refs_2_, ...), custom_call_target="tpu_custom_call" | custom-call | flops 15728640 | bytes 3932160 | tf_op jit(solution)/shard_map/pallas_call | solution.py:43
  21.5 0.0 collective-permute-done.7.refs_6_
  21.5 0.1 collective-permute-done.8.refs_7_
  21.6 0.0 collective-permute-done.6
  21.6 0.0 collective-permute-done.9
  21.6 0.3 shard_map.69
  21.9 3.8 %collective-permute-start.10 = (f16[3,64,256]{2,1,0:T(8,128)(2,1)S(1)}, f16[3,64,256]{2,1,0:T(8,128)(2,1)S(1)}, u32[]{:S(2)}, u32[]{:S(2)}) collective-permute-start(f16[3,64,256]{2,1,0:T(8,128)(2,1)S(1)} %multiply_convert_fusion.3), channel_id=1, source_target_pairs={{0,4},{4,0},{8,12},{12,8},{1,5},{5,1},{9,13},{13,9},{2,6},{6,2},{1... | collective-permute-start | bytes 294920 | tf_op jit(solution)/shard_map/ppermute | solution.py:400
  25.7 0.7 %collective-permute-start.11 = (f16[3,64,256]{2,1,0:T(8,128)(2,1)S(1)}, f16[3,64,256]{2,1,0:T(8,128)(2,1)S(1)}, u32[]{:S(2)}, u32[]{:S(2)}) collective-permute-start(f16[3,64,256]{2,1,0:T(8,128)(2,1)S(1)} %multiply_convert_fusion.2), channel_id=1, source_target_pairs={{0,0},{4,8},{8,4},{12,12},{1,1},{5,9},{9,5},{13,13},{2,2},{6,10},{... | collective-permute-start | bytes 294920 | tf_op jit(solution)/shard_map/ppermute | solution.py:400
  26.4 0.4 %collective-permute-start.12 = (f32[3,8,256]{2,1,0:T(8,128)S(1)}, f32[3,8,256]{2,1,0:T(8,128)S(1)}, u32[]{:S(2)}, u32[]{:S(2)}) collective-permute-start(f32[3,8,256]{2,1,0:T(8,128)S(1)} %get-tuple-element.58), channel_id=1, source_target_pairs={{0,1},{1,0},{2,3},{3,2},{4,5},{5,4},{6,7},{7,6},{8,9},{9,8},{10,11... | collective-permute-start | bytes 73736 | tf_op jit(solution)/shard_map/ppermute | solution.py:404
  26.8 0.5 %collective-permute-start.13 = (f32[3,8,256]{2,1,0:T(8,128)S(1)}, f32[3,8,256]{2,1,0:T(8,128)S(1)}, u32[]{:S(2)}, u32[]{:S(2)}) collective-permute-start(f32[3,8,256]{2,1,0:T(8,128)S(1)} %get-tuple-element.59), channel_id=1, source_target_pairs={{0,3},{1,2},{2,1},{3,0},{4,7},{5,6},{6,5},{7,4},{8,11},{9,10},{10,... | collective-permute-start | bytes 73736 | tf_op jit(solution)/shard_map/ppermute | solution.py:404
  27.3 1.8 %shard_map.70.refs_0_ = f32[3,8,64,256]{3,2,1,0:T(8,128)S(1)} custom-call(f32[3,8,64,256]{3,2,1,0:T(8,128)S(1)} %get-tuple-element.55.refs_0_, f32[3,8,64,256]{3,2,1,0:T(8,128)S(1)} %get-tuple-element.35.refs_1_.refs_3_, f32[5,3,64,256]{3,2,1,0:T(8,128)S(1)} %get-tuple-element.46.refs_2_.refs_1_, f32[7,8,128]{2,1,0:T(8,128)S(1)} %get-tuple-element.43.words.refs_3_.refs_2_, ...), custom_call_target="tpu_custom_call" | custom-call | flops 15728640 | bytes 3932160 | tf_op jit(solution)/shard_map/pallas_call | solution.py:43
  29.1 0.0 collective-permute-done.10
  29.1 0.0 collective-permute-done.11
  29.1 0.0 collective-permute-done.12.refs_4_
  29.2 0.9 %collective-permute-done.13.refs_5_ = f32[3,8,256]{2,1,0:T(8,128)S(1)} collective-permute-done((f32[3,8,256]{2,1,0:T(8,128)S(1)}, f32[3,8,256]{2,1,0:T(8,128)S(1)}, u32[]{:S(2)}, u32[]{:S(2)}) %collective-permute-start.13) | collective-permute-done | bytes 24608 | tf_op jit(solution)/shard_map/ppermute | solution.py:404
  30.1 1.2 %shard_map.71 = (f32[3,8,64,256]{3,2,1,0:T(8,128)S(1)}, f32[3,8,64,256]{3,2,1,0:T(8,128)}) custom-call(f32[3,8,64,256]{3,2,1,0:T(8,128)S(1)} %shard_map.70.refs_0_, f32[3,8,64,256]{3,2,1,0:T(8,128)S(1)} %get-tuple-element.35.refs_1_.refs_3_, f32[3,64,256]{2,1,0:T(8,128)S(1)} %convert_element_type.45.refs_2_, ...), custom_call_target="tpu_custom_call", output_to_operand_aliasing={{0}: (0, {})} | custom-call | flops 1572864 | bytes 393216 | tf_op jit(solution)/shard_map/pallas_call | solution.py:43
  (13 shorter events, 0.3 us)
Async XLA Ops:
  0.0 9.8 %copy-start = (bf16[1,3,64,256]{3,2,1,0:T(8,128)(2,1)S(1)}, bf16[1,3,64,256]{3,2,1,0:T(8,128)(2,1)}, u32[]{:S(2)}) copy-start(bf16[1,3,64,256]{3,2,1,0:T(8,128)(2,1)} %refs_0_.1) | copy-start | bytes 294916
  0.0 9.8 %collective-permute-start = (bf16[1,3,64,256]{3,2,1,0:T(8,128)(2,1)}, bf16[1,3,64,256]{3,2,1,0:T(8,128)(2,1)S(1)}, u32[]{:S(2)}, u32[]{:S(2)}) collective-permute-start(bf16[1,3,64,256]{3,2,1,0:T(8,128)(2,1)} %refs_0_.1), channel_id=1, source_target_pairs={{0,8},{4,12},{8,0},{12,4},{1,9},{5,13},{9,1},{13,5},{2,10},{6,14},... | collective-permute-start | bytes 294920 | tf_op jit(solution)/shard_map/ppermute | solution.py:363
  5.2 6.6 %copy-start.1 = (s32[4,32,2]{1,2,0:T(2,128)S(1)}, s32[4,32,2]{1,2,0:T(2,128)}, u32[]{:S(2)}) copy-start(s32[4,32,2]{1,2,0:T(2,128)} %param.9) | copy-start | bytes 3076
  5.2 6.6 %copy-start.2 = (s32[3]{0:T(128)S(1)}, s32[3]{0:T(128)}, u32[]{:S(2)}) copy-start(s32[3]{0:T(128)} %azimuth.1) | copy-start | bytes 40
  5.3 9.7 %collective-permute-start.1 = (f16[6,64,256]{2,1,0:T(8,128)(2,1)S(1)}, f16[6,64,256]{2,1,0:T(8,128)(2,1)S(1)}, u32[]{:S(2)}, u32[]{:S(2)}) collective-permute-start(f16[6,64,256]{2,1,0:T(8,128)(2,1)S(1)} %multiply_convert_fusion.1), channel_id=1, source_target_pairs={{0,4},{4,0},{8,12},{12,8},{1,5},{5,1},{9,13},{13,9},{2,6},{6,2},{1... | collective-permute-start | bytes 589832 | tf_op jit(solution)/shard_map/ppermute | solution.py:400
  6.7 8.3 %collective-permute-start.2 = (f16[6,64,256]{2,1,0:T(8,128)(2,1)S(1)}, f16[6,64,256]{2,1,0:T(8,128)(2,1)S(1)}, u32[]{:S(2)}, u32[]{:S(2)}) collective-permute-start(f16[6,64,256]{2,1,0:T(8,128)(2,1)S(1)} %multiply_convert_fusion), channel_id=1, source_target_pairs={{0,0},{4,8},{8,4},{12,12},{1,1},{5,9},{9,5},{13,13},{2,2},{6,10},{... | collective-permute-start | bytes 589832 | tf_op jit(solution)/shard_map/ppermute | solution.py:400
  7.4 7.7 %collective-permute-start.3 = (f32[6,8,256]{2,1,0:T(8,128)S(1)}, f32[6,8,256]{2,1,0:T(8,128)S(1)}, u32[]{:S(2)}, u32[]{:S(2)}) collective-permute-start(f32[6,8,256]{2,1,0:T(8,128)S(1)} %get-tuple-element.40), channel_id=1, source_target_pairs={{0,1},{1,0},{2,3},{3,2},{4,5},{5,4},{6,7},{7,6},{8,9},{9,8},{10,11... | collective-permute-start | bytes 147464 | tf_op jit(solution)/shard_map/ppermute | solution.py:404
  8.7 6.4 %collective-permute-start.4 = (f32[6,8,256]{2,1,0:T(8,128)S(1)}, f32[6,8,256]{2,1,0:T(8,128)S(1)}, u32[]{:S(2)}, u32[]{:S(2)}) collective-permute-start(f32[6,8,256]{2,1,0:T(8,128)S(1)} %get-tuple-element.41), channel_id=1, source_target_pairs={{0,3},{1,2},{2,1},{3,0},{4,7},{5,6},{6,5},{7,4},{8,11},{9,10},{10,... | collective-permute-start | bytes 147464 | tf_op jit(solution)/shard_map/ppermute | solution.py:404
  9.9 6.9 %collective-permute-start.5 = (bf16[2,3,64,256]{3,2,1,0:T(8,128)(2,1)S(1)}, bf16[2,3,64,256]{3,2,1,0:T(8,128)(2,1)S(1)}, u32[]{:S(2)}, u32[]{:S(2)}) collective-permute-start(bf16[2,3,64,256]{3,2,1,0:T(8,128)(2,1)S(1)} %pad_maximum_fusion), channel_id=1, source_target_pairs={{0,4},{4,0},{8,12},{12,8},{1,5},{5,1},{9,13},{13,9},{2,6},{6,2},{1... | collective-permute-start | bytes 589832 | tf_op jit(solution)/shard_map/ppermute | solution.py:363
  15.4 6.2 %collective-permute-start.6 = (f16[3,64,256]{2,1,0:T(8,128)(2,1)S(1)}, f16[3,64,256]{2,1,0:T(8,128)(2,1)S(1)}, u32[]{:S(2)}, u32[]{:S(2)}) collective-permute-start(f16[3,64,256]{2,1,0:T(8,128)(2,1)S(1)} %multiply_convert_fusion.5), channel_id=1, source_target_pairs={{0,4},{4,0},{8,12},{12,8},{1,5},{5,1},{9,13},{13,9},{2,6},{6,2},{1... | collective-permute-start | bytes 294920 | tf_op jit(solution)/shard_map/ppermute | solution.py:400
  15.5 6.1 %collective-permute-start.9 = (f16[3,64,256]{2,1,0:T(8,128)(2,1)S(1)}, f16[3,64,256]{2,1,0:T(8,128)(2,1)S(1)}, u32[]{:S(2)}, u32[]{:S(2)}) collective-permute-start(f16[3,64,256]{2,1,0:T(8,128)(2,1)S(1)} %multiply_convert_fusion.4), channel_id=1, source_target_pairs={{0,0},{4,8},{8,4},{12,12},{1,1},{5,9},{9,5},{13,13},{2,2},{6,10},{... | collective-permute-start | bytes 294920 | tf_op jit(solution)/shard_map/ppermute | solution.py:400
  17.3 4.1 %collective-permute-start.7 = (f32[3,8,256]{2,1,0:T(8,128)S(1)}, f32[3,8,256]{2,1,0:T(8,128)S(1)}, u32[]{:S(2)}, u32[]{:S(2)}) collective-permute-start(f32[3,8,256]{2,1,0:T(8,128)S(1)} %get-tuple-element.49), channel_id=1, source_target_pairs={{0,1},{1,0},{2,3},{3,2},{4,5},{5,4},{6,7},{7,6},{8,9},{9,8},{10,11... | collective-permute-start | bytes 73736 | tf_op jit(solution)/shard_map/ppermute | solution.py:404
  18.3 3.3 %collective-permute-start.8 = (f32[3,8,256]{2,1,0:T(8,128)S(1)}, f32[3,8,256]{2,1,0:T(8,128)S(1)}, u32[]{:S(2)}, u32[]{:S(2)}) collective-permute-start(f32[3,8,256]{2,1,0:T(8,128)S(1)} %get-tuple-element.50), channel_id=1, source_target_pairs={{0,3},{1,2},{2,1},{3,0},{4,7},{5,6},{6,5},{7,4},{8,11},{9,10},{10,... | collective-permute-start | bytes 73736 | tf_op jit(solution)/shard_map/ppermute | solution.py:404
  21.9 7.2 %collective-permute-start.10 = (f16[3,64,256]{2,1,0:T(8,128)(2,1)S(1)}, f16[3,64,256]{2,1,0:T(8,128)(2,1)S(1)}, u32[]{:S(2)}, u32[]{:S(2)}) collective-permute-start(f16[3,64,256]{2,1,0:T(8,128)(2,1)S(1)} %multiply_convert_fusion.3), channel_id=1, source_target_pairs={{0,4},{4,0},{8,12},{12,8},{1,5},{5,1},{9,13},{13,9},{2,6},{6,2},{1... | collective-permute-start | bytes 294920 | tf_op jit(solution)/shard_map/ppermute | solution.py:400
  25.7 3.4 %collective-permute-start.11 = (f16[3,64,256]{2,1,0:T(8,128)(2,1)S(1)}, f16[3,64,256]{2,1,0:T(8,128)(2,1)S(1)}, u32[]{:S(2)}, u32[]{:S(2)}) collective-permute-start(f16[3,64,256]{2,1,0:T(8,128)(2,1)S(1)} %multiply_convert_fusion.2), channel_id=1, source_target_pairs={{0,0},{4,8},{8,4},{12,12},{1,1},{5,9},{9,5},{13,13},{2,2},{6,10},{... | collective-permute-start | bytes 294920 | tf_op jit(solution)/shard_map/ppermute | solution.py:400
  26.4 2.8 %collective-permute-start.12 = (f32[3,8,256]{2,1,0:T(8,128)S(1)}, f32[3,8,256]{2,1,0:T(8,128)S(1)}, u32[]{:S(2)}, u32[]{:S(2)}) collective-permute-start(f32[3,8,256]{2,1,0:T(8,128)S(1)} %get-tuple-element.58), channel_id=1, source_target_pairs={{0,1},{1,0},{2,3},{3,2},{4,5},{5,4},{6,7},{7,6},{8,9},{9,8},{10,11... | collective-permute-start | bytes 73736 | tf_op jit(solution)/shard_map/ppermute | solution.py:404
  26.8 3.3 %collective-permute-start.13 = (f32[3,8,256]{2,1,0:T(8,128)S(1)}, f32[3,8,256]{2,1,0:T(8,128)S(1)}, u32[]{:S(2)}, u32[]{:S(2)}) collective-permute-start(f32[3,8,256]{2,1,0:T(8,128)S(1)} %get-tuple-element.59), channel_id=1, source_target_pairs={{0,3},{1,2},{2,1},{3,0},{4,7},{5,6},{6,5},{7,4},{8,11},{9,10},{10,... | collective-permute-start | bytes 73736 | tf_op jit(solution)/shard_map/ppermute | solution.py:404
